TPU v7x, 512 devices: a whole 4x4x16 slice. The times are simulated.
512 devices in a mesh: gx: 8 (over x, core), gy: 8 (over z_hi, y), gz: 8 (over z_lo).
Axes of the slice: x: 4, y: 4, z: 16 (z_hi: 2, z_lo: 8; z = z_hi * 8 + z_lo), core: 2. Of those that a mesh axis runs over, the one named last changes fastest.
Arguments:
- charge: bfloat16 [128, 256, 1024], P('gx', 'gy', 'gz'), may hold values from -6 to 6
- kernel_taps: float32 [2, 17], replicated, may hold values from 0 to 1, as said below
- top_x: float32 [32], replicated, may hold values from 0 to 1, as said below
- top_y: float32 [64], replicated, may hold values from 0 to 1, as said below
- top_z: float32 [256], replicated, may hold values from 0 to 1, as said below
Outputs:
- potential: float32 [128, 256, 1024], P('gx', 'gy', 'gz')
Inputs may be any that keep to these rules, and one draw needn't show every extreme that they name: `kernel_taps`: positive taps. `top_x`: positive. `top_y`: positive. `top_z`: positive.
All inputs are finite; a program needn't handle non-finite values.
Results may differ from a plain program's by a relative error of at most 0.00041.
Values may be sent and summed in bfloat16 or wider, within the bound.
No kernel may reach another device: no remote copies, remote signals or barrier semaphores. Data moves between devices by JAX's collectives and lax.ppermute only.
A program may use at most 64 MiB of HBM per device.

v0:
```python
import jax
import jax.numpy as jnp
from jax import lax
from jax.sharding import PartitionSpec as P

spread_weights = (-1.0 / 16.0, 0.0, 9.0 / 16.0, 1.0, 9.0 / 16.0, 0.0, -1.0 / 16.0)
reach = 8


def with_halo(block, sides, width):
    for axis, dim in sides:
        count = lax.axis_size(axis)
        forward = [(i, i + 1) for i in range(count - 1)]
        forward.append((count - 1, 0))
        backward = [(target, source) for source, target in forward]
        low = lax.ppermute(
            lax.slice_in_dim(block, block.shape[dim] - width, None, axis=dim), axis, forward
        )
        high = lax.ppermute(lax.slice_in_dim(block, 0, width, axis=dim), axis, backward)
        block = jnp.concatenate([low, block, high], axis=dim)
    return block


def band_matrix(taps_row, length_now):
    rows_index = jnp.arange(length_now + 2 * reach, dtype=jnp.int32)[:, None]
    cols_index = jnp.arange(length_now, dtype=jnp.int32)[None, :]
    offset_gap = rows_index - cols_index
    inside = (offset_gap >= 0) & (offset_gap <= 2 * reach)
    values = jnp.take(taps_row, jnp.clip(offset_gap, 0, 2 * reach))
    return jnp.where(inside, values, 0.0)


def convolve_block(padded, taps_row):
    size_x = padded.shape[0] - 2 * reach
    size_y = padded.shape[1] - 2 * reach
    size_z = padded.shape[2] - 2 * reach
    along_x = taps_row[0] * padded[0:size_x]
    for offset in range(1, 2 * reach + 1):
        along_x = along_x + taps_row[offset] * padded[offset : offset + size_x]
    along_y = taps_row[0] * along_x[:, 0:size_y]
    for offset in range(1, 2 * reach + 1):
        along_y = along_y + taps_row[offset] * along_x[:, offset : offset + size_y]
    flat_rows = along_y.reshape(size_x * size_y, size_z + 2 * reach)
    along_z = jnp.dot(
        flat_rows,
        band_matrix(taps_row, size_z),
        precision=lax.Precision.HIGHEST,
        preferred_element_type=jnp.float32,
    )
    return along_z.reshape(size_x, size_y, size_z)


def restrict_block(padded):
    margin = reach - 3
    field = padded[margin:-margin, margin:-margin, margin:-margin]
    for axis in range(3):
        length_now = field.shape[axis] - 6
        summed = spread_weights[0] * lax.slice_in_dim(field, 0, length_now, 2, axis)
        for offset in range(1, 7):
            summed = summed + spread_weights[offset] * lax.slice_in_dim(
                field, offset, offset + length_now, 2, axis
            )
        field = summed
    return field


def prolong_block(padded):
    field = padded
    for axis in range(3):
        length_now = field.shape[axis] - 4
        middle = lax.slice_in_dim(field, 2, 2 + length_now, 1, axis)
        upper = lax.slice_in_dim(field, 3, 3 + length_now, 1, axis)
        lower = lax.slice_in_dim(field, 1, 1 + length_now, 1, axis)
        farther = lax.slice_in_dim(field, 4, 4 + length_now, 1, axis)
        odd_cells = 9.0 / 16.0 * (middle + upper) - 1.0 / 16.0 * (lower + farther)
        stacked = jnp.stack([middle, odd_cells], axis=axis + 1)
        new_shape = list(middle.shape)
        new_shape[axis] = 2 * length_now
        field = stacked.reshape(new_shape)
    return field


def own_rows(profile, first, count):
    length_now = profile.shape[0]
    mine = first + jnp.arange(count, dtype=jnp.int32)[:, None]
    theirs = jnp.arange(length_now, dtype=jnp.int32)[None, :]
    return jnp.take(profile, (mine - theirs) % length_now)


def per_device(charge, kernel_taps, top_x, top_y, top_z):
    highest = lax.Precision.HIGHEST
    field = charge.astype(jnp.float32)
    nears = []
    for section in range(2):
        padded = with_halo(field, (("gx", 0), ("gy", 1), ("gz", 2)), reach)
        nears.append(convolve_block(padded, kernel_taps[section]))
        field = restrict_block(padded)
    coarse = field.astype(jnp.bfloat16)
    size_a, size_b, size_c = coarse.shape
    rows_x = own_rows(top_x, lax.axis_index("gx") * size_a, size_a)
    rows_y = own_rows(top_y, lax.axis_index("gy") * size_b, size_b)
    rows_z = own_rows(top_z, lax.axis_index("gz") * size_c, size_c)
    count_x = lax.axis_size("gx")
    count_y = lax.axis_size("gy")
    count_z = lax.axis_size("gz")
    gathered = lax.all_gather(
        coarse.reshape(1, size_a * size_b * size_c), ("gx", "gy", "gz"), axis=0, tiled=True
    )
    whole = gathered.reshape(count_x, count_y, count_z, size_a, size_b, size_c)
    whole = whole.transpose(0, 3, 1, 4, 2, 5).reshape(
        count_x * size_a, count_y * size_b, count_z * size_c
    )

    def plane_sum(plane):
        return jnp.dot(
            plane.astype(jnp.float32),
            rows_z.T,
            precision=highest,
            preferred_element_type=jnp.float32,
        )

    result = lax.map(plane_sum, whole)
    result = jnp.einsum("xyc,by->xbc", result, rows_y, precision=highest)
    result = jnp.einsum("xbc,ax->abc", result, rows_x, precision=highest)
    for section in (1, 0):
        padded = with_halo(result, (("gx", 0), ("gy", 1), ("gz", 2)), 2)
        result = nears[section] + prolong_block(padded)
    return result


def solution(mesh):
    return jax.shard_map(
        per_device,
        mesh=mesh,
        in_specs=(P("gx", "gy", "gz"), P(), P(), P(), P()),
        out_specs=P("gx", "gy", "gz"),
        check_vma=False,
    )
```

profile of v0, /device:TPU:1, one launch (start us, length us, event | category | flops | bytes accessed | tf_op | source)
XLA Modules:
  0.0 1388.5 jit_solution(9187464631501591779)
XLA Ops:
  6.5 0.9 fusion.366
  7.4 2.6 collective-permute-start
  10.1 4.3 collective-permute-start.1
  14.4 0.9 convert_element_type.7
  15.4 2.3 collective-permute-start.2
  17.7 16.6 %collective-permute-start.3 = (f32[32,8,128]{2,1,0:T(8,128)S(1)}, f32[32,8,128]{2,1,0:T(8,128)S(1)}, u32[]{:S(2)}, u32[]{:S(2)}) collective-permute-start(f32[32,8,128]{2,1,0:T(8,128)S(1)} %get-tuple-element.39), channel_id=1, source_target_pairs={{8,0},{16,8},{24,16},{32,24},{40,32},{48,40},{56,48},{0,56},{9,1},... | collective-permute-start | bytes 393224 | tf_op jit(solution)/shard_map/ppermute | solution.py:19
  35.0 1.2 collective-permute-done.3
  37.5 11.9 collective-permute-start.4
  49.6 1.9 collective-permute-start.5
  51.5 3.8 collective-permute-done.4
  55.6 2.3 collective-permute-done.5
  58.2 1.7 pad_maximum_fusion
  61.4 1.1 slice.764
  62.5 1.2 slice.763
  63.7 1.2 slice.762
  64.8 1.2 slice.761
  66.0 1.2 slice.760
  67.2 1.2 slice.759
  68.3 1.1 slice.758
  69.5 0.9 collective-permute-start.7
  70.4 0.9 collective-permute-start.6
  71.3 1.9 collective-permute-done.7
  73.4 1.9 collective-permute-start.8
  75.3 14.2 %collective-permute-start.9 = (f32[24,8,64]{2,1,0:T(8,128)S(1)}, f32[24,8,64]{2,1,0:T(8,128)S(1)}, u32[]{:S(2)}, u32[]{:S(2)}) collective-permute-start(f32[24,8,64]{2,1,0:T(8,128)S(1)} %get-tuple-element.45), channel_id=1, source_target_pairs={{8,0},{16,8},{24,16},{32,24},{40,32},{48,40},{56,48},{0,56},{9,1},... | collective-permute-start | bytes 147464 | tf_op jit(solution)/shard_map/ppermute | solution.py:19
  89.7 1.4 collective-permute-done.9
  91.3 4.8 collective-permute-start.10
  96.1 7.1 collective-permute-start.11
  103.3 8.8 collective-permute-done.10
  112.1 2.9 collective-permute-done.11
  117.9 1.4 gather_fusion.1
  119.6 3.3 gather_fusion.2
  123.2 51.2 %gather_fusion.3 = f32[8192]{0:T(1024)S(1)} fusion(f32[256]{0:T(256)S(1)} %copy-done, s32[8192]{0:T(1024)S(1)} %broadcast_clamp_fusion), kind=kCustom, calls=%fused_computation.3 | custom fusion | bytes 98304 | tf_op jit(solution)/shard_map/jit(_take)/gather | solution.py:87
  174.6 1009.4 %all-gather.3.cloned.1.call-done = bf16[512,1,1024]{2,1,0:T(2,128)(2,1)} async-done(((bf16[1,1,1024]{2,1,0:T(2,128)(2,1)}), bf16[512,1,1024]{2,1,0:T(2,128)(2,1)}) %all-gather.3.cloned.1.call-update) | async-done | bytes 1048592 | tf_op jit(solution)/shard_map/all_gather | solution.py:106
  1184.0 7.4 reduce
  1191.4 4.3 reshape.493
  1195.7 6.9 copy.76
  1202.6 5.3 reshape.494
  1207.9 24.4 %while.10 = (s32[]{:T(128)}, f32[32,64,32]{1,2,0:T(8,128)}, bf16[32,64,256]{2,1,0:T(8,128)(2,1)S(1)}, f32[32,256]{1,0:T(8,128)S(1)}, s32[]{:T(128)}) while((s32[]{:T(128)}, f32[32,64,32]{1,2,0:T(8,128)}, bf16[32,64,256]{2,1,0:T(8,128)(2,1)S(1)}, f32[32,256]{1,0:T(8,128)S(1)}, s32[]{:T(128)}) %tuple.67), condition=%wide.region_1.2_spmd, body=%wide.region_0.1_spmd.sunk | while | flops 6291458 | bytes 83013 | solution.py:122
  1208.0 0.8 fusion.379
  1210.3 0.8 fusion.379
  1219.4 0.8 fusion.379
  1221.7 0.8 fusion.379
  1230.8 0.8 fusion.379
  1231.6 0.8 fusion.379
  1232.4 3.2 convolution_bitcast_fusion.1
  1237.2 2.6 collective-permute-done.13
  1239.7 1.9 collective-permute-start.14
  1241.7 14.2 %collective-permute-start.15 = (f32[8,2,32]{2,0,1:T(8,128)S(1)}, f32[8,2,32]{2,0,1:T(8,128)S(1)}, u32[]{:S(2)}, u32[]{:S(2)}) collective-permute-start(f32[8,2,32]{2,0,1:T(8,128)S(1)} %get-tuple-element.67), channel_id=1, source_target_pairs={{8,0},{16,8},{24,16},{32,24},{40,32},{48,40},{56,48},{0,56},{9,1},... | collective-permute-start | bytes 6152 | tf_op jit(solution)/shard_map/ppermute | solution.py:19
  1256.6 30.7 %gather_fusion = f32[5120]{0:T(1024)S(1)} fusion(f32[17]{0:T(128)S(1)} %slice_bitcast_fusion.6, s32[5120]{0:T(1024)S(1)} %broadcast_clamp_fusion.1), kind=kCustom, calls=%fused_computation | custom fusion | bytes 61440 | tf_op jit(solution)/shard_map/jit(_take)/gather | solution.py:29
  1287.5 3.0 collective-permute-start.16
  1290.5 8.9 collective-permute-start.17
  1299.4 10.8 fusion.77
  1311.0 11.0 convolution_add_fusion.1
  1322.0 0.9 collective-permute-start.18
  1322.9 1.1 collective-permute-start.19
  1324.6 1.4 collective-permute-done.19
  1326.1 1.9 collective-permute-start.20
  1328.0 14.2 %collective-permute-start.21 = (f32[12,2,64]{2,1,0:T(2,128)S(1)}, f32[12,2,64]{2,1,0:T(2,128)S(1)}, u32[]{:S(2)}, u32[]{:S(2)}) collective-permute-start(f32[12,2,64]{2,1,0:T(2,128)S(1)} %get-tuple-element.55), channel_id=1, source_target_pairs={{8,0},{16,8},{24,16},{32,24},{40,32},{48,40},{56,48},{0,56},{9,1},... | collective-permute-start | bytes 18440 | tf_op jit(solution)/shard_map/ppermute | solution.py:19
  1342.2 0.8 collective-permute-done.21
  1343.2 1.9 collective-permute-start.22
  1345.1 10.0 collective-permute-start.23
  1355.1 11.4 fusion.4
  1367.3 1.0 copy.88
  1368.8 12.8 convolution_add_fusion
  (154 shorter events, 33.3 us)
Async XLA Ops:
  6.5 116.6 %copy-start = (f32[256]{0:T(256)S(1)}, f32[256]{0:T(256)}, u32[]{:S(2)}) copy-start(f32[256]{0:T(256)} %param.11) | copy-start | bytes 3076
  6.5 1177.5 %all-gather.3.cloned.1.call-start = ((), (), s32[]{:S(2)}) async-start(), calls=%async_computation | async-start | bytes 2101248 | tf_op jit(solution)/shard_map/all_gather | solution.py:106
  7.4 7.8 collective-permute-start
  10.1 5.3 collective-permute-start.1
  15.3 20.9 %copy-start.3 = (f32[8,32,128]{2,1,0:T(8,128)}, f32[8,32,128]{2,1,0:T(8,128)S(1)}, u32[]{:S(2)}) copy-start(f32[8,32,128]{2,1,0:T(8,128)S(1)} %collective-permute-done.1) | copy-start | bytes 393220
  15.4 19.6 %collective-permute-start.2 = (f32[32,8,128]{2,1,0:T(8,128)S(1)}, f32[32,8,128]{2,1,0:T(8,128)S(1)}, u32[]{:S(2)}, u32[]{:S(2)}) collective-permute-start(f32[32,8,128]{2,1,0:T(8,128)S(1)} %get-tuple-element.38), channel_id=1, source_target_pairs={{0,8},{8,16},{16,24},{24,32},{32,40},{40,48},{48,56},{56,0},{1,9},... | collective-permute-start | bytes 393224 | tf_op jit(solution)/shard_map/ppermute | solution.py:16
  17.7 18.5 %collective-permute-start.3 = (f32[32,8,128]{2,1,0:T(8,128)S(1)}, f32[32,8,128]{2,1,0:T(8,128)S(1)}, u32[]{:S(2)}, u32[]{:S(2)}) collective-permute-start(f32[32,8,128]{2,1,0:T(8,128)S(1)} %get-tuple-element.39), channel_id=1, source_target_pairs={{8,0},{16,8},{24,16},{32,24},{40,32},{48,40},{56,48},{0,56},{9,1},... | collective-permute-start | bytes 393224 | tf_op jit(solution)/shard_map/ppermute | solution.py:19
  35.0 1.2 copy-start.4
  36.2 0.7 copy-start.5
  37.5 17.9 %collective-permute-start.4 = (f32[32,48,8]{1,2,0:T(8,128)S(1)}, f32[32,48,8]{1,2,0:T(8,128)S(1)}, u32[]{:S(2)}, u32[]{:S(2)}) collective-permute-start(f32[32,48,8]{1,2,0:T(8,128)S(1)} %copy.94), channel_id=1, source_target_pairs={{0,1},{1,2},{2,3},{3,4},{4,5},{5,6},{6,7},{7,0},{8,9},{9,10},{10,1... | collective-permute-start | bytes 147464 | tf_op jit(solution)/shard_map/ppermute | solution.py:16
  49.6 8.3 collective-permute-start.5
  69.5 3.7 collective-permute-start.7
  70.4 3.0 collective-permute-start.6
  73.4 16.3 %collective-permute-start.8 = (f32[24,8,64]{2,1,0:T(8,128)S(1)}, f32[24,8,64]{2,1,0:T(8,128)S(1)}, u32[]{:S(2)}, u32[]{:S(2)}) collective-permute-start(f32[24,8,64]{2,1,0:T(8,128)S(1)} %get-tuple-element.44), channel_id=1, source_target_pairs={{0,8},{8,16},{16,24},{24,32},{32,40},{40,48},{48,56},{56,0},{1,9},... | collective-permute-start | bytes 147464 | tf_op jit(solution)/shard_map/ppermute | solution.py:16
  75.3 15.8 %collective-permute-start.9 = (f32[24,8,64]{2,1,0:T(8,128)S(1)}, f32[24,8,64]{2,1,0:T(8,128)S(1)}, u32[]{:S(2)}, u32[]{:S(2)}) collective-permute-start(f32[24,8,64]{2,1,0:T(8,128)S(1)} %get-tuple-element.45), channel_id=1, source_target_pairs={{8,0},{16,8},{24,16},{32,24},{40,32},{48,40},{56,48},{0,56},{9,1},... | collective-permute-start | bytes 147464 | tf_op jit(solution)/shard_map/ppermute | solution.py:19
  91.3 26.6 %copy-start.2 = (f32[32]{0:T(128)S(1)}, f32[32]{0:T(128)}, u32[]{:S(2)}) copy-start(f32[32]{0:T(128)} %param.9) | copy-start | bytes 388
  91.3 20.8 %collective-permute-start.10 = (f32[24,32,8]{2,1,0:T(8,128)S(1)}, f32[24,32,8]{2,1,0:T(8,128)S(1)}, u32[]{:S(2)}, u32[]{:S(2)}) collective-permute-start(f32[24,32,8]{2,1,0:T(8,128)S(1)} %get-tuple-element.40), channel_id=1, source_target_pairs={{0,1},{1,2},{2,3},{3,4},{4,5},{5,6},{6,7},{7,0},{8,9},{9,10},{10,1... | collective-permute-start | bytes 73736 | tf_op jit(solution)/shard_map/ppermute | solution.py:16
  96.1 18.9 %collective-permute-start.11 = (f32[24,32,8]{2,1,0:T(8,128)S(1)}, f32[24,32,8]{2,1,0:T(8,128)S(1)}, u32[]{:S(2)}, u32[]{:S(2)}) collective-permute-start(f32[24,32,8]{2,1,0:T(8,128)S(1)} %get-tuple-element.41), channel_id=1, source_target_pairs={{1,0},{2,1},{3,2},{4,3},{5,4},{6,5},{7,6},{0,7},{9,8},{10,9},{11,1... | collective-permute-start | bytes 73736 | tf_op jit(solution)/shard_map/ppermute | solution.py:19
  115.4 4.2 copy-start.1
  123.2 51.3 %copy-start.6 = (f32[2,17]{1,0:T(2,128)S(1)}, f32[2,17]{1,0:T(2,128)}, u32[]{:S(2)}) copy-start(f32[2,17]{1,0:T(2,128)} %param.8) | copy-start | bytes 412
  1235.9 1.3 collective-permute-start.12
  1236.4 3.4 collective-permute-start.13
  1239.7 47.7 %collective-permute-start.14 = (f32[8,2,32]{2,0,1:T(8,128)S(1)}, f32[8,2,32]{2,0,1:T(8,128)S(1)}, u32[]{:S(2)}, u32[]{:S(2)}) collective-permute-start(f32[8,2,32]{2,0,1:T(8,128)S(1)} %get-tuple-element.66), channel_id=1, source_target_pairs={{0,8},{8,16},{16,24},{24,32},{32,40},{40,48},{48,56},{56,0},{1,9},... | collective-permute-start | bytes 6152 | tf_op jit(solution)/shard_map/ppermute | solution.py:16
  1241.7 45.7 %collective-permute-start.15 = (f32[8,2,32]{2,0,1:T(8,128)S(1)}, f32[8,2,32]{2,0,1:T(8,128)S(1)}, u32[]{:S(2)}, u32[]{:S(2)}) collective-permute-start(f32[8,2,32]{2,0,1:T(8,128)S(1)} %get-tuple-element.67), channel_id=1, source_target_pairs={{8,0},{16,8},{24,16},{32,24},{40,32},{48,40},{56,48},{0,56},{9,1},... | collective-permute-start | bytes 6152 | tf_op jit(solution)/shard_map/ppermute | solution.py:19
  1287.5 22.7 %collective-permute-start.16 = (f32[8,12,2]{2,0,1:T(8,128)S(1)}, f32[8,12,2]{2,0,1:T(8,128)S(1)}, u32[]{:S(2)}, u32[]{:S(2)}) collective-permute-start(f32[8,12,2]{2,0,1:T(8,128)S(1)} %get-tuple-element.64), channel_id=1, source_target_pairs={{0,1},{1,2},{2,3},{3,4},{4,5},{5,6},{6,7},{7,0},{8,9},{9,10},{10,1... | collective-permute-start | bytes 2312 | tf_op jit(solution)/shard_map/ppermute | solution.py:16
  1290.5 19.7 %collective-permute-start.17 = (f32[8,12,2]{2,0,1:T(8,128)S(1)}, f32[8,12,2]{2,0,1:T(8,128)S(1)}, u32[]{:S(2)}, u32[]{:S(2)}) collective-permute-start(f32[8,12,2]{2,0,1:T(8,128)S(1)} %get-tuple-element.65), channel_id=1, source_target_pairs={{1,0},{2,1},{3,2},{4,3},{5,4},{6,5},{7,6},{0,7},{9,8},{10,9},{11,1... | collective-permute-start | bytes 2312 | tf_op jit(solution)/shard_map/ppermute | solution.py:19
  1322.0 2.6 collective-permute-start.18
  1322.9 3.2 collective-permute-start.19
  1326.1 16.1 %collective-permute-start.20 = (f32[12,2,64]{2,1,0:T(2,128)S(1)}, f32[12,2,64]{2,1,0:T(2,128)S(1)}, u32[]{:S(2)}, u32[]{:S(2)}) collective-permute-start(f32[12,2,64]{2,1,0:T(2,128)S(1)} %get-tuple-element.54), channel_id=1, source_target_pairs={{0,8},{8,16},{16,24},{24,32},{32,40},{40,48},{48,56},{56,0},{1,9},... | collective-permute-start | bytes 18440 | tf_op jit(solution)/shard_map/ppermute | solution.py:16
  1328.0 15.0 %collective-permute-start.21 = (f32[12,2,64]{2,1,0:T(2,128)S(1)}, f32[12,2,64]{2,1,0:T(2,128)S(1)}, u32[]{:S(2)}, u32[]{:S(2)}) collective-permute-start(f32[12,2,64]{2,1,0:T(2,128)S(1)} %get-tuple-element.55), channel_id=1, source_target_pairs={{8,0},{16,8},{24,16},{32,24},{40,32},{48,40},{56,48},{0,56},{9,1},... | collective-permute-start | bytes 18440 | tf_op jit(solution)/shard_map/ppermute | solution.py:19
  1343.2 23.3 %collective-permute-start.22 = (f32[12,20,2]{2,1,0:T(8,128)S(1)}, f32[12,20,2]{2,1,0:T(8,128)S(1)}, u32[]{:S(2)}, u32[]{:S(2)}) collective-permute-start(f32[12,20,2]{2,1,0:T(8,128)S(1)} %get-tuple-element.50), channel_id=1, source_target_pairs={{0,1},{1,2},{2,3},{3,4},{4,5},{5,6},{6,7},{7,0},{8,9},{9,10},{10,1... | collective-permute-start | bytes 5768 | tf_op jit(solution)/shard_map/ppermute | solution.py:16
  1345.1 21.4 %collective-permute-start.23 = (f32[12,20,2]{2,1,0:T(8,128)S(1)}, f32[12,20,2]{2,1,0:T(8,128)S(1)}, u32[]{:S(2)}, u32[]{:S(2)}) collective-permute-start(f32[12,20,2]{2,1,0:T(8,128)S(1)} %get-tuple-element.51), channel_id=1, source_target_pairs={{1,0},{2,1},{3,2},{4,3},{5,4},{6,5},{7,6},{0,7},{9,8},{10,9},{11,1... | collective-permute-start | bytes 5768 | tf_op jit(solution)/shard_map/ppermute | solution.py:19
Sparse Core Ops, SparseCore 0:
  117.9 1066.0 all-gather.2
where the time goes:
time: 1400 us; the launch traced here: 1390 us
  waiting for transfers between devices  1040 us (74%)
  starting transfers between devices  128 us (9%)
  local copies, waits for them, and re-layouts  122 us (9%)
  matrix products  51.8 us (4%)
  other arithmetic  34.4 us (2%)
  between operations  14.2 us (1%)
    all_gather x1, waiting for transfers between devices, per_device(): lax.all_gather(coarse.reshape(1, size_a * size_b * size_c), ('gx', 'gy',...  1010 us
    ppermute x12, starting transfers between devices, with_halo(): lax.ppermute(lax.slice_in_dim(block, 0, width, axis=dim), axis, backward)  93.3 us
    gather x6, local copies, waits for them, and re-layouts, own_rows(): return jnp.take(profile, (mine - theirs) % length_now)  56.1 us
    ppermute x12, starting transfers between devices, with_halo(): lax.ppermute(lax.slice_in_dim(block, block.shape[dim] - width, None, axis...  34.5 us
    gather x2, local copies, waits for them, and re-layouts, band_matrix(): values = jnp.take(taps_row, jnp.clip(offset_gap, 0, 2 * reach))  30.8 us
  transfers between devices with their start and end apart: 25, of which 15 were waited for; matrix products, arithmetic and copies ran while one was open for 8% of the time, Pallas kernels for 0%

commit v1 on v0

v1 whole, which is shorter than its diff:
```python
import jax
import jax.numpy as jnp
import numpy as np
from jax import lax
from jax.experimental import pallas as pl
from jax.experimental.pallas import tpu as pltpu
from jax.sharding import PartitionSpec as P

f32 = jnp.float32
bf16 = jnp.bfloat16
highest = lax.Precision.HIGHEST
weight = {-3: -1.0 / 16.0, -1: 9.0 / 16.0, 0: 1.0, 1: 9.0 / 16.0, 3: -1.0 / 16.0}

twice = {}
for d0, w0 in weight.items():
    for d1, w1 in weight.items():
        twice[d0 + 2 * d1] = twice.get(d0 + 2 * d1, 0.0) + w0 * w1

swap_even = [(0, 1), (1, 0), (2, 3), (3, 2), (4, 5), (5, 4), (6, 7), (7, 6)]
swap_odd = [(1, 2), (2, 1), (3, 4), (4, 3), (5, 6), (6, 5), (7, 0), (0, 7)]


def table(rows, cols, entry):
    return np.array([[entry(r, c) for c in range(cols)] for r in range(rows)], np.float32)


def z_cell(row, width):
    if row < 128:
        return row
    if row < 128 + width:
        return row - 128 - width
    if row < 128 + 2 * width:
        return row - width
    return None


def z_twice(row, col):
    cell = z_cell(row, 32)
    return 0.0 if cell is None else twice.get(cell - 4 * (col % 32), 0.0)


y_twice = table(8, 64, lambda r, c: twice.get(c - 16 - 4 * r, 0.0))
z_twice_matrix = table(256, 128, z_twice)
y_raise_top = table(24, 16, lambda r, c: weight.get((r - 1) - 2 * (c - 2), 0.0) if r < 19 and c < 13 else 0.0)
z_raise_top = table(128, 128, lambda r, c: weight.get((c - 1) - 2 * (r - 2), 0.0) if r < 37 and c < 67 else 0.0)
y_raise = table(32, 24, lambda r, c: weight.get(r - 2 * (c - 1), 0.0) if c < 19 else 0.0)
z_raise = table(128, 128, lambda r, c: weight.get(c - 2 * (r - 1), 0.0) if r < 67 else 0.0)


def dot(a, b):
    return jnp.dot(a, b, precision=highest, preferred_element_type=f32)


def lanes(parts):
    return jnp.concatenate(parts, axis=1)


def iota(shape, dim):
    return lax.broadcasted_iota(jnp.int32, shape, dim)


def call(body, outs, args, smem=(), scratch=(), flops=1_000_000, bytes_accessed=1_000_000):
    return pl.pallas_call(
        body,
        out_shape=[jax.ShapeDtypeStruct(s, d) for s, d in outs],
        in_specs=[
            pl.BlockSpec(memory_space=pltpu.SMEM if i in smem else pltpu.VMEM)
            for i in range(len(args))
        ],
        out_specs=[pl.BlockSpec(memory_space=pltpu.VMEM) for _ in outs],
        scratch_shapes=list(scratch),
        compiler_params=pltpu.CompilerParams(vmem_limit_bytes=32 * 1024 * 1024),
        cost_estimate=pl.CostEstimate(
            flops=flops, bytes_accessed=bytes_accessed, transcendentals=0
        ),
    )(*args)


def pair_taps(taps):
    merged = {}
    for b in range(-8, 9):
        for d, w in weight.items():
            merged.setdefault(2 * b + d, []).append(w * taps[1, b + 8])
    return {m: sum(terms[1:], terms[0]) for m, terms in merged.items()}


def prep_near(taps, my1, my2, mz1, mz2):
    merged = pair_taps(taps)

    def fill(gap, values):
        out = jnp.zeros(gap.shape, f32)
        for m, value in values.items():
            out = jnp.where(gap == m, value, out)
        return out

    single = {m: taps[0, m + 8] for m in range(-8, 9)}
    my1[...] = fill(iota((32, 48), 1) - 8 - iota((32, 48), 0), single)
    my2[...] = fill(iota((24, 80), 1) - 24 - 2 * (iota((24, 80), 0) - 1), merged)
    far_off = 1 << 20

    def z_cells(width):
        row = iota((256, 128), 0)
        cell = jnp.where(row < 128, row, jnp.where(row < 128 + width, row - 128 - width, row - width))
        return jnp.where(row < 128 + 2 * width, cell, far_off)

    mz1[...] = fill(z_cells(8) - iota((256, 128), 1), single)
    mz2[...] = fill(z_cells(32) - 2 * (iota((256, 128), 1) - 1), merged)


def toeplitz(profile, shift, size):
    start = pltpu.roll(jnp.broadcast_to(profile, (8, size)), shift, 1)[0:1]
    return pltpu.roll(jnp.broadcast_to(start, (size, size)), 0, 1, stride=1, stride_axis=0)


def prep_top(where, top_x, top_y, top_z, wz1, wz2, wz3, my, wx):
    gx, gy, gz = where[0], where[1], where[2]
    tz = toeplitz(top_z[...], lax.rem(258 - 32 * gz, 256), 256)
    lane = iota((256, 256), 1)
    near = jnp.where(lane < 64, tz, 0.0)
    blocks = [near] + [pltpu.roll(near, 64 * a, 1) for a in range(1, 4)]
    for g in range(8):
        for a in range(4):
            rows = pl.ds(128 * g + 32 * a, 32)
            part = blocks[a][32 * g : 32 * g + 32]
            first = part.astype(bf16)
            rest = part - first.astype(f32)
            second = rest.astype(bf16)
            wz1[rows, :] = first
            wz2[rows, :] = second
            wz3[rows, :] = (rest - second.astype(f32)).astype(bf16)
    ty = toeplitz(top_y[...], lax.rem(130 - 8 * gy, 128), 128)
    my[...] = ty.T[0:16, 0:64]
    tx = toeplitz(top_x[...], lax.rem(130 - 4 * gx, 128), 128)
    spread = jnp.where(iota((32, 2048), 1) // 64 == iota((32, 2048), 0), 1.0, 0.0)
    wx[...] = dot(tx.T[0:16, 0:32], spread)


def x_step(where, taps, lo2, lo1, own, hi1, hi2, n1, n2, q3, out_even, out_odd, ext):
    at = 0
    for part in (lo2, lo1, own, hi1, hi2):
        count = part.shape[0]
        ext[at : at + count] = part[...].astype(f32)
        at += count
    for t in range(4):
        rows = pl.ds(8 * t, 8)
        f = {r: ext[r + 22, rows, :] for r in range(-22, 38)}
        for i in range(16):
            total = taps[0, 0] * f[i - 8]
            for a in range(-7, 9):
                total = total + taps[0, a + 8] * f[i + a]
            n1[i, rows, :] = total
        half = {
            j: f[2 * j]
            + (9.0 / 16.0) * (f[2 * j - 1] + f[2 * j + 1])
            - (1.0 / 16.0) * (f[2 * j - 3] + f[2 * j + 3])
            for j in range(-9, 18)
        }
        for i in range(-1, 10):
            total = taps[1, 0] * half[i - 8]
            for a in range(-7, 9):
                total = total + taps[1, a + 8] * half[i + a]
            n2[i + 1, rows, :] = total
        for j in range(4):
            q3[j, rows, :] = (
                half[2 * j]
                + (9.0 / 16.0) * (half[2 * j - 1] + half[2 * j + 1])
                - (1.0 / 16.0) * (half[2 * j - 3] + half[2 * j + 3])
            )
    odd = lax.rem(where[1], 2)
    for out, low in ((out_even, odd), (out_odd, 1 - odd)):
        for i in range(16):
            out[8 * i : 8 * i + 8] = n1[i, pl.ds(pl.multiple_of(24 * (1 - low), 8), 8), :]
        for i in range(11):
            out[128 + 24 * i : 152 + 24 * i] = n2[i, pl.ds(pl.multiple_of(8 * (1 - low), 8), 24), :]
        for i in range(4):
            out[392 + 16 * i : 408 + 16 * i] = q3[i, pl.ds(pl.multiple_of(16 * (1 - low), 8), 16), :]


def pick(is_odd, even_ref, odd_ref, rows):
    even_part, odd_part = even_ref[rows, :], odd_ref[rows, :]
    low = jnp.where(is_odd, even_part, odd_part)
    high = jnp.where(is_odd, odd_part, even_part)
    return low, high


def y_step(where, n1, n2, q3, from_even, from_odd, my1, my2, my3, n1_out, n2_out, q3_out, out_even, out_odd):
    is_odd = lax.rem(where[1], 2) == 1

    def columns(ref, count, at, width):
        parts = []
        for i in range(count):
            low, high = pick(is_odd, from_even, from_odd, pl.ds(at + width * i, width))
            parts.append(jnp.concatenate([low, ref[i], high], axis=0))
        return lanes(parts)

    r1 = dot(my1[...], columns(n1, 16, 0, 8))
    r2 = dot(my2[...], columns(n2, 11, 128, 24))
    r3 = dot(my3[...], columns(q3, 4, 392, 16))
    parts1 = [r1[:, 128 * i : 128 * i + 128] for i in range(16)]
    parts2 = [r2[:, 128 * i : 128 * i + 128] for i in range(11)]
    parts3 = [r3[:, 128 * i : 128 * i + 128] for i in range(4)]
    for i in range(16):
        n1_out[i] = parts1[i]
    for i in range(11):
        n2_out[i] = parts2[i]
    for i in range(4):
        q3_out[i] = parts3[i]

    def pack(parts, width, high):
        lane = iota(parts[0].shape, 1) // width
        out = jnp.zeros(parts[0].shape, f32)
        for s, part in enumerate(parts):
            shift = (width * s + (width if high else 0)) % 128
            moved = part if shift == 0 else pltpu.roll(part, shift, 1)
            out = jnp.where(lane == s, moved, out)
        return out

    def packed(high):
        groups = [pack(parts1, 8, high)]
        groups += [pack(parts2[4 * g : 4 * g + 4], 32, high) for g in range(3)]
        groups += [pack(parts3, 32, high)]
        return jnp.concatenate(groups, axis=0)

    z_odd = lax.rem(where[2], 2) == 1
    low, high = packed(False), packed(True)
    out_even[...] = jnp.where(z_odd, low, high)
    out_odd[...] = jnp.where(z_odd, high, low)


def windows(low, high, slot, width):
    down = (128 - width * slot) % 128
    up = (128 + width - width * slot) % 128
    low = low if down == 0 else pltpu.roll(low, down, 1)
    high = high if up == 0 else pltpu.roll(high, up, 1)
    return jnp.where(iota(low.shape, 1) < width, low, high)


def q3_step(where, q3, from_even, from_odd, mz3, out):
    z_odd = lax.rem(where[2], 2) == 1
    low, high = pick(z_odd, from_even, from_odd, pl.ds(104, 8))
    rows = jnp.concatenate([lanes([q3[a], windows(low, high, a, 32)]) for a in range(4)], axis=0)
    full = dot(rows, mz3[...])
    lane = iota((8, 128), 1) // 32
    block = full[0:8]
    for a in range(1, 4):
        block = jnp.where(lane == a, full[8 * a : 8 * a + 8], block)
    out[...] = jnp.broadcast_to(block.astype(bf16)[None], (64, 8, 128))


def near_step(where, n1, n2, from_even, from_odd, mz1, mz2, n1_out, n2_out):
    z_odd = lax.rem(where[2], 2) == 1
    low, high = pick(z_odd, from_even, from_odd, pl.ds(0, 32))
    rows = jnp.concatenate([lanes([n1[i], windows(low, high, i, 8)]) for i in range(16)], axis=0)
    n1_out[...] = dot(rows, mz1[...]).reshape(16, 32, 128)
    rows = []
    for g in range(3):
        low, high = pick(z_odd, from_even, from_odd, pl.ds(32 + 24 * g, 24))
        for s in range(4):
            if 4 * g + s < 11:
                rows.append(lanes([n2[4 * g + s], windows(low, high, s, 32)]))
    n2_out[...] = dot(jnp.concatenate(rows, axis=0), mz2[...]).reshape(11, 24, 128)


def top_step(gathered, wz1, wz2, wz3, my, out):
    whole = gathered[...].astype(f32).reshape(8, 8, 8, 128)
    rows = lanes([whole[:, g].reshape(64, 128) for g in range(8)]).astype(bf16)
    along_z = jnp.dot(rows, wz1[...], preferred_element_type=f32)
    along_z = along_z + jnp.dot(rows, wz2[...], preferred_element_type=f32)
    along_z = along_z + jnp.dot(rows, wz3[...], preferred_element_type=f32)
    out[...] = jnp.broadcast_to(dot(my[...], along_z)[None], (8, 16, 256))


def raise_rows(rows, first, last):
    out = {}
    for i in range(first, last + 1):
        if i % 2 == 0:
            out[i] = rows[i // 2]
        else:
            j = (i - 1) // 2
            out[i] = (9.0 / 16.0) * (rows[j] + rows[j + 1]) - (1.0 / 16.0) * (rows[j - 1] + rows[j + 2])
    return out


def last_step(top, wx, n1, n2, y1, z1, y2, z2, out):
    e3 = {}
    for i in range(9):
        total = None
        for g in range(8):
            for h in range(2):
                at = 256 * g + 128 * h
                term = wx[i : i + 1, at : at + 128] * top[g, :, 128 * h : 128 * h + 128]
                total = term if total is None else total + term
        e3[i - 2] = total + pltpu.roll(total, 64, 1)
    e2 = raise_rows(e3, -1, 9)
    wide = dot(y1[...], lanes([e2[i] for i in range(-1, 10)]))
    tall = jnp.concatenate([wide[:, 128 * i : 128 * i + 128] for i in range(11)], axis=0)
    tall = dot(tall, z1[...]) + n2[...].reshape(264, 128)
    tall = dot(tall, z2[...])
    wide = dot(y2[...], lanes([tall[24 * i : 24 * i + 24] for i in range(11)]))
    rows = raise_rows({i - 1: wide[:, 128 * i : 128 * i + 128] for i in range(11)}, 0, 15)
    for i in range(16):
        out[i] = rows[i] + n1[i]


def per_device(charge, kernel_taps, top_x, top_y, top_z):
    where = jnp.stack([lax.axis_index("gx"), lax.axis_index("gy"), lax.axis_index("gz")]).astype(jnp.int32)

    def shift(block, by):
        return lax.ppermute(block, "gx", [(i, (i + by) % 8) for i in range(8)])

    lo1 = shift(charge, 1)
    hi1 = shift(charge, -1)
    lo2 = shift(charge[10:16], 2)
    hi2 = shift(charge[0:6], -2)

    my1, my2, mz1, mz2 = call(
        prep_near,
        [((32, 48), f32), ((24, 80), f32), ((256, 128), f32), ((256, 128), f32)],
        [kernel_taps], smem=(0,),
    )
    wz1, wz2, wz3, my, wx = call(
        prep_top,
        [((1024, 256), bf16)] * 3 + [((16, 64), f32), ((16, 2048), f32)],
        [where, jnp.tile(top_x, 4)[None], jnp.tile(top_y, 2)[None], top_z[None]], smem=(0,),
    )

    n1, n2, q3, to_even, to_odd = call(
        x_step,
        [((16, 32, 128), f32), ((11, 32, 128), f32), ((4, 32, 128), f32), ((456, 128), f32), ((456, 128), f32)],
        [where, kernel_taps, lo2, lo1, charge, hi1, hi2], smem=(0, 1),
        scratch=[pltpu.VMEM((60, 32, 128), f32)],
    )
    from_even = lax.ppermute(to_even, "gy", swap_even)
    from_odd = lax.ppermute(to_odd, "gy", swap_odd)

    n1, n2, q3, to_even, to_odd = call(
        y_step,
        [((16, 32, 128), f32), ((11, 24, 128), f32), ((4, 8, 128), f32), ((112, 128), f32), ((112, 128), f32)],
        [where, n1, n2, q3, from_even, from_odd, my1, my2, jnp.asarray(y_twice)], smem=(0,),
    )
    from_even = lax.ppermute(to_even, "gz", swap_even)
    from_odd = lax.ppermute(to_odd, "gz", swap_odd)

    (message,) = call(
        q3_step, [((64, 8, 128), bf16)],
        [where, q3, from_even, from_odd, jnp.asarray(z_twice_matrix)], smem=(0,),
    )
    gathered = lax.all_to_all(message, ("gy", "gz"), split_axis=0, concat_axis=0, tiled=True)
    n1, n2 = call(
        near_step, [((16, 32, 128), f32), ((11, 24, 128), f32)],
        [where, n1, n2, from_even, from_odd, mz1, mz2], smem=(0,),
    )
    (message,) = call(top_step, [((8, 16, 256), f32)], [gathered, wz1, wz2, wz3, my])
    top = lax.all_to_all(message, "gx", split_axis=0, concat_axis=0, tiled=True)
    (result,) = call(
        last_step, [((16, 32, 128), f32)],
        [top, wx, n1, n2, jnp.asarray(y_raise_top), jnp.asarray(z_raise_top), jnp.asarray(y_raise), jnp.asarray(z_raise)],
    )
    return result


def solution(mesh):
    return jax.shard_map(
        per_device,
        mesh=mesh,
        in_specs=(P("gx", "gy", "gz"), P(), P(), P(), P()),
        out_specs=P("gx", "gy", "gz"),
        check_vma=False,
    )
```

time: 1400 us -> 119 us (0.09)
  waiting for transfers between devices: 1040 us -> 26.3 us
  local copies, waits for them, and re-layouts: 122 us -> 2.97 us
  matrix products: 51.8 us -> 0 us
  starting transfers between devices: 128 us -> 78.2 us
  other arithmetic: 34.4 us -> 0.08 us
  between operations: 14.2 us -> 0.19 us
    all_gather x1 -> x0, waiting for transfers between devices: 1010 us -> none  [per_device(): lax.all_gather(coarse.reshape(1, size_a * size_b * size_c), ('gx', 'gy',...]
    gather x8 -> x0, local copies, waits for them, and re-layouts: 86.9 us -> none  [the longest x6 56.1 us: own_rows(): return jnp.take(profile, (mine - theirs) % length_now)]
    ppermute x24 -> x8, starting transfers between devices: 128 us -> 55.1 us  [the longest x1 13.7 us: per_device(): from_odd = lax.ppermute(to_odd, 'gz', swap_odd)]
    dot_general x36 -> x0, matrix products: 51.8 us -> none  [the longest x32 24.4 us: plane_sum(): jnp.dot(plane.astype(jnp.float32), rows_z.T, precision=highest, preferred...]
    all_to_all x0 -> x2, starting transfers between devices: none -> 23.1 us  [the longest x1 12 us: per_device(): top = lax.all_to_all(message, 'gx', split_axis=0, concat_axis=0, tiled=True)]
    add x10 -> x0, other arithmetic: 22.5 us -> none  [the longest x2 22.2 us: convolve_block(): along_x = along_x + taps_row[offset] * padded[offset:offset + size_x]]
    ppermute x24 -> x8, waiting for transfers between devices: 28.9 us -> 9.76 us  [the longest x1 4.08 us: per_device(): from_odd = lax.ppermute(to_odd, 'gy', swap_odd)]
    all_to_all x0 -> x2, waiting for transfers between devices: none -> 16.5 us  [the longest x1 12.7 us: per_device(): lax.all_to_all(message, ('gy', 'gz'), split_axis=0, concat_axis=0, tiled=...]
  transfers between devices with their start and end apart: 25 -> 10, of which waited for: 15 -> 5; matrix products, arithmetic and copies ran while one was open for 8% -> 1% of each run, Pallas kernels for 0% -> 3%
where the time goes in v1:
time: 119 us
  starting transfers between devices  78.2 us (66%)
  waiting for transfers between devices  26.3 us (22%)
  Pallas kernels  10.9 us (9%)
  local copies, waits for them, and re-layouts  2.97 us (2%)
    ppermute x1, starting transfers between devices, per_device(): from_odd = lax.ppermute(to_odd, 'gz', swap_odd)  13.7 us
    ppermute x4, starting transfers between devices, shift(): return lax.ppermute(block, 'gx', [(i, (i + by) % 8) for i in range(8)])  13.3 us
    ppermute x1, starting transfers between devices, per_device(): from_even = lax.ppermute(to_even, 'gz', swap_even)  13.2 us
    ppermute x1, starting transfers between devices, per_device(): from_odd = lax.ppermute(to_odd, 'gy', swap_odd)  13 us
    all_to_all x1, waiting for transfers between devices, per_device(): lax.all_to_all(message, ('gy', 'gz'), split_axis=0, concat_axis=0, tiled=...  12.7 us
    all_to_all x1, starting transfers between devices, per_device(): top = lax.all_to_all(message, 'gx', split_axis=0, concat_axis=0, tiled=True)  12 us
    all_to_all x1, starting transfers between devices, per_device(): lax.all_to_all(message, ('gy', 'gz'), split_axis=0, concat_axis=0, tiled=...  11.1 us
    pallas_call x8, Pallas kernels, call(): pl.pallas_call(body, out_shape=[jax.ShapeDtypeStruct(s, d) for s, d in ou...  10.9 us
  transfers between devices with their start and end apart: 10, of which 5 were waited for; matrix products, arithmetic and copies ran while one was open for 1% of the time, Pallas kernels for 3%

profile of v1, /device:TPU:1, one launch (start us, length us, event | category | flops | bytes accessed | tf_op | source)
XLA Modules:
  0.0 118.6 jit_solution(16073377726934529911)
XLA Ops:
  0.0 0.0 copy-start
  0.0 2.6 %collective-permute-start.1 = (bf16[16,32,128]{2,1,0:T(8,128)(2,1)}, bf16[16,32,128]{2,1,0:T(8,128)(2,1)S(1)}, u32[]{:S(2)}, u32[]{:S(2)}) collective-permute-start(bf16[16,32,128]{2,1,0:T(8,128)(2,1)} %own.1), channel_id=1, source_target_pairs={{0,64},{64,128},{128,192},{192,256},{256,320},{320,384},{384,448},... | collective-permute-start | bytes 393224 | tf_op jit(solution)/shard_map/ppermute | solution.py:309
  2.6 4.3 %collective-permute-start.2 = (bf16[16,32,128]{2,1,0:T(8,128)(2,1)}, bf16[16,32,128]{2,1,0:T(8,128)(2,1)S(1)}, u32[]{:S(2)}, u32[]{:S(2)}) collective-permute-start(bf16[16,32,128]{2,1,0:T(8,128)(2,1)} %own.1), channel_id=1, source_target_pairs={{0,448},{64,0},{128,64},{192,128},{256,192},{320,256},{384,320},{4... | collective-permute-start | bytes 393224 | tf_op jit(solution)/shard_map/ppermute | solution.py:309
  6.9 0.8 fusion
  7.7 4.5 %collective-permute-start.3 = (bf16[6,32,128]{2,1,0:T(8,128)(2,1)S(1)}, bf16[6,32,128]{2,1,0:T(8,128)(2,1)S(1)}, u32[]{:S(2)}, u32[]{:S(2)}) collective-permute-start(bf16[6,32,128]{2,1,0:T(8,128)(2,1)S(1)} %get-tuple-element.47), channel_id=1, source_target_pairs={{0,384},{64,448},{128,0},{192,64},{256,128},{320,192},{384,256},{4... | collective-permute-start | bytes 147464 | tf_op jit(solution)/shard_map/ppermute | solution.py:309
  12.2 1.9 %collective-permute-start = (bf16[6,32,128]{2,1,0:T(8,128)(2,1)S(1)}, bf16[6,32,128]{2,1,0:T(8,128)(2,1)S(1)}, u32[]{:S(2)}, u32[]{:S(2)}) collective-permute-start(bf16[6,32,128]{2,1,0:T(8,128)(2,1)S(1)} %get-tuple-element.48), channel_id=1, source_target_pairs={{0,128},{64,192},{128,256},{192,320},{256,384},{320,448},{384,0},{... | collective-permute-start | bytes 147464 | tf_op jit(solution)/shard_map/ppermute | solution.py:309
  14.1 0.0 copy-start.7
  14.1 0.1 pad_add_fusion.where
  14.2 0.0 collective-permute-done.3.hi2
  14.2 4.0 %collective-permute-done.lo2 = bf16[6,32,128]{2,1,0:T(8,128)(2,1)S(1)} collective-permute-done((bf16[6,32,128]{2,1,0:T(8,128)(2,1)S(1)}, bf16[6,32,128]{2,1,0:T(8,128)(2,1)S(1)}, u32[]{:S(2)}, u32[]{:S(2)}) %collective-permute-start) | collective-permute-done | bytes 49184 | tf_op jit(solution)/shard_map/ppermute | solution.py:309
  18.2 0.0 collective-permute-done.1.lo1
  18.2 0.0 collective-permute-done.2.hi1
  18.2 0.0 copy-done
  18.3 0.0 copy-done.7
  18.3 1.3 %shard_map.109 = (f32[16,32,128]{2,1,0:T(8,128)S(1)}, f32[11,32,128]{2,1,0:T(8,128)S(1)}, f32[4,32,128]{2,1,0:T(8,128)S(1)}, f32[456,128]{1,0:T(8,128)S(1)}, f32[456,128]{1,0:T(8,128)S(1)}) custom-call(s32[3]{0:T(128)S(1)} %pad_add_fusion.where, f32[2,17]{1,0:T(2,128)S(1)} %copy-done.7, bf16[6,32,128]{2,1,0:T(8,128)(2,1)S(1)} %collective-permute-done.lo2, ...), custom_call_target="tpu_custom_call" | custom-call | flops 1000000 | bytes 1000000 | tf_op jit(solution)/shard_map/pallas_call | solution.py:63
  19.5 1.9 %collective-permute-start.4 = (f32[456,128]{1,0:T(8,128)S(1)}, f32[456,128]{1,0:T(8,128)S(1)}, u32[]{:S(2)}, u32[]{:S(2)}) collective-permute-start(f32[456,128]{1,0:T(8,128)S(1)} %get-tuple-element.29), channel_id=1, source_target_pairs={{0,8},{8,0},{16,24},{24,16},{32,40},{40,32},{48,56},{56,48},{1,9},... | collective-permute-start | bytes 700424 | tf_op jit(solution)/shard_map/ppermute | solution.py:333
  21.4 13.0 %collective-permute-start.5 = (f32[456,128]{1,0:T(8,128)S(1)}, f32[456,128]{1,0:T(8,128)S(1)}, u32[]{:S(2)}, u32[]{:S(2)}) collective-permute-start(f32[456,128]{1,0:T(8,128)S(1)} %get-tuple-element.30), channel_id=1, source_target_pairs={{8,16},{16,8},{24,32},{32,24},{40,48},{48,40},{56,0},{0,56},{9,17}... | collective-permute-start | bytes 700424 | tf_op jit(solution)/shard_map/ppermute | solution.py:334
  34.4 1.0 shard_map.110
  35.4 0.0 collective-permute-done.4.from_even
  35.4 4.1 %collective-permute-done.5.from_odd = f32[456,128]{1,0:T(8,128)S(1)} collective-permute-done((f32[456,128]{1,0:T(8,128)S(1)}, f32[456,128]{1,0:T(8,128)S(1)}, u32[]{:S(2)}, u32[]{:S(2)}) %collective-permute-start.5) | collective-permute-done | bytes 233504 | tf_op jit(solution)/shard_map/ppermute | solution.py:334
  39.5 0.0 copy-start.6
  39.5 0.7 copy-done.6
  40.2 0.0 copy-start.1
  40.2 1.3 %shard_map.111 = (f32[16,32,128]{2,1,0:T(8,128)S(1)}, f32[11,24,128]{2,1,0:T(8,128)S(1)}, f32[4,8,128]{2,1,0:T(8,128)S(1)}, f32[112,128]{1,0:T(8,128)S(1)}, f32[112,128]{1,0:T(8,128)S(1)}) custom-call(s32[3]{0:T(128)S(1)} %pad_add_fusion.where, f32[16,32,128]{2,1,0:T(8,128)S(1)} %get-tuple-element.26.n1, f32[11,32,128]{2,1,0:T(8,128)S(1)} %get-tuple-element.27.n2, ...), custom_call_target="tpu_custom_call" | custom-call | flops 1000000 | bytes 1000000 | tf_op jit(solution)/shard_map/pallas_call | solution.py:63
  41.4 13.2 %collective-permute-start.6 = (f32[112,128]{1,0:T(8,128)S(1)}, f32[112,128]{1,0:T(8,128)S(1)}, u32[]{:S(2)}, u32[]{:S(2)}) collective-permute-start(f32[112,128]{1,0:T(8,128)S(1)} %get-tuple-element.34), channel_id=1, source_target_pairs={{0,1},{1,0},{2,3},{3,2},{4,5},{5,4},{6,7},{7,6},{8,9},{9,8},{10,11... | collective-permute-start | bytes 172040 | tf_op jit(solution)/shard_map/ppermute | solution.py:341
  54.6 13.7 %collective-permute-start.7 = (f32[112,128]{1,0:T(8,128)S(1)}, f32[112,128]{1,0:T(8,128)S(1)}, u32[]{:S(2)}, u32[]{:S(2)}) collective-permute-start(f32[112,128]{1,0:T(8,128)S(1)} %get-tuple-element.35), channel_id=1, source_target_pairs={{1,2},{2,1},{3,4},{4,3},{5,6},{6,5},{7,0},{0,7},{9,10},{10,9},{11,... | collective-permute-start | bytes 172040 | tf_op jit(solution)/shard_map/ppermute | solution.py:342
  68.4 0.0 collective-permute-done.6.from_even
  68.4 1.6 %collective-permute-done.7.from_odd = f32[112,128]{1,0:T(8,128)S(1)} collective-permute-done((f32[112,128]{1,0:T(8,128)S(1)}, f32[112,128]{1,0:T(8,128)S(1)}, u32[]{:S(2)}, u32[]{:S(2)}) %collective-permute-start.7) | collective-permute-done | bytes 57376 | tf_op jit(solution)/shard_map/ppermute | solution.py:342
  70.0 0.0 copy-done.1
  70.0 1.5 %shard_map.112 = bf16[64,8,128]{2,1,0:T(8,128)(2,1)} custom-call(s32[3]{0:T(128)S(1)} %pad_add_fusion.where, f32[4,8,128]{2,1,0:T(8,128)S(1)} %get-tuple-element.33.q3, f32[112,128]{1,0:T(8,128)S(1)} %collective-permute-done.6.from_even, f32[112,128]{1,0:T(8,128)S(1)} %collective-permute-done.7.from_odd, f32[256,128]{1,0:T(8,128)S(1)} %copy-done.1), custom_call_target="tpu_custom_call" | custom-call | flops 1000000 | bytes 1000000 | tf_op jit(solution)/shard_map/pallas_call | solution.py:63
  71.5 0.0 copy-start.10
  71.5 11.1 %all-to-all-start = ((bf16[64,8,128]{2,1,0:T(8,128)(2,1)}), bf16[64,8,128]{2,1,0:T(8,128)(2,1)S(1)}, u32[]{:S(2)}, u32[]{:S(2)}) async-start(bf16[64,8,128]{2,1,0:T(8,128)(2,1)} %shard_map.112), calls=%async_computation | async-start | bytes 262144 | tf_op jit(solution)/shard_map/all_to_all | solution.py:348
  82.6 0.0 copy-done.10
  82.6 0.0 copy-start.9
  82.6 0.1 broadcast_in_dim_tile.7.top_y
  82.7 0.6 copy-done.9
  83.2 0.1 broadcast_in_dim_tile.6.top_x
  83.3 0.0 copy-start.8
  83.3 0.7 copy-done.8
  84.0 1.1 shard_map.113
  85.1 12.7 %all-to-all-done.gathered = bf16[64,8,128]{2,1,0:T(8,128)(2,1)S(1)} async-done(((bf16[64,8,128]{2,1,0:T(8,128)(2,1)}), bf16[64,8,128]{2,1,0:T(8,128)(2,1)S(1)}, u32[]{:S(2)}, u32[]{:S(2)}) %all-to-all-start) | async-done | bytes 131104 | tf_op jit(solution)/shard_map/all_to_all | solution.py:348
  97.7 1.2 %shard_map.114 = f32[8,16,256]{2,1,0:T(8,128)} custom-call(bf16[64,8,128]{2,1,0:T(8,128)(2,1)S(1)} %all-to-all-done.gathered, bf16[1024,256]{1,0:T(8,128)(2,1)S(1)} %get-tuple-element.36.wz1, bf16[1024,256]{1,0:T(8,128)(2,1)S(1)} %get-tuple-element.37.wz2, bf16[1024,256]{1,0:T(8,128)(2,1)S(1)} %get-tuple-element.38.wz3, f32[16,64]{1,0:T(8,128)S(1)} %get-tuple-element.39.my), custom_call_target="tpu_custom_call" | custom-call | flops 1000000 | bytes 1000000 | tf_op jit(solution)/shard_map/pallas_call | solution.py:63
  99.0 12.0 %all-to-all-start.1 = ((f32[8,16,256]{2,1,0:T(8,128)}), f32[8,16,256]{2,1,0:T(8,128)S(1)}, u32[]{:S(2)}, u32[]{:S(2)}) async-start(f32[8,16,256]{2,1,0:T(8,128)} %shard_map.114), calls=%async_computation.1 | async-start | bytes 262144 | tf_op jit(solution)/shard_map/all_to_all | solution.py:354
  111.0 0.0 copy-start.2
  111.0 0.0 copy-start.3
  111.0 0.0 copy-start.4
  111.0 0.0 copy-start.5
  111.0 1.4 %shard_map.115 = (f32[16,32,128]{2,1,0:T(8,128)S(1)}, f32[11,24,128]{2,1,0:T(8,128)S(1)}) custom-call(s32[3]{0:T(128)S(1)} %pad_add_fusion.where, f32[16,32,128]{2,1,0:T(8,128)S(1)} %get-tuple-element.41.n1, f32[11,24,128]{2,1,0:T(8,128)S(1)} %get-tuple-element.42.n2, f32[112,128]{1,0:T(8,128)S(1)} %collective-permute-done.6.from_even, ...), custom_call_target="tpu_custom_call" | custom-call | flops 1000000 | bytes 1000000 | tf_op jit(solution)/shard_map/pallas_call | solution.py:63
  112.4 3.9 %all-to-all-done.1.top = f32[8,16,256]{2,1,0:T(8,128)S(1)} async-done(((f32[8,16,256]{2,1,0:T(8,128)}), f32[8,16,256]{2,1,0:T(8,128)S(1)}, u32[]{:S(2)}, u32[]{:S(2)}) %all-to-all-start.1) | async-done | bytes 131104 | tf_op jit(solution)/shard_map/all_to_all | solution.py:354
  116.3 0.0 copy-done.2
  116.3 0.0 copy-done.3
  116.3 0.0 copy-done.4
  116.3 0.0 copy-done.5
  116.3 2.3 %shard_map.116 = f32[16,32,128]{2,1,0:T(8,128)} custom-call(f32[8,16,256]{2,1,0:T(8,128)S(1)} %all-to-all-done.1.top, f32[16,2048]{1,0:T(8,128)S(1)} %get-tuple-element.40.wx, f32[16,32,128]{2,1,0:T(8,128)S(1)} %get-tuple-element.45.n1, f32[11,24,128]{2,1,0:T(8,128)S(1)} %get-tuple-element.46.n2, f32[24,16]{1,0:T(8,128)S(1)} %copy-done.5, ...), custom_call_target="tpu_custom_call" | custom-call | flops 1000000 | bytes 1000000 | tf_op jit(solution)/shard_map/pallas_call | solution.py:63
  (2 shorter events, 0.0 us)
Async XLA Ops:
  0.0 18.2 %copy-start = (bf16[16,32,128]{2,1,0:T(8,128)(2,1)S(1)}, bf16[16,32,128]{2,1,0:T(8,128)(2,1)}, u32[]{:S(2)}) copy-start(bf16[16,32,128]{2,1,0:T(8,128)(2,1)} %own.1) | copy-start | bytes 393220
  0.0 18.2 %collective-permute-start.1 = (bf16[16,32,128]{2,1,0:T(8,128)(2,1)}, bf16[16,32,128]{2,1,0:T(8,128)(2,1)S(1)}, u32[]{:S(2)}, u32[]{:S(2)}) collective-permute-start(bf16[16,32,128]{2,1,0:T(8,128)(2,1)} %own.1), channel_id=1, source_target_pairs={{0,64},{64,128},{128,192},{192,256},{256,320},{320,384},{384,448},... | collective-permute-start | bytes 393224 | tf_op jit(solution)/shard_map/ppermute | solution.py:309
  2.6 15.6 %collective-permute-start.2 = (bf16[16,32,128]{2,1,0:T(8,128)(2,1)}, bf16[16,32,128]{2,1,0:T(8,128)(2,1)S(1)}, u32[]{:S(2)}, u32[]{:S(2)}) collective-permute-start(bf16[16,32,128]{2,1,0:T(8,128)(2,1)} %own.1), channel_id=1, source_target_pairs={{0,448},{64,0},{128,64},{192,128},{256,192},{320,256},{384,320},{4... | collective-permute-start | bytes 393224 | tf_op jit(solution)/shard_map/ppermute | solution.py:309
  7.7 6.5 %collective-permute-start.3 = (bf16[6,32,128]{2,1,0:T(8,128)(2,1)S(1)}, bf16[6,32,128]{2,1,0:T(8,128)(2,1)S(1)}, u32[]{:S(2)}, u32[]{:S(2)}) collective-permute-start(bf16[6,32,128]{2,1,0:T(8,128)(2,1)S(1)} %get-tuple-element.47), channel_id=1, source_target_pairs={{0,384},{64,448},{128,0},{192,64},{256,128},{320,192},{384,256},{4... | collective-permute-start | bytes 147464 | tf_op jit(solution)/shard_map/ppermute | solution.py:309
  12.2 6.0 %collective-permute-start = (bf16[6,32,128]{2,1,0:T(8,128)(2,1)S(1)}, bf16[6,32,128]{2,1,0:T(8,128)(2,1)S(1)}, u32[]{:S(2)}, u32[]{:S(2)}) collective-permute-start(bf16[6,32,128]{2,1,0:T(8,128)(2,1)S(1)} %get-tuple-element.48), channel_id=1, source_target_pairs={{0,128},{64,192},{128,256},{192,320},{256,384},{320,448},{384,0},{... | collective-permute-start | bytes 147464 | tf_op jit(solution)/shard_map/ppermute | solution.py:309
  14.1 4.1 %copy-start.7 = (f32[2,17]{1,0:T(2,128)S(1)}, f32[2,17]{1,0:T(2,128)}, u32[]{:S(2)}) copy-start(f32[2,17]{1,0:T(2,128)} %taps.3) | copy-start | bytes 412
  19.5 15.9 %collective-permute-start.4 = (f32[456,128]{1,0:T(8,128)S(1)}, f32[456,128]{1,0:T(8,128)S(1)}, u32[]{:S(2)}, u32[]{:S(2)}) collective-permute-start(f32[456,128]{1,0:T(8,128)S(1)} %get-tuple-element.29), channel_id=1, source_target_pairs={{0,8},{8,0},{16,24},{24,16},{32,40},{40,32},{48,56},{56,48},{1,9},... | collective-permute-start | bytes 700424 | tf_op jit(solution)/shard_map/ppermute | solution.py:333
  21.4 18.0 %collective-permute-start.5 = (f32[456,128]{1,0:T(8,128)S(1)}, f32[456,128]{1,0:T(8,128)S(1)}, u32[]{:S(2)}, u32[]{:S(2)}) collective-permute-start(f32[456,128]{1,0:T(8,128)S(1)} %get-tuple-element.30), channel_id=1, source_target_pairs={{8,16},{16,8},{24,32},{32,24},{40,48},{48,40},{56,0},{0,56},{9,17}... | collective-permute-start | bytes 700424 | tf_op jit(solution)/shard_map/ppermute | solution.py:334
  39.5 0.7 copy-start.6
  40.2 29.9 %copy-start.1 = (f32[256,128]{1,0:T(8,128)S(1)}, f32[256,128]{1,0:T(8,128)}, u32[]{:S(2)}) copy-start(f32[256,128]{1,0:T(8,128)} %constant.24.clone.mz3) | copy-start | bytes 393220
  41.4 26.9 %collective-permute-start.6 = (f32[112,128]{1,0:T(8,128)S(1)}, f32[112,128]{1,0:T(8,128)S(1)}, u32[]{:S(2)}, u32[]{:S(2)}) collective-permute-start(f32[112,128]{1,0:T(8,128)S(1)} %get-tuple-element.34), channel_id=1, source_target_pairs={{0,1},{1,0},{2,3},{3,2},{4,5},{5,4},{6,7},{7,6},{8,9},{9,8},{10,11... | collective-permute-start | bytes 172040 | tf_op jit(solution)/shard_map/ppermute | solution.py:341
  54.6 15.4 %collective-permute-start.7 = (f32[112,128]{1,0:T(8,128)S(1)}, f32[112,128]{1,0:T(8,128)S(1)}, u32[]{:S(2)}, u32[]{:S(2)}) collective-permute-start(f32[112,128]{1,0:T(8,128)S(1)} %get-tuple-element.35), channel_id=1, source_target_pairs={{1,2},{2,1},{3,4},{4,3},{5,6},{6,5},{7,0},{0,7},{9,10},{10,9},{11,... | collective-permute-start | bytes 172040 | tf_op jit(solution)/shard_map/ppermute | solution.py:342
  71.5 11.1 %copy-start.10 = (f32[64]{0:T(128)S(1)}, f32[64]{0:T(128)}, u32[]{:S(2)}) copy-start(f32[64]{0:T(128)} %param.14) | copy-start | bytes 772
  71.5 26.3 %all-to-all-start = ((bf16[64,8,128]{2,1,0:T(8,128)(2,1)}), bf16[64,8,128]{2,1,0:T(8,128)(2,1)S(1)}, u32[]{:S(2)}, u32[]{:S(2)}) async-start(bf16[64,8,128]{2,1,0:T(8,128)(2,1)} %shard_map.112), calls=%async_computation | async-start | bytes 262144 | tf_op jit(solution)/shard_map/all_to_all | solution.py:348
  82.6 0.7 copy-start.9
  83.3 0.7 copy-start.8
  99.0 17.3 %all-to-all-start.1 = ((f32[8,16,256]{2,1,0:T(8,128)}), f32[8,16,256]{2,1,0:T(8,128)S(1)}, u32[]{:S(2)}, u32[]{:S(2)}) async-start(f32[8,16,256]{2,1,0:T(8,128)} %shard_map.114), calls=%async_computation.1 | async-start | bytes 262144 | tf_op jit(solution)/shard_map/all_to_all | solution.py:354
  111.0 5.3 %copy-start.2 = (f32[128,128]{1,0:T(8,128)S(1)}, f32[128,128]{1,0:T(8,128)}, u32[]{:S(2)}) copy-start(f32[128,128]{1,0:T(8,128)} %constant.28.clone.z2) | copy-start | bytes 196612
  111.0 5.3 %copy-start.3 = (f32[128,128]{1,0:T(8,128)S(1)}, f32[128,128]{1,0:T(8,128)}, u32[]{:S(2)}) copy-start(f32[128,128]{1,0:T(8,128)} %constant.26.clone.z1) | copy-start | bytes 196612
  111.0 5.3 %copy-start.4 = (f32[32,24]{1,0:T(8,128)S(1)}, f32[32,24]{1,0:T(8,128)}, u32[]{:S(2)}) copy-start(f32[32,24]{1,0:T(8,128)} %constant.27.clone.y2) | copy-start | bytes 9220
  111.0 5.3 %copy-start.5 = (f32[24,16]{1,0:T(8,128)S(1)}, f32[24,16]{1,0:T(8,128)}, u32[]{:S(2)}) copy-start(f32[24,16]{1,0:T(8,128)} %constant.25.clone.y1) | copy-start | bytes 4612

commit v2 on v1

v2 whole, which is shorter than its diff:
```python
import jax
import jax.numpy as jnp
import numpy as np
from jax import lax
from jax.experimental import pallas as pl
from jax.experimental.pallas import tpu as pltpu
from jax.sharding import PartitionSpec as P

f32 = jnp.float32
bf16 = jnp.bfloat16
highest = lax.Precision.HIGHEST
weight = {-3: -1.0 / 16.0, -1: 9.0 / 16.0, 0: 1.0, 1: 9.0 / 16.0, 3: -1.0 / 16.0}

twice = {}
for d0, w0 in weight.items():
    for d1, w1 in weight.items():
        twice[d0 + 2 * d1] = twice.get(d0 + 2 * d1, 0.0) + w0 * w1

swap_even = [(0, 1), (1, 0), (2, 3), (3, 2), (4, 5), (5, 4), (6, 7), (7, 6)]
swap_odd = [(1, 2), (2, 1), (3, 4), (4, 3), (5, 6), (6, 5), (7, 0), (0, 7)]


def table(rows, cols, entry):
    return np.array([[entry(r, c) for c in range(cols)] for r in range(rows)], np.float32)


def z_cell(row, width):
    if row < 128:
        return row
    if row < 128 + width:
        return row - 128 - width
    if row < 128 + 2 * width:
        return row - width
    return None


def z_twice16(row, col):
    cell = z_cell(row, 16)
    return 0.0 if cell is None else twice.get(cell - 4 * (col % 32), 0.0)


z_twice_matrix = table(256, 128, z_twice16)
y_raise_top = table(24, 16, lambda r, c: weight.get((r - 1) - 2 * (c - 2), 0.0) if r < 19 and c < 13 else 0.0)
z_raise_top = table(128, 128, lambda r, c: weight.get((c - 1) - 2 * (r - 2), 0.0) if r < 37 and c < 67 else 0.0)
y_raise = table(32, 24, lambda r, c: weight.get(r - 2 * (c - 1), 0.0) if c < 19 else 0.0)
z_raise = table(128, 128, lambda r, c: weight.get(c - 2 * (r - 1), 0.0) if r < 67 else 0.0)


def dot(a, b):
    return jnp.dot(a, b, precision=highest, preferred_element_type=f32)


def lanes(parts):
    return jnp.concatenate(parts, axis=1)


def iota(shape, dim):
    return lax.broadcasted_iota(jnp.int32, shape, dim)


def call(body, outs, args, smem=(), after=(), flops=1_000_000, bytes_accessed=1_000_000):
    def kernel(*refs):
        body(*refs[: len(args)], *refs[len(args) + len(after) :])

    return pl.pallas_call(
        kernel,
        out_shape=[jax.ShapeDtypeStruct(s, d) for s, d in outs],
        in_specs=[
            pl.BlockSpec(memory_space=pltpu.SMEM if i in smem else pltpu.VMEM)
            for i in range(len(args))
        ]
        + [pl.BlockSpec(memory_space=pl.ANY) for _ in after],
        out_specs=[pl.BlockSpec(memory_space=pltpu.VMEM) for _ in outs],
        compiler_params=pltpu.CompilerParams(vmem_limit_bytes=32 * 1024 * 1024),
        cost_estimate=pl.CostEstimate(
            flops=flops, bytes_accessed=bytes_accessed, transcendentals=0
        ),
        name=body.__name__,
    )(*args, *after)


def pair_taps(taps):
    merged = {}
    for b in range(-8, 9):
        for d, w in weight.items():
            merged.setdefault(2 * b + d, []).append(w * taps[1, b + 8])
    return {m: sum(terms[1:], terms[0]) for m, terms in merged.items()}


def fill(gap, values):
    out = jnp.zeros(gap.shape, f32)
    for m, value in values.items():
        out = jnp.where(gap == m, value, out)
    return out


def prep_y(taps, my):
    def gap(rows, first, step):
        return iota((rows, 80), 1) - 24 - step * (iota((rows, 80), 0) + first)

    single = {m: taps[0, m + 8] for m in range(-8, 9)}
    part = jnp.concatenate(
        [fill(gap(32, 0, 1), single), fill(gap(24, -1, 2), pair_taps(taps)), fill(gap(8, 0, 4), twice)], axis=0
    )
    first = part.astype(bf16)
    rest = part - first.astype(f32)
    second = rest.astype(bf16)
    third = (rest - second.astype(f32)).astype(bf16)
    my[...] = jnp.concatenate([first.astype(f32), second.astype(f32), third.astype(f32)], axis=0).astype(bf16)


def prep_z(taps, mz1, mz2):
    far_off = 1 << 20

    def z_cells(width):
        row = iota((256, 128), 0)
        cell = jnp.where(row < 128, row, jnp.where(row < 128 + width, row - 128 - width, row - width))
        return jnp.where(row < 128 + 2 * width, cell, far_off)

    single = {m: taps[0, m + 8] for m in range(-8, 9)}
    mz1[...] = fill(z_cells(8) - iota((256, 128), 1), single)
    mz2[...] = fill(z_cells(32) - 2 * (iota((256, 128), 1) - 1), pair_taps(taps))


def toeplitz(profile, shift, size):
    start = pltpu.roll(jnp.broadcast_to(profile, (8, size)), shift, 1)[0:1]
    return pltpu.roll(jnp.broadcast_to(start, (size, size)), 0, 1, stride=1, stride_axis=0)


def prep_top(top_x, top_y, top_z, wz1, wz2, wz3, my, wx):
    gx, gy, gz = lax.axis_index("gx"), lax.axis_index("gy"), lax.axis_index("gz")
    tz = toeplitz(top_z[...], lax.rem(258 - 32 * gz, 256), 256)
    lane = iota((256, 256), 1)
    near = jnp.where(lane < 64, tz, 0.0)
    blocks = [near] + [pltpu.roll(near, 64 * a, 1) for a in range(1, 4)]
    for g in range(8):
        for a in range(4):
            rows = pl.ds(128 * g + 32 * a, 32)
            part = blocks[a][32 * g : 32 * g + 32]
            first = part.astype(bf16)
            rest = part - first.astype(f32)
            second = rest.astype(bf16)
            wz1[rows, :] = first
            wz2[rows, :] = second
            wz3[rows, :] = (rest - second.astype(f32)).astype(bf16)
    ty = toeplitz(lanes([top_y[...]] * 2), lax.rem(130 - 8 * gy, 128), 128)
    my[...] = ty.T[0:16, 0:64]
    tx = toeplitz(lanes([top_x[...]] * 4), lax.rem(130 - 4 * gx, 128), 128)
    spread = jnp.where(iota((32, 2048), 1) // 64 == iota((32, 2048), 0), 1.0, 0.0)
    wx[...] = dot(tx.T[0:16, 0:32], spread)


def odd_place(axis):
    return lax.rem(lax.axis_index(axis), 2) == 1


def choose(is_odd, low, high):
    return jnp.where(is_odd, low, high), jnp.where(is_odd, high, low)


def y_send(own, out_even, out_odd):
    is_odd = odd_place("gy")
    cells = own[...].astype(f32)
    low = jnp.concatenate([cells[i, 0:24] for i in range(16)], axis=0)
    high = jnp.concatenate([cells[i, 8:32] for i in range(16)], axis=0)
    even, odd = choose(is_odd, low, high)
    out_even[...] = even.astype(bf16)
    out_odd[...] = odd.astype(bf16)


def y_step(own, from_even, from_odd, my, n1, n2, q3, out_even, out_odd):
    low, high = arrived("gy", from_even, from_odd, pl.ds(0, 384))
    low, high = low.astype(f32), high.astype(f32)
    cells = own[...].astype(f32)
    columns = lanes([
        jnp.concatenate([low[24 * i : 24 * i + 24], cells[i], high[24 * i : 24 * i + 24]], axis=0)
        for i in range(16)
    ])
    terms = jnp.dot(my[...], columns.astype(bf16), preferred_element_type=f32)
    done = terms[0:64] + (terms[64:128] + terms[128:192])
    parts = [done[:, 128 * i : 128 * i + 128] for i in range(16)]
    parts1 = [part[0:32] for part in parts]
    parts2 = [part[32:56] for part in parts]
    parts3 = [part[56:64] for part in parts]
    for i in range(16):
        n1[i] = parts1[i]
        n2[i] = parts2[i]
        q3[i] = parts3[i]

    def pack(parts, width, high):
        lane = iota(parts[0].shape, 1) // width
        out = jnp.zeros(parts[0].shape, f32)
        for s, part in enumerate(parts):
            shift = (width * s + (width if high else 0)) % 128
            moved = part if shift == 0 else pltpu.roll(part, shift, 1)
            out = jnp.where(lane == s, moved, out)
        return out

    def packed(high):
        groups = [pack(parts1, 8, high)]
        groups += [pack(parts2[4 * g : 4 * g + 4], 32, high) for g in range(4)]
        groups += [pack(parts3[8 * g : 8 * g + 8], 16, high) for g in range(2)]
        return jnp.concatenate(groups, axis=0)

    out_even[...], out_odd[...] = choose(odd_place("gz"), packed(False), packed(True))


def arrived(axis, from_even, from_odd, rows):
    is_odd = odd_place(axis)
    even_part, odd_part = from_even[rows, :], from_odd[rows, :]
    return jnp.where(is_odd, even_part, odd_part), jnp.where(is_odd, odd_part, even_part)


def windows(low, high, slot, width):
    down = (128 - width * slot) % 128
    up = (128 + width - width * slot) % 128
    low = low if down == 0 else pltpu.roll(low, down, 1)
    high = high if up == 0 else pltpu.roll(high, up, 1)
    return jnp.where(iota(low.shape, 1) < width, low, high)


def q3_z_step(q3, from_even, from_odd, mz3, out):
    rows = []
    for g in range(2):
        low, high = arrived("gz", from_even, from_odd, pl.ds(128 + 8 * g, 8))
        rows += [lanes([q3[8 * g + s], windows(low, high, s, 16)]) for s in range(8)]
    full = dot(jnp.concatenate(rows, axis=0), mz3[...])
    slot = iota((8, 128), 1) // 32
    for g in range(4):
        block = full[32 * g : 32 * g + 8]
        for s in range(1, 4):
            block = jnp.where(slot == s, full[32 * g + 8 * s : 32 * g + 8 * s + 8], block)
        out[8 * g : 8 * g + 8] = block


def q3_x_step(low, own, high, out):
    groups = {}
    for first, ref in ((-4, low), (0, own), (4, high)):
        for g in range(4):
            groups[first + g] = ref[8 * g : 8 * g + 8]
    slot = iota((8, 128), 1) // 32
    block = jnp.zeros((8, 128), f32)
    for j in range(4):
        total = jnp.zeros((8, 128), f32)
        for q in range(-3, 3):
            factor = fill(slot, {s: twice.get(4 * q + s, 0.0) for s in range(4)})
            total = total + factor * groups[j + q]
        total = total + pltpu.roll(total, 64, 1)
        total = total + pltpu.roll(total, 32, 1)
        block = jnp.where(slot == j, total, block)
    out[...] = jnp.broadcast_to(block.astype(bf16)[None], (64, 8, 128))


def near_z_step(n1, n2, from_even, from_odd, mz1, mz2, n1_out, n2_out, to_low, to_high, to_low2, to_high2):
    low, high = arrived("gz", from_even, from_odd, pl.ds(0, 32))
    rows = jnp.concatenate([lanes([n1[i], windows(low, high, i, 8)]) for i in range(16)], axis=0)
    done1 = dot(rows, mz1[...])
    n1_out[...] = done1.reshape(16, 32, 128)
    rows = []
    for g in range(4):
        low, high = arrived("gz", from_even, from_odd, pl.ds(32 + 24 * g, 24))
        rows += [lanes([n2[4 * g + s], windows(low, high, s, 32)]) for s in range(4)]
    done2 = dot(jnp.concatenate(rows, axis=0), mz2[...])
    n2_out[...] = done2.reshape(16, 24, 128)
    to_low[0:256] = done1[0:256]
    to_low[256:640] = done2
    to_high[0:256] = done1[256:512]
    to_high[256:640] = done2
    to_low2[...] = done2[0:144]
    to_high2[...] = done2[240:384]


def near_x_step(taps, n1, n2, low, high, low2, high2, n1_out, n2_out):
    for t in range(4):
        f = {}
        for i in range(8):
            f[i - 8] = low[32 * i + 8 * t : 32 * i + 8 * t + 8]
            f[i + 16] = high[32 * i + 8 * t : 32 * i + 8 * t + 8]
        for i in range(16):
            f[i] = n1[i, 8 * t : 8 * t + 8]
        for i in range(16):
            total = taps[0, 0] * f[i - 8]
            for a in range(-7, 9):
                total = total + taps[0, a + 8] * f[i + a]
            n1_out[i, 8 * t : 8 * t + 8] = total
    for t in range(3):
        f = {}
        for i in range(16):
            at = 256 + 24 * i + 8 * t
            f[i - 16] = low[at : at + 8]
            f[i + 16] = high[at : at + 8]
            f[i] = n2[i, 8 * t : 8 * t + 8]
        for i in range(6):
            at = 24 * i + 8 * t
            f[i - 22] = low2[at : at + 8]
            f[i + 32] = high2[at : at + 8]
        half = {
            j: f[2 * j]
            + (9.0 / 16.0) * (f[2 * j - 1] + f[2 * j + 1])
            - (1.0 / 16.0) * (f[2 * j - 3] + f[2 * j + 3])
            for j in range(-9, 18)
        }
        for i in range(-1, 10):
            total = taps[1, 0] * half[i - 8]
            for a in range(-7, 9):
                total = total + taps[1, a + 8] * half[i + a]
            n2_out[i + 1, 8 * t : 8 * t + 8] = total


def top_step(gathered, wz1, wz2, wz3, my, out):
    whole = gathered[...].astype(f32).reshape(8, 8, 8, 128)
    rows = lanes([whole[:, g].reshape(64, 128) for g in range(8)]).astype(bf16)
    along_z = jnp.dot(rows, wz1[...], preferred_element_type=f32)
    along_z = along_z + jnp.dot(rows, wz2[...], preferred_element_type=f32)
    along_z = along_z + jnp.dot(rows, wz3[...], preferred_element_type=f32)
    out[...] = jnp.broadcast_to(dot(my[...], along_z)[None], (8, 16, 256))


def raise_rows(rows, first, last):
    out = {}
    for i in range(first, last + 1):
        if i % 2 == 0:
            out[i] = rows[i // 2]
        else:
            j = (i - 1) // 2
            out[i] = (9.0 / 16.0) * (rows[j] + rows[j + 1]) - (1.0 / 16.0) * (rows[j - 1] + rows[j + 2])
    return out


def last_step(top, wx, n1, n2, y1, z1, y2, z2, out):
    e3 = {}
    for i in range(9):
        total = None
        for g in range(8):
            for h in range(2):
                at = 256 * g + 128 * h
                term = wx[i : i + 1, at : at + 128] * top[g, :, 128 * h : 128 * h + 128]
                total = term if total is None else total + term
        e3[i - 2] = total + pltpu.roll(total, 64, 1)
    e2 = raise_rows(e3, -1, 9)
    wide = dot(y1[...], lanes([e2[i] for i in range(-1, 10)]))
    tall = jnp.concatenate([wide[:, 128 * i : 128 * i + 128] for i in range(11)], axis=0)
    tall = dot(tall, z1[...]) + n2[...].reshape(264, 128)
    tall = dot(tall, z2[...])
    wide = dot(y2[...], lanes([tall[24 * i : 24 * i + 24] for i in range(11)]))
    rows = raise_rows({i - 1: wide[:, 128 * i : 128 * i + 128] for i in range(11)}, 0, 15)
    for i in range(16):
        out[i] = rows[i] + n1[i]


def per_device(charge, kernel_taps, top_x, top_y, top_z):
    def shift(block, by):
        return lax.ppermute(block, "gx", [(i, (i + by) % 8) for i in range(8)])

    to_even, to_odd = call(y_send, [((384, 128), bf16)] * 2, [charge])
    from_odd = lax.ppermute(to_odd, "gy", swap_odd)
    from_even = lax.ppermute(to_even, "gy", swap_even)
    (my,) = call(prep_y, [((192, 80), bf16)], [kernel_taps], smem=(0,))
    mz1, mz2 = call(prep_z, [((256, 128), f32)] * 2, [kernel_taps], smem=(0,))
    wz1, wz2, wz3, ty, wx = call(
        prep_top,
        [((1024, 256), bf16)] * 3 + [((16, 64), f32), ((16, 2048), f32)],
        [top_x[None], top_y[None], top_z[None]],
    )

    n1, n2, q3, to_even, to_odd = call(
        y_step,
        [((16, 32, 128), f32), ((16, 24, 128), f32), ((16, 8, 128), f32), ((144, 128), f32), ((144, 128), f32)],
        [charge, from_even, from_odd, my], after=[mz1, wx],
    )
    from_odd = lax.ppermute(to_odd, "gz", swap_odd)
    from_even = lax.ppermute(to_even, "gz", swap_even)

    (q3,) = call(
        q3_z_step, [((32, 128), f32)],
        [q3, from_even, from_odd, jnp.asarray(z_twice_matrix)],
    )
    (message,) = call(q3_x_step, [((64, 8, 128), bf16)], [shift(q3, 1), q3, shift(q3, -1)])
    gathered = lax.all_to_all(message, ("gy", "gz"), split_axis=0, concat_axis=0, tiled=True)

    n1, n2, to_low, to_high, to_low2, to_high2 = call(
        near_z_step,
        [((16, 32, 128), f32), ((16, 24, 128), f32)] + [((640, 128), f32)] * 2 + [((144, 128), f32)] * 2,
        [n1, n2, from_even, from_odd, mz1, mz2], after=[message],
    )
    n1, n2 = call(
        near_x_step, [((16, 32, 128), f32), ((11, 24, 128), f32)],
        [kernel_taps, n1, n2, shift(to_high, 1), shift(to_low, -1), shift(to_high2, 2), shift(to_low2, -2)],
        smem=(0,),
    )
    (message,) = call(top_step, [((8, 16, 256), f32)], [gathered, wz1, wz2, wz3, ty], after=[n1])
    top = lax.all_to_all(message, "gx", split_axis=0, concat_axis=0, tiled=True)
    (result,) = call(
        last_step, [((16, 32, 128), f32)],
        [top, wx, n1, n2, jnp.asarray(y_raise_top), jnp.asarray(z_raise_top), jnp.asarray(y_raise), jnp.asarray(z_raise)],
    )
    return result


def solution(mesh):
    return jax.shard_map(
        per_device,
        mesh=mesh,
        in_specs=(P("gx", "gy", "gz"), P(), P(), P(), P()),
        out_specs=P("gx", "gy", "gz"),
        check_vma=False,
    )
```

time: 119 us -> 98.8 us (0.83)
  starting transfers between devices: 78.2 us -> 60.9 us
  blocking collectives: 0 us -> 11.2 us
  waiting for transfers between devices: 26.3 us -> 15.8 us
  Pallas kernels: 10.9 us -> 8.7 us
  local copies, waits for them, and re-layouts: 2.97 us -> 1.63 us
    all_to_all x1 -> x0, starting transfers between devices: 12 us -> none  [per_device(): top = lax.all_to_all(message, 'gx', split_axis=0, concat_axis=0, tiled=True)]
    ppermute x1, starting transfers between devices: 13.2 us -> 1.92 us  [per_device(): from_even = lax.ppermute(to_even, 'gz', swap_even)]
    all_to_all x0 -> x1, blocking collectives: none -> 11.2 us  [per_device(): top = lax.all_to_all(message, 'gx', split_axis=0, concat_axis=0, tiled=True)]
    all_to_all x1, waiting for transfers between devices: 12.7 us -> 4.53 us  [per_device(): lax.all_to_all(message, ('gy', 'gz'), split_axis=0, concat_axis=0, tiled=...]
    all_to_all x1, starting transfers between devices: 11.1 us -> 15.3 us  [per_device(): lax.all_to_all(message, ('gy', 'gz'), split_axis=0, concat_axis=0, tiled=...]
    ppermute x1, starting transfers between devices: 13 us -> 17.1 us  [per_device(): from_odd = lax.ppermute(to_odd, 'gy', swap_odd)]
    all_to_all x1 -> x0, waiting for transfers between devices: 3.87 us -> none  [per_device(): top = lax.all_to_all(message, 'gx', split_axis=0, concat_axis=0, tiled=True)]
    ppermute x1, starting transfers between devices: 13.7 us -> 11.4 us  [per_device(): from_odd = lax.ppermute(to_odd, 'gz', swap_odd)]
  transfers between devices with their start and end apart: 10 -> 11, of which waited for: 5 -> 7; matrix products, arithmetic and copies ran while one was open for 1% -> 0% of each run, Pallas kernels for 3% -> 4%
where the time goes in v2:
time: 98.8 us; the launch traced here: 98.4 us
  starting transfers between devices  60.9 us (62%)
  waiting for transfers between devices  15.8 us (16%)
  blocking collectives  11.2 us (11%)
  Pallas kernels  8.7 us (9%)
  local copies, waits for them, and re-layouts  1.63 us (2%)
    ppermute x1, starting transfers between devices, per_device(): from_odd = lax.ppermute(to_odd, 'gy', swap_odd)  17.1 us
    all_to_all x1, starting transfers between devices, per_device(): lax.all_to_all(message, ('gy', 'gz'), split_axis=0, concat_axis=0, tiled=...  15.3 us
    ppermute x1, starting transfers between devices, per_device(): from_odd = lax.ppermute(to_odd, 'gz', swap_odd)  11.4 us
    all_to_all x1, blocking collectives, per_device(): top = lax.all_to_all(message, 'gx', split_axis=0, concat_axis=0, tiled=True)  11.2 us
    ppermute x6, starting transfers between devices, shift(): return lax.ppermute(block, 'gx', [(i, (i + by) % 8) for i in range(8)])  11 us
    pallas_call x11, Pallas kernels, call(): pl.pallas_call(kernel, out_shape=[jax.ShapeDtypeStruct(s, d) for s, d in...  8.7 us
    ppermute x6, waiting for transfers between devices, shift(): return lax.ppermute(block, 'gx', [(i, (i + by) % 8) for i in range(8)])  5.13 us
    all_to_all x1, waiting for transfers between devices, per_device(): lax.all_to_all(message, ('gy', 'gz'), split_axis=0, concat_axis=0, tiled=...  4.53 us
  transfers between devices with their start and end apart: 11, of which 7 were waited for; matrix products, arithmetic and copies ran while one was open for 0% of the time, Pallas kernels for 4%

profile of v2, /device:TPU:1, one launch (start us, length us, event | category | flops | bytes accessed | tf_op | source)
XLA Modules:
  0.0 98.4 jit_solution(8501173981902225574)
XLA Ops:
  0.0 0.0 copy-start
  0.0 0.9 copy-done
  0.9 0.0 copy-start.1
  1.0 0.0 copy-start.7
  1.0 4.2 %collective-permute-start = (bf16[384,128]{1,0:T(8,128)(2,1)S(1)}, bf16[384,128]{1,0:T(8,128)(2,1)S(1)}, u32[]{:S(2)}, u32[]{:S(2)}) collective-permute-start(bf16[384,128]{1,0:T(8,128)(2,1)S(1)} %get-tuple-element.27), channel_id=1, source_target_pairs={{0,8},{8,0},{16,24},{24,16},{32,40},{40,32},{48,56},{56,48},{1,9},... | collective-permute-start | bytes 294920 | tf_op jit(solution)/shard_map/ppermute | solution.py:357
  5.1 17.1 %collective-permute-start.1 = (bf16[384,128]{1,0:T(8,128)(2,1)S(1)}, bf16[384,128]{1,0:T(8,128)(2,1)S(1)}, u32[]{:S(2)}, u32[]{:S(2)}) collective-permute-start(bf16[384,128]{1,0:T(8,128)(2,1)S(1)} %get-tuple-element.28), channel_id=1, source_target_pairs={{8,16},{16,8},{24,32},{32,24},{40,48},{48,40},{56,0},{0,56},{9,17}... | collective-permute-start | bytes 294920 | tf_op jit(solution)/shard_map/ppermute | solution.py:356
  22.2 0.0 copy-done.7
  22.2 0.9 prep_z.1
  23.1 0.6 prep_y.1.refs_3_
  23.8 0.0 copy-start.10
  23.8 0.0 copy-start.8
  23.8 0.0 copy-start.9
  23.8 0.6 copy-done.10
  24.4 0.0 copy-done.8
  24.5 0.0 copy-done.9
  24.5 0.6 prep_top.1
  25.1 0.0 collective-permute-done.refs_1_
  25.1 4.3 %collective-permute-done.1.refs_2_ = bf16[384,128]{1,0:T(8,128)(2,1)S(1)} collective-permute-done((bf16[384,128]{1,0:T(8,128)(2,1)S(1)}, bf16[384,128]{1,0:T(8,128)(2,1)S(1)}, u32[]{:S(2)}, u32[]{:S(2)}) %collective-permute-start.1) | collective-permute-done | bytes 98336 | tf_op jit(solution)/shard_map/ppermute | solution.py:356
  29.3 0.0 copy-done.1
  29.3 0.0 copy-start.2
  29.3 0.5 y_step.1
  29.8 1.9 %collective-permute-start.2 = (f32[144,128]{1,0:T(8,128)S(1)}, f32[144,128]{1,0:T(8,128)S(1)}, u32[]{:S(2)}, u32[]{:S(2)}) collective-permute-start(f32[144,128]{1,0:T(8,128)S(1)} %get-tuple-element.32), channel_id=1, source_target_pairs={{0,1},{1,0},{2,3},{3,2},{4,5},{5,4},{6,7},{7,6},{8,9},{9,8},{10,11... | collective-permute-start | bytes 221192 | tf_op jit(solution)/shard_map/ppermute | solution.py:372
  31.8 11.4 %collective-permute-start.3 = (f32[144,128]{1,0:T(8,128)S(1)}, f32[144,128]{1,0:T(8,128)S(1)}, u32[]{:S(2)}, u32[]{:S(2)}) collective-permute-start(f32[144,128]{1,0:T(8,128)S(1)} %get-tuple-element.33), channel_id=1, source_target_pairs={{1,2},{2,1},{3,4},{4,3},{5,6},{6,5},{7,0},{0,7},{9,10},{10,9},{11,... | collective-permute-start | bytes 221192 | tf_op jit(solution)/shard_map/ppermute | solution.py:371
  43.1 0.0 collective-permute-done.2.refs_1_.refs_2_
  43.1 1.8 %collective-permute-done.3.refs_2_.refs_3_ = f32[144,128]{1,0:T(8,128)S(1)} collective-permute-done((f32[144,128]{1,0:T(8,128)S(1)}, f32[144,128]{1,0:T(8,128)S(1)}, u32[]{:S(2)}, u32[]{:S(2)}) %collective-permute-start.3) | collective-permute-done | bytes 73760 | tf_op jit(solution)/shard_map/ppermute | solution.py:371
  45.0 0.0 copy-done.2
  45.0 0.3 q3_z_step.1.refs_1_
  45.3 4.0 %collective-permute-start.4 = (f32[32,128]{1,0:T(8,128)S(1)}, f32[32,128]{1,0:T(8,128)S(1)}, u32[]{:S(2)}, u32[]{:S(2)}) collective-permute-start(f32[32,128]{1,0:T(8,128)S(1)} %q3_z_step.1.refs_1_), channel_id=1, source_target_pairs={{0,64},{64,128},{128,192},{192,256},{256,320},{320,384},{384,448},... | collective-permute-start | bytes 49160 | tf_op jit(solution)/shard_map/ppermute | solution.py:353
  49.3 0.0 collective-permute-start.5
  49.3 0.9 collective-permute-done.4.refs_0_
  50.2 2.3 %collective-permute-done.5.refs_2_ = f32[32,128]{1,0:T(8,128)S(1)} collective-permute-done((f32[32,128]{1,0:T(8,128)S(1)}, f32[32,128]{1,0:T(8,128)S(1)}, u32[]{:S(2)}, u32[]{:S(2)}) %collective-permute-start.5) | collective-permute-done | bytes 16416 | tf_op jit(solution)/shard_map/ppermute | solution.py:353
  52.5 0.8 q3_x_step.1.refs_6_
  53.3 15.3 %all-to-all-start = ((bf16[64,8,128]{2,1,0:T(8,128)(2,1)}), bf16[64,8,128]{2,1,0:T(8,128)(2,1)S(1)}, u32[]{:S(2)}, u32[]{:S(2)}) async-start(bf16[64,8,128]{2,1,0:T(8,128)(2,1)} %q3_x_step.1.refs_6_), calls=%async_computation | async-start | bytes 262144 | tf_op jit(solution)/shard_map/all_to_all | solution.py:379
  68.6 1.0 near_z_step.1
  69.6 0.3 collective-permute-start.6
  69.9 0.2 collective-permute-start.7
  70.1 3.1 %collective-permute-start.8 = (f32[144,128]{1,0:T(8,128)S(1)}, f32[144,128]{1,0:T(8,128)S(1)}, u32[]{:S(2)}, u32[]{:S(2)}) collective-permute-start(f32[144,128]{1,0:T(8,128)S(1)} %get-tuple-element.45), channel_id=1, source_target_pairs={{0,128},{64,192},{128,256},{192,320},{256,384},{320,448},{384,0},{... | collective-permute-start | bytes 221192 | tf_op jit(solution)/shard_map/ppermute | solution.py:353
  73.2 3.4 %collective-permute-start.9 = (f32[144,128]{1,0:T(8,128)S(1)}, f32[144,128]{1,0:T(8,128)S(1)}, u32[]{:S(2)}, u32[]{:S(2)}) collective-permute-start(f32[144,128]{1,0:T(8,128)S(1)} %get-tuple-element.46), channel_id=1, source_target_pairs={{0,384},{64,448},{128,0},{192,64},{256,128},{320,192},{384,256},{4... | collective-permute-start | bytes 221192 | tf_op jit(solution)/shard_map/ppermute | solution.py:353
  76.6 1.5 %collective-permute-done.8.refs_5_ = f32[144,128]{1,0:T(8,128)S(1)} collective-permute-done((f32[144,128]{1,0:T(8,128)S(1)}, f32[144,128]{1,0:T(8,128)S(1)}, u32[]{:S(2)}, u32[]{:S(2)}) %collective-permute-start.8) | collective-permute-done | bytes 73760 | tf_op jit(solution)/shard_map/ppermute | solution.py:353
  78.1 0.5 collective-permute-done.9.refs_6_
  78.6 0.0 collective-permute-done.6.refs_3_
  78.6 0.0 collective-permute-done.7.refs_4_
  78.6 1.1 %near_x_step.1 = (f32[16,32,128]{2,1,0:T(8,128)S(1)}, f32[11,24,128]{2,1,0:T(8,128)S(1)}) custom-call(f32[2,17]{1,0:T(2,128)S(1)} %copy-done.7, f32[16,32,128]{2,1,0:T(8,128)S(1)} %get-tuple-element.41.refs_1_, f32[16,24,128]{2,1,0:T(8,128)S(1)} %get-tuple-element.42.refs_2_, f32[640,128]{1,0:T(8,128)S(1)} %collective-permute-done.6.refs_3_, ...), custom_call_target="tpu_custom_call" | custom-call | flops 1000000 | bytes 1000000 | tf_op jit(solution)/shard_map/near_x_step/pallas_call | solution.py:65
  79.7 4.5 %all-to-all-done.refs_0_ = bf16[64,8,128]{2,1,0:T(8,128)(2,1)S(1)} async-done(((bf16[64,8,128]{2,1,0:T(8,128)(2,1)}), bf16[64,8,128]{2,1,0:T(8,128)(2,1)S(1)}, u32[]{:S(2)}, u32[]{:S(2)}) %all-to-all-start) | async-done | bytes 131104 | tf_op jit(solution)/shard_map/all_to_all | solution.py:379
  84.2 0.6 top_step.1
  84.8 0.0 copy-start.3
  84.8 0.0 copy-start.4
  84.8 0.0 copy-start.5
  84.8 0.0 copy-start.6
  84.9 11.2 %all_to_all.10.refs_0_ = f32[8,16,256]{2,1,0:T(8,128)S(1)} all-to-all(f32[8,16,256]{2,1,0:T(8,128)S(1)} %top_step.1), channel_id=1, replica_groups=mesh['gx'=8,'gy'=8,'gz'=8] {'gx'}, dimensions={0} | all-to-all | bytes 262144 | tf_op jit(solution)/shard_map/all_to_all | solution.py:392
  96.1 0.0 copy-done.3
  96.1 0.0 copy-done.4
  96.1 0.0 copy-done.5
  96.1 0.0 copy-done.6
  96.1 2.3 %last_step.1 = f32[16,32,128]{2,1,0:T(8,128)} custom-call(f32[8,16,256]{2,1,0:T(8,128)S(1)} %all_to_all.10.refs_0_, f32[16,2048]{1,0:T(8,128)S(1)} %get-tuple-element.30.refs_5_.refs_1_, f32[16,32,128]{2,1,0:T(8,128)S(1)} %get-tuple-element.47.refs_5_.refs_2_, f32[11,24,128]{2,1,0:T(8,128)S(1)} %get-tuple-element.48.refs_3_, f32[24,16]{1,0:T(8,128)S(1)} %copy-done.6, ...), custom_call_target="tpu_custom_call" | custom-call | flops 1000000 | bytes 1000000 | tf_op jit(solution)/shard_map/last_step/pallas_call | solution.py:65
  (1 shorter events, 0.0 us)
Async XLA Ops:
  0.0 0.9 copy-start
  0.9 28.4 %copy-start.1 = (bf16[16,32,128]{2,1,0:T(8,128)(2,1)S(1)}, bf16[16,32,128]{2,1,0:T(8,128)(2,1)}, u32[]{:S(2)}) copy-start(bf16[16,32,128]{2,1,0:T(8,128)(2,1)} %refs_0_.8) | copy-start | bytes 393220
  1.0 21.3 %copy-start.7 = (f32[2,17]{1,0:T(2,128)S(1)}, f32[2,17]{1,0:T(2,128)}, u32[]{:S(2)}) copy-start(f32[2,17]{1,0:T(2,128)} %refs_0_.9) | copy-start | bytes 412
  1.0 24.1 %collective-permute-start = (bf16[384,128]{1,0:T(8,128)(2,1)S(1)}, bf16[384,128]{1,0:T(8,128)(2,1)S(1)}, u32[]{:S(2)}, u32[]{:S(2)}) collective-permute-start(bf16[384,128]{1,0:T(8,128)(2,1)S(1)} %get-tuple-element.27), channel_id=1, source_target_pairs={{0,8},{8,0},{16,24},{24,16},{32,40},{40,32},{48,56},{56,48},{1,9},... | collective-permute-start | bytes 294920 | tf_op jit(solution)/shard_map/ppermute | solution.py:357
  5.1 24.2 %collective-permute-start.1 = (bf16[384,128]{1,0:T(8,128)(2,1)S(1)}, bf16[384,128]{1,0:T(8,128)(2,1)S(1)}, u32[]{:S(2)}, u32[]{:S(2)}) collective-permute-start(bf16[384,128]{1,0:T(8,128)(2,1)S(1)} %get-tuple-element.28), channel_id=1, source_target_pairs={{8,16},{16,8},{24,32},{32,24},{40,48},{48,40},{56,0},{0,56},{9,17}... | collective-permute-start | bytes 294920 | tf_op jit(solution)/shard_map/ppermute | solution.py:356
  23.8 0.7 copy-start.10
  23.8 0.7 copy-start.8
  23.8 0.7 copy-start.9
  29.3 15.6 %copy-start.2 = (f32[256,128]{1,0:T(8,128)S(1)}, f32[256,128]{1,0:T(8,128)}, u32[]{:S(2)}) copy-start(f32[256,128]{1,0:T(8,128)} %constant.10.clone.refs_3_) | copy-start | bytes 393220
  29.8 13.3 %collective-permute-start.2 = (f32[144,128]{1,0:T(8,128)S(1)}, f32[144,128]{1,0:T(8,128)S(1)}, u32[]{:S(2)}, u32[]{:S(2)}) collective-permute-start(f32[144,128]{1,0:T(8,128)S(1)} %get-tuple-element.32), channel_id=1, source_target_pairs={{0,1},{1,0},{2,3},{3,2},{4,5},{5,4},{6,7},{7,6},{8,9},{9,8},{10,11... | collective-permute-start | bytes 221192 | tf_op jit(solution)/shard_map/ppermute | solution.py:372
  31.8 13.2 %collective-permute-start.3 = (f32[144,128]{1,0:T(8,128)S(1)}, f32[144,128]{1,0:T(8,128)S(1)}, u32[]{:S(2)}, u32[]{:S(2)}) collective-permute-start(f32[144,128]{1,0:T(8,128)S(1)} %get-tuple-element.33), channel_id=1, source_target_pairs={{1,2},{2,1},{3,4},{4,3},{5,6},{6,5},{7,0},{0,7},{9,10},{10,9},{11,... | collective-permute-start | bytes 221192 | tf_op jit(solution)/shard_map/ppermute | solution.py:371
  45.3 4.9 %collective-permute-start.4 = (f32[32,128]{1,0:T(8,128)S(1)}, f32[32,128]{1,0:T(8,128)S(1)}, u32[]{:S(2)}, u32[]{:S(2)}) collective-permute-start(f32[32,128]{1,0:T(8,128)S(1)} %q3_z_step.1.refs_1_), channel_id=1, source_target_pairs={{0,64},{64,128},{128,192},{192,256},{256,320},{320,384},{384,448},... | collective-permute-start | bytes 49160 | tf_op jit(solution)/shard_map/ppermute | solution.py:353
  49.3 3.2 %collective-permute-start.5 = (f32[32,128]{1,0:T(8,128)S(1)}, f32[32,128]{1,0:T(8,128)S(1)}, u32[]{:S(2)}, u32[]{:S(2)}) collective-permute-start(f32[32,128]{1,0:T(8,128)S(1)} %q3_z_step.1.refs_1_), channel_id=1, source_target_pairs={{0,448},{64,0},{128,64},{192,128},{256,192},{320,256},{384,320},{4... | collective-permute-start | bytes 49160 | tf_op jit(solution)/shard_map/ppermute | solution.py:353
  53.3 30.9 %all-to-all-start = ((bf16[64,8,128]{2,1,0:T(8,128)(2,1)}), bf16[64,8,128]{2,1,0:T(8,128)(2,1)S(1)}, u32[]{:S(2)}, u32[]{:S(2)}) async-start(bf16[64,8,128]{2,1,0:T(8,128)(2,1)} %q3_x_step.1.refs_6_), calls=%async_computation | async-start | bytes 262144 | tf_op jit(solution)/shard_map/all_to_all | solution.py:379
  69.6 9.0 %collective-permute-start.6 = (f32[640,128]{1,0:T(8,128)S(1)}, f32[640,128]{1,0:T(8,128)S(1)}, u32[]{:S(2)}, u32[]{:S(2)}) collective-permute-start(f32[640,128]{1,0:T(8,128)S(1)} %get-tuple-element.43), channel_id=1, source_target_pairs={{0,64},{64,128},{128,192},{192,256},{256,320},{320,384},{384,448},... | collective-permute-start | bytes 983048 | tf_op jit(solution)/shard_map/ppermute | solution.py:353
  69.9 8.7 %collective-permute-start.7 = (f32[640,128]{1,0:T(8,128)S(1)}, f32[640,128]{1,0:T(8,128)S(1)}, u32[]{:S(2)}, u32[]{:S(2)}) collective-permute-start(f32[640,128]{1,0:T(8,128)S(1)} %get-tuple-element.44), channel_id=1, source_target_pairs={{0,448},{64,0},{128,64},{192,128},{256,192},{320,256},{384,320},{4... | collective-permute-start | bytes 983048 | tf_op jit(solution)/shard_map/ppermute | solution.py:353
  70.1 8.1 %collective-permute-start.8 = (f32[144,128]{1,0:T(8,128)S(1)}, f32[144,128]{1,0:T(8,128)S(1)}, u32[]{:S(2)}, u32[]{:S(2)}) collective-permute-start(f32[144,128]{1,0:T(8,128)S(1)} %get-tuple-element.45), channel_id=1, source_target_pairs={{0,128},{64,192},{128,256},{192,320},{256,384},{320,448},{384,0},{... | collective-permute-start | bytes 221192 | tf_op jit(solution)/shard_map/ppermute | solution.py:353
  73.2 5.4 %collective-permute-start.9 = (f32[144,128]{1,0:T(8,128)S(1)}, f32[144,128]{1,0:T(8,128)S(1)}, u32[]{:S(2)}, u32[]{:S(2)}) collective-permute-start(f32[144,128]{1,0:T(8,128)S(1)} %get-tuple-element.46), channel_id=1, source_target_pairs={{0,384},{64,448},{128,0},{192,64},{256,128},{320,192},{384,256},{4... | collective-permute-start | bytes 221192 | tf_op jit(solution)/shard_map/ppermute | solution.py:353
  84.8 11.3 %copy-start.3 = (f32[128,128]{1,0:T(8,128)S(1)}, f32[128,128]{1,0:T(8,128)}, u32[]{:S(2)}) copy-start(f32[128,128]{1,0:T(8,128)} %constant.12.clone.refs_5_) | copy-start | bytes 196612
  84.8 11.3 %copy-start.4 = (f32[128,128]{1,0:T(8,128)S(1)}, f32[128,128]{1,0:T(8,128)}, u32[]{:S(2)}) copy-start(f32[128,128]{1,0:T(8,128)} %constant.14.clone.refs_7_) | copy-start | bytes 196612
  84.8 11.3 %copy-start.5 = (f32[32,24]{1,0:T(8,128)S(1)}, f32[32,24]{1,0:T(8,128)}, u32[]{:S(2)}) copy-start(f32[32,24]{1,0:T(8,128)} %constant.13.clone.refs_6_) | copy-start | bytes 9220
  84.8 11.3 %copy-start.6 = (f32[24,16]{1,0:T(8,128)S(1)}, f32[24,16]{1,0:T(8,128)}, u32[]{:S(2)}) copy-start(f32[24,16]{1,0:T(8,128)} %constant.11.clone.refs_4_) | copy-start | bytes 4612

commit v3 on v2

--- a/solution.py
+++ b/solution.py
@@ -50,6 +50,19 @@
     return jnp.dot(a, b, precision=highest, preferred_element_type=f32)
 
 
+def halves(x):
+    first = x.astype(bf16)
+    return first, (x - first.astype(f32)).astype(bf16)
+
+
+def from_left(m, x):
+    return sum(jnp.dot(m[...], term, preferred_element_type=f32) for term in halves(x))
+
+
+def from_right(x, m):
+    return sum(jnp.dot(term, m[...], preferred_element_type=f32) for term in halves(x))
+
+
 def lanes(parts):
     return jnp.concatenate(parts, axis=1)
 
@@ -59,6 +72,7 @@
 
 
 def call(body, outs, args, smem=(), after=(), flops=1_000_000, bytes_accessed=1_000_000):
+
     def kernel(*refs):
         body(*refs[: len(args)], *refs[len(args) + len(after) :])
 
@@ -96,7 +110,9 @@
 
 def prep_y(taps, my):
     def gap(rows, first, step):
-        return iota((rows, 80), 1) - 24 - step * (iota((rows, 80), 0) + first)
+        column = iota((rows, 76), 1)
+        cell = jnp.where(column < 32, column, jnp.where(column < 54, column - 54, column - 22))
+        return cell - step * (iota((rows, 76), 0) + first)
 
     single = {m: taps[0, m + 8] for m in range(-8, 9)}
     part = jnp.concatenate(
@@ -127,7 +143,7 @@
     return pltpu.roll(jnp.broadcast_to(start, (size, size)), 0, 1, stride=1, stride_axis=0)
 
 
-def prep_top(top_x, top_y, top_z, wz1, wz2, wz3, my, wx):
+def prep_top(top_x, top_y, top_z, wz1, wz2, my, wx):
     gx, gy, gz = lax.axis_index("gx"), lax.axis_index("gy"), lax.axis_index("gz")
     tz = toeplitz(top_z[...], lax.rem(258 - 32 * gz, 256), 256)
     lane = iota((256, 256), 1)
@@ -137,12 +153,7 @@
         for a in range(4):
             rows = pl.ds(128 * g + 32 * a, 32)
             part = blocks[a][32 * g : 32 * g + 32]
-            first = part.astype(bf16)
-            rest = part - first.astype(f32)
-            second = rest.astype(bf16)
-            wz1[rows, :] = first
-            wz2[rows, :] = second
-            wz3[rows, :] = (rest - second.astype(f32)).astype(bf16)
+            wz1[rows, :], wz2[rows, :] = halves(part)
     ty = toeplitz(lanes([top_y[...]] * 2), lax.rem(130 - 8 * gy, 128), 128)
     my[...] = ty.T[0:16, 0:64]
     tx = toeplitz(lanes([top_x[...]] * 4), lax.rem(130 - 4 * gx, 128), 128)
@@ -161,19 +172,19 @@
 def y_send(own, out_even, out_odd):
     is_odd = odd_place("gy")
     cells = own[...].astype(f32)
-    low = jnp.concatenate([cells[i, 0:24] for i in range(16)], axis=0)
-    high = jnp.concatenate([cells[i, 8:32] for i in range(16)], axis=0)
+    low = jnp.concatenate([cells[i, 0:22] for i in range(16)], axis=0)
+    high = jnp.concatenate([cells[i, 10:32] for i in range(16)], axis=0)
     even, odd = choose(is_odd, low, high)
     out_even[...] = even.astype(bf16)
     out_odd[...] = odd.astype(bf16)
 
 
-def y_step(own, from_even, from_odd, my, n1, n2, q3, out_even, out_odd):
-    low, high = arrived("gy", from_even, from_odd, pl.ds(0, 384))
+def y_step(own, from_odd, from_even, my, n1, n2, q3, out_even, out_odd):
+    low, high = arrived("gy", from_even, from_odd, pl.ds(0, 352))
     low, high = low.astype(f32), high.astype(f32)
     cells = own[...].astype(f32)
     columns = lanes([
-        jnp.concatenate([low[24 * i : 24 * i + 24], cells[i], high[24 * i : 24 * i + 24]], axis=0)
+        jnp.concatenate([cells[i], low[22 * i : 22 * i + 22], high[22 * i : 22 * i + 22]], axis=0)
         for i in range(16)
     ])
     terms = jnp.dot(my[...], columns.astype(bf16), preferred_element_type=f32)
@@ -219,7 +230,7 @@
     return jnp.where(iota(low.shape, 1) < width, low, high)
 
 
-def q3_z_step(q3, from_even, from_odd, mz3, out):
+def q3_z_step(q3, from_odd, from_even, mz3, out):
     rows = []
     for g in range(2):
         low, high = arrived("gz", from_even, from_odd, pl.ds(128 + 8 * g, 8))
@@ -248,10 +259,11 @@
         total = total + pltpu.roll(total, 64, 1)
         total = total + pltpu.roll(total, 32, 1)
         block = jnp.where(slot == j, total, block)
-    out[...] = jnp.broadcast_to(block.astype(bf16)[None], (64, 8, 128))
-
-
-def near_z_step(n1, n2, from_even, from_odd, mz1, mz2, n1_out, n2_out, to_low, to_high, to_low2, to_high2):
+    pair = jnp.concatenate([block, block], axis=0).astype(bf16)
+    out[...] = jnp.broadcast_to(pair[None], (32, 16, 128))
+
+
+def near_z_step(n1, n2, from_odd, from_even, mz1, mz2, n1_out, n2_out, to_low, to_high, to_low2, to_high2):
     low, high = arrived("gz", from_even, from_odd, pl.ds(0, 32))
     rows = jnp.concatenate([lanes([n1[i], windows(low, high, i, 8)]) for i in range(16)], axis=0)
     done1 = dot(rows, mz1[...])
@@ -261,13 +273,21 @@
         low, high = arrived("gz", from_even, from_odd, pl.ds(32 + 24 * g, 24))
         rows += [lanes([n2[4 * g + s], windows(low, high, s, 32)]) for s in range(4)]
     done2 = dot(jnp.concatenate(rows, axis=0), mz2[...])
-    n2_out[...] = done2.reshape(16, 24, 128)
     to_low[0:256] = done1[0:256]
-    to_low[256:640] = done2
     to_high[0:256] = done1[256:512]
-    to_high[256:640] = done2
-    to_low2[...] = done2[0:144]
-    to_high2[...] = done2[240:384]
+    for j in range(-1, 10):
+        share = jnp.zeros((24, 128), f32)
+        for d, w in weight.items():
+            if 0 <= 2 * j + d < 16:
+                share = share + w * done2[24 * (2 * j + d) : 24 * (2 * j + d) + 24]
+        at = 256 + 24 * (j + 1)
+        n2_out[j + 1] = share
+        to_low[at : at + 24] = share
+        to_high[at : at + 24] = share
+        if j < 2:
+            to_low2[24 * (j + 1) : 24 * (j + 1) + 24] = share
+        if j > 6:
+            to_high2[24 * (j - 7) : 24 * (j - 7) + 24] = share
 
 
 def near_x_step(taps, n1, n2, low, high, low2, high2, n1_out, n2_out):
@@ -284,22 +304,15 @@
                 total = total + taps[0, a + 8] * f[i + a]
             n1_out[i, 8 * t : 8 * t + 8] = total
     for t in range(3):
-        f = {}
-        for i in range(16):
-            at = 256 + 24 * i + 8 * t
-            f[i - 16] = low[at : at + 8]
-            f[i + 16] = high[at : at + 8]
-            f[i] = n2[i, 8 * t : 8 * t + 8]
-        for i in range(6):
-            at = 24 * i + 8 * t
-            f[i - 22] = low2[at : at + 8]
-            f[i + 32] = high2[at : at + 8]
-        half = {
-            j: f[2 * j]
-            + (9.0 / 16.0) * (f[2 * j - 1] + f[2 * j + 1])
-            - (1.0 / 16.0) * (f[2 * j - 3] + f[2 * j + 3])
-            for j in range(-9, 18)
-        }
+        half = {}
+        for j in range(-1, 10):
+            at = 256 + 24 * (j + 1) + 8 * t
+            for place, part in ((j - 8, low[at : at + 8]), (j, n2[j + 1, 8 * t : 8 * t + 8]), (j + 8, high[at : at + 8])):
+                half[place] = half[place] + part if place in half else part
+        for k in range(3):
+            at = 24 * k + 8 * t
+            half[k - 9] = half[k - 9] + low2[at : at + 8]
+            half[k + 15] = half[k + 15] + high2[at : at + 8]
         for i in range(-1, 10):
             total = taps[1, 0] * half[i - 8]
             for a in range(-7, 9):
@@ -307,12 +320,11 @@
             n2_out[i + 1, 8 * t : 8 * t + 8] = total
 
 
-def top_step(gathered, wz1, wz2, wz3, my, out):
+def top_step(gathered, wz1, wz2, my, out):
     whole = gathered[...].astype(f32).reshape(8, 8, 8, 128)
     rows = lanes([whole[:, g].reshape(64, 128) for g in range(8)]).astype(bf16)
     along_z = jnp.dot(rows, wz1[...], preferred_element_type=f32)
     along_z = along_z + jnp.dot(rows, wz2[...], preferred_element_type=f32)
-    along_z = along_z + jnp.dot(rows, wz3[...], preferred_element_type=f32)
     out[...] = jnp.broadcast_to(dot(my[...], along_z)[None], (8, 16, 256))
 
 
@@ -338,11 +350,11 @@
                 total = term if total is None else total + term
         e3[i - 2] = total + pltpu.roll(total, 64, 1)
     e2 = raise_rows(e3, -1, 9)
-    wide = dot(y1[...], lanes([e2[i] for i in range(-1, 10)]))
+    wide = from_left(y1, lanes([e2[i] for i in range(-1, 10)]))
     tall = jnp.concatenate([wide[:, 128 * i : 128 * i + 128] for i in range(11)], axis=0)
-    tall = dot(tall, z1[...]) + n2[...].reshape(264, 128)
-    tall = dot(tall, z2[...])
-    wide = dot(y2[...], lanes([tall[24 * i : 24 * i + 24] for i in range(11)]))
+    tall = from_right(tall, z1) + n2[...].reshape(264, 128)
+    tall = from_right(tall, z2)
+    wide = from_left(y2, lanes([tall[24 * i : 24 * i + 24] for i in range(11)]))
     rows = raise_rows({i - 1: wide[:, 128 * i : 128 * i + 128] for i in range(11)}, 0, 15)
     for i in range(16):
         out[i] = rows[i] + n1[i]
@@ -352,47 +364,48 @@
     def shift(block, by):
         return lax.ppermute(block, "gx", [(i, (i + by) % 8) for i in range(8)])
 
-    to_even, to_odd = call(y_send, [((384, 128), bf16)] * 2, [charge])
+    to_even, to_odd = call(y_send, [((352, 128), bf16)] * 2, [charge])
     from_odd = lax.ppermute(to_odd, "gy", swap_odd)
     from_even = lax.ppermute(to_even, "gy", swap_even)
-    (my,) = call(prep_y, [((192, 80), bf16)], [kernel_taps], smem=(0,))
+    (my,) = call(prep_y, [((192, 76), bf16)], [kernel_taps], smem=(0,))
     mz1, mz2 = call(prep_z, [((256, 128), f32)] * 2, [kernel_taps], smem=(0,))
-    wz1, wz2, wz3, ty, wx = call(
+    wz1, wz2, ty, wx = call(
         prep_top,
-        [((1024, 256), bf16)] * 3 + [((16, 64), f32), ((16, 2048), f32)],
+        [((1024, 256), bf16)] * 2 + [((16, 64), f32), ((16, 2048), f32)],
         [top_x[None], top_y[None], top_z[None]],
     )
 
     n1, n2, q3, to_even, to_odd = call(
         y_step,
         [((16, 32, 128), f32), ((16, 24, 128), f32), ((16, 8, 128), f32), ((144, 128), f32), ((144, 128), f32)],
-        [charge, from_even, from_odd, my], after=[mz1, wx],
+        [charge, from_odd, from_even, my], after=[mz1, wx],
     )
     from_odd = lax.ppermute(to_odd, "gz", swap_odd)
     from_even = lax.ppermute(to_even, "gz", swap_even)
 
     (q3,) = call(
         q3_z_step, [((32, 128), f32)],
-        [q3, from_even, from_odd, jnp.asarray(z_twice_matrix)],
-    )
-    (message,) = call(q3_x_step, [((64, 8, 128), bf16)], [shift(q3, 1), q3, shift(q3, -1)])
-    gathered = lax.all_to_all(message, ("gy", "gz"), split_axis=0, concat_axis=0, tiled=True)
-
+        [q3, from_odd, from_even, jnp.asarray(z_twice_matrix)],
+    )
+    (message,) = call(q3_x_step, [((32, 16, 128), bf16)], [shift(q3, 1), q3, shift(q3, -1)])
+    gathered = lax.all_to_all(
+        message.reshape(64, 8, 128), ("gy", "gz"), split_axis=0, concat_axis=0, tiled=True
+    )
     n1, n2, to_low, to_high, to_low2, to_high2 = call(
         near_z_step,
-        [((16, 32, 128), f32), ((16, 24, 128), f32)] + [((640, 128), f32)] * 2 + [((144, 128), f32)] * 2,
-        [n1, n2, from_even, from_odd, mz1, mz2], after=[message],
-    )
+        [((16, 32, 128), f32), ((11, 24, 128), f32)] + [((520, 128), f32)] * 2 + [((72, 128), f32)] * 2,
+        [n1, n2, from_odd, from_even, mz1, mz2], after=[message],
+    )
+    halos = [shift(to_high, 1), shift(to_low, -1), shift(to_high2, 2), shift(to_low2, -2)]
+    (message,) = call(top_step, [((8, 16, 256), f32)], [gathered, wz1, wz2, ty], after=halos)
     n1, n2 = call(
         near_x_step, [((16, 32, 128), f32), ((11, 24, 128), f32)],
-        [kernel_taps, n1, n2, shift(to_high, 1), shift(to_low, -1), shift(to_high2, 2), shift(to_low2, -2)],
-        smem=(0,),
-    )
-    (message,) = call(top_step, [((8, 16, 256), f32)], [gathered, wz1, wz2, wz3, ty], after=[n1])
+        [kernel_taps, n1, n2, *halos], smem=(0,), after=[message],
+    )
     top = lax.all_to_all(message, "gx", split_axis=0, concat_axis=0, tiled=True)
     (result,) = call(
         last_step, [((16, 32, 128), f32)],
-        [top, wx, n1, n2, jnp.asarray(y_raise_top), jnp.asarray(z_raise_top), jnp.asarray(y_raise), jnp.asarray(z_raise)],
+        [top, wx, n1, n2, *(jnp.asarray(m, bf16) for m in (y_raise_top, z_raise_top, y_raise, z_raise))],
     )
     return result
 

time: 98.8 us -> 92.3 us (0.934)
  blocking collectives: 11.2 us -> 0 us
  waiting for transfers between devices: 15.8 us -> 23.7 us
  starting transfers between devices: 60.9 us -> 57.9 us
    all_to_all x1 -> x0, blocking collectives: 11.2 us -> none  [per_device(): top = lax.all_to_all(message, 'gx', split_axis=0, concat_axis=0, tiled=True)]
    ppermute x1, starting transfers between devices: 11.4 us -> 3.77 us  [per_device(): from_odd = lax.ppermute(to_odd, 'gz', swap_odd)]
    all_to_all x1 -> x2, starting transfers between devices: 15.3 us -> 21.4 us  [the longest x1 15 us: per_device(): lax.all_to_all(message.reshape(64, 8, 128), ('gy', 'gz'), split_axis=0, c...]
    all_to_all x1 -> x2, waiting for transfers between devices: 4.53 us -> 10.2 us  [the longest x1 5.98 us: per_device(): lax.all_to_all(message.reshape(64, 8, 128), ('gy', 'gz'), split_axis=0, c...]
    ppermute x1, waiting for transfers between devices: 1.84 us -> 6.14 us  [per_device(): from_odd = lax.ppermute(to_odd, 'gz', swap_odd)]
    ppermute x1, starting transfers between devices: 4.17 us -> 1.92 us  [per_device(): from_even = lax.ppermute(to_even, 'gy', swap_even)]
    ppermute x1, starting transfers between devices: 17.1 us -> 18.9 us  [per_device(): from_odd = lax.ppermute(to_odd, 'gy', swap_odd)]
    ppermute x1, waiting for transfers between devices: 4.25 us -> 2.56 us  [per_device(): from_odd = lax.ppermute(to_odd, 'gy', swap_odd)]
  transfers between devices with their start and end apart: 11 -> 12, of which waited for: 7 -> 8; matrix products, arithmetic and copies ran while one was open for 0% -> 0% of each run, Pallas kernels for 4% -> 4%
where the time goes in v3:
time: 92.3 us; the launch traced here: 91.9 us
  starting transfers between devices  57.9 us (63%)
  waiting for transfers between devices  23.7 us (26%)
  Pallas kernels  8.51 us (9%)
  local copies, waits for them, and re-layouts  1.61 us (2%)
    ppermute x1, starting transfers between devices, per_device(): from_odd = lax.ppermute(to_odd, 'gy', swap_odd)  18.9 us
    all_to_all x1, starting transfers between devices, per_device(): lax.all_to_all(message.reshape(64, 8, 128), ('gy', 'gz'), split_axis=0, c...  15 us
    ppermute x6, starting transfers between devices, shift(): return lax.ppermute(block, 'gx', [(i, (i + by) % 8) for i in range(8)])  9.98 us
    pallas_call x11, Pallas kernels, call(): pl.pallas_call(kernel, out_shape=[jax.ShapeDtypeStruct(s, d) for s, d in...  8.51 us
    all_to_all x1, starting transfers between devices, per_device(): top = lax.all_to_all(message, 'gx', split_axis=0, concat_axis=0, tiled=True)  6.46 us
    ppermute x1, waiting for transfers between devices, per_device(): from_odd = lax.ppermute(to_odd, 'gz', swap_odd)  6.14 us
    all_to_all x1, waiting for transfers between devices, per_device(): lax.all_to_all(message.reshape(64, 8, 128), ('gy', 'gz'), split_axis=0, c...  5.98 us
    ppermute x6, waiting for transfers between devices, shift(): return lax.ppermute(block, 'gx', [(i, (i + by) % 8) for i in range(8)])  4.76 us
  transfers between devices with their start and end apart: 12, of which 8 were waited for; matrix products, arithmetic and copies ran while one was open for 0% of the time, Pallas kernels for 4%

profile of v3, /device:TPU:1, one launch (start us, length us, event | category | flops | bytes accessed | tf_op | source)
XLA Modules:
  0.0 91.9 jit_solution(14032286019190853272)
XLA Ops:
  0.0 0.0 copy-start
  0.0 0.9 copy-done
  0.9 0.0 copy-start.1
  0.9 0.1 y_send.1
  1.0 0.0 copy-start.7
  1.0 18.9 %collective-permute-start = (bf16[352,128]{1,0:T(8,128)(2,1)S(1)}, bf16[352,128]{1,0:T(8,128)(2,1)S(1)}, u32[]{:S(2)}, u32[]{:S(2)}) collective-permute-start(bf16[352,128]{1,0:T(8,128)(2,1)S(1)} %get-tuple-element.26), channel_id=1, source_target_pairs={{8,16},{16,8},{24,32},{32,24},{40,48},{48,40},{56,0},{0,56},{9,17}... | collective-permute-start | bytes 270344 | tf_op jit(solution)/shard_map/ppermute | solution.py:368
  19.8 1.9 %collective-permute-start.1 = (bf16[352,128]{1,0:T(8,128)(2,1)S(1)}, bf16[352,128]{1,0:T(8,128)(2,1)S(1)}, u32[]{:S(2)}, u32[]{:S(2)}) collective-permute-start(bf16[352,128]{1,0:T(8,128)(2,1)S(1)} %get-tuple-element.27), channel_id=1, source_target_pairs={{0,8},{8,0},{16,24},{24,16},{32,40},{40,32},{48,56},{56,48},{1,9},... | collective-permute-start | bytes 270344 | tf_op jit(solution)/shard_map/ppermute | solution.py:369
  21.8 0.0 copy-done.7
  21.8 0.9 prep_z.1
  22.7 0.6 prep_y.1.refs_3_
  23.3 0.0 copy-start.10
  23.3 0.0 copy-start.8
  23.3 0.0 copy-start.9
  23.3 0.6 copy-done.10
  24.0 0.0 copy-done.8
  24.0 0.0 copy-done.9
  24.0 0.6 prep_top.1
  24.6 2.6 %collective-permute-done.refs_1_ = bf16[352,128]{1,0:T(8,128)(2,1)S(1)} collective-permute-done((bf16[352,128]{1,0:T(8,128)(2,1)S(1)}, bf16[352,128]{1,0:T(8,128)(2,1)S(1)}, u32[]{:S(2)}, u32[]{:S(2)}) %collective-permute-start) | collective-permute-done | bytes 90144 | tf_op jit(solution)/shard_map/ppermute | solution.py:368
  27.1 0.0 collective-permute-done.1.refs_2_
  27.2 0.0 copy-done.1
  27.2 0.0 copy-start.2
  27.2 0.5 y_step.1
  27.7 3.8 %collective-permute-start.2 = (f32[144,128]{1,0:T(8,128)S(1)}, f32[144,128]{1,0:T(8,128)S(1)}, u32[]{:S(2)}, u32[]{:S(2)}) collective-permute-start(f32[144,128]{1,0:T(8,128)S(1)} %get-tuple-element.31), channel_id=1, source_target_pairs={{1,2},{2,1},{3,4},{4,3},{5,6},{6,5},{7,0},{0,7},{9,10},{10,9},{11,... | collective-permute-start | bytes 221192 | tf_op jit(solution)/shard_map/ppermute | solution.py:383
  31.4 1.9 %collective-permute-start.3 = (f32[144,128]{1,0:T(8,128)S(1)}, f32[144,128]{1,0:T(8,128)S(1)}, u32[]{:S(2)}, u32[]{:S(2)}) collective-permute-start(f32[144,128]{1,0:T(8,128)S(1)} %get-tuple-element.32), channel_id=1, source_target_pairs={{0,1},{1,0},{2,3},{3,2},{4,5},{5,4},{6,7},{7,6},{8,9},{9,8},{10,11... | collective-permute-start | bytes 221192 | tf_op jit(solution)/shard_map/ppermute | solution.py:384
  33.4 6.1 %collective-permute-done.2.refs_1_.refs_2_ = f32[144,128]{1,0:T(8,128)S(1)} collective-permute-done((f32[144,128]{1,0:T(8,128)S(1)}, f32[144,128]{1,0:T(8,128)S(1)}, u32[]{:S(2)}, u32[]{:S(2)}) %collective-permute-start.2) | collective-permute-done | bytes 73760 | tf_op jit(solution)/shard_map/ppermute | solution.py:383
  39.5 0.0 collective-permute-done.3.refs_2_.refs_3_
  39.5 0.0 copy-done.2
  39.5 0.3 q3_z_step.1.refs_1_
  39.8 3.0 %collective-permute-start.4 = (f32[32,128]{1,0:T(8,128)S(1)}, f32[32,128]{1,0:T(8,128)S(1)}, u32[]{:S(2)}, u32[]{:S(2)}) collective-permute-start(f32[32,128]{1,0:T(8,128)S(1)} %q3_z_step.1.refs_1_), channel_id=1, source_target_pairs={{0,64},{64,128},{128,192},{192,256},{256,320},{320,384},{384,448},... | collective-permute-start | bytes 49160 | tf_op jit(solution)/shard_map/ppermute | solution.py:365
  42.8 0.0 collective-permute-start.5
  42.8 0.9 collective-permute-done.4.refs_0_
  43.7 2.3 %collective-permute-done.5.refs_2_ = f32[32,128]{1,0:T(8,128)S(1)} collective-permute-done((f32[32,128]{1,0:T(8,128)S(1)}, f32[32,128]{1,0:T(8,128)S(1)}, u32[]{:S(2)}, u32[]{:S(2)}) %collective-permute-start.5) | collective-permute-done | bytes 16416 | tf_op jit(solution)/shard_map/ppermute | solution.py:365
  46.0 0.8 q3_x_step.1.refs_6_
  46.8 15.0 %all-to-all-start = ((bf16[64,8,128]{2,1,0:T(8,128)(2,1)}), bf16[64,8,128]{2,1,0:T(8,128)(2,1)S(1)}, u32[]{:S(2)}, u32[]{:S(2)}) async-start(bf16[64,8,128]{2,1,0:T(8,128)(2,1)} %bitcast.3), calls=%async_computation | async-start | bytes 262144 | tf_op jit(solution)/shard_map/all_to_all | solution.py:391
  61.8 1.0 %near_z_step.1 = (f32[16,32,128]{2,1,0:T(8,128)S(1)}, f32[11,24,128]{2,1,0:T(8,128)S(1)}, f32[520,128]{1,0:T(8,128)S(1)}, f32[520,128]{1,0:T(8,128)S(1)}, f32[72,128]{1,0:T(8,128)S(1)}, /*index=5*/f32[72,128]{1,0:T(8,128)S(1)}) custom-call(f32[16,32,128]{2,1,0:T(8,128)S(1)} %get-tuple-element.36.refs_0_, f32[16,24,128]{2,1,0:T(8,128)S(1)} %get-tuple-element.37.refs_1_, ...), custom_call_target="tpu_custom_call" | custom-call | flops 1000000 | bytes 1000000 | tf_op jit(solution)/shard_map/near_z_step/pallas_call | solution.py:79
  62.7 0.3 collective-permute-start.6
  63.0 0.2 collective-permute-start.7
  63.2 3.1 %collective-permute-start.8 = (f32[72,128]{1,0:T(8,128)S(1)}, f32[72,128]{1,0:T(8,128)S(1)}, u32[]{:S(2)}, u32[]{:S(2)}) collective-permute-start(f32[72,128]{1,0:T(8,128)S(1)} %get-tuple-element.41), channel_id=1, source_target_pairs={{0,128},{64,192},{128,256},{192,320},{256,384},{320,448},{384,0},{... | collective-permute-start | bytes 110600 | tf_op jit(solution)/shard_map/ppermute | solution.py:365
  66.4 3.4 %collective-permute-start.9 = (f32[72,128]{1,0:T(8,128)S(1)}, f32[72,128]{1,0:T(8,128)S(1)}, u32[]{:S(2)}, u32[]{:S(2)}) collective-permute-start(f32[72,128]{1,0:T(8,128)S(1)} %get-tuple-element.42), channel_id=1, source_target_pairs={{0,384},{64,448},{128,0},{192,64},{256,128},{320,192},{384,256},{4... | collective-permute-start | bytes 110600 | tf_op jit(solution)/shard_map/ppermute | solution.py:365
  69.8 0.5 collective-permute-done.8.refs_6_.refs_5_
  70.2 1.1 %collective-permute-done.9.refs_7_.refs_6_ = f32[72,128]{1,0:T(8,128)S(1)} collective-permute-done((f32[72,128]{1,0:T(8,128)S(1)}, f32[72,128]{1,0:T(8,128)S(1)}, u32[]{:S(2)}, u32[]{:S(2)}) %collective-permute-start.9) | collective-permute-done | bytes 36896 | tf_op jit(solution)/shard_map/ppermute | solution.py:365
  71.4 0.0 collective-permute-done.6.refs_4_.refs_3_
  71.4 0.0 collective-permute-done.7.refs_5_.refs_4_
  71.4 6.0 %all-to-all-done.refs_0_ = bf16[64,8,128]{2,1,0:T(8,128)(2,1)S(1)} async-done(((bf16[64,8,128]{2,1,0:T(8,128)(2,1)}), bf16[64,8,128]{2,1,0:T(8,128)(2,1)S(1)}, u32[]{:S(2)}, u32[]{:S(2)}) %all-to-all-start) | async-done | bytes 131104 | tf_op jit(solution)/shard_map/all_to_all | solution.py:391
  77.4 1.2 %top_step.1.refs_7_ = f32[8,16,256]{2,1,0:T(8,128)} custom-call(bf16[64,8,128]{2,1,0:T(8,128)(2,1)S(1)} %all-to-all-done.refs_0_, bf16[1024,256]{1,0:T(8,128)(2,1)S(1)} %get-tuple-element.33.refs_1_, bf16[1024,256]{1,0:T(8,128)(2,1)S(1)} %get-tuple-element.34.refs_2_, f32[16,64]{1,0:T(8,128)S(1)} %get-tuple-element.35.refs_3_, ...), custom_call_target="tpu_custom_call" | custom-call | flops 1000000 | bytes 1000000 | tf_op jit(solution)/shard_map/top_step/pallas_call | solution.py:79
  78.5 6.5 %all-to-all-start.1 = ((f32[8,16,256]{2,1,0:T(8,128)}), f32[8,16,256]{2,1,0:T(8,128)S(1)}, u32[]{:S(2)}, u32[]{:S(2)}) async-start(f32[8,16,256]{2,1,0:T(8,128)} %top_step.1.refs_7_), calls=%async_computation.1 | async-start | bytes 262144 | tf_op jit(solution)/shard_map/all_to_all | solution.py:405
  85.0 0.0 copy-start.3
  85.0 0.0 copy-start.4
  85.0 0.0 copy-start.5
  85.0 0.0 copy-start.6
  85.0 1.0 %near_x_step.1 = (f32[16,32,128]{2,1,0:T(8,128)S(1)}, f32[11,24,128]{2,1,0:T(8,128)S(1)}) custom-call(f32[2,17]{1,0:T(2,128)S(1)} %copy-done.7, f32[16,32,128]{2,1,0:T(8,128)S(1)} %get-tuple-element.43.refs_1_, f32[11,24,128]{2,1,0:T(8,128)S(1)} %get-tuple-element.44.refs_2_, f32[520,128]{1,0:T(8,128)S(1)} %collective-permute-done.6.refs_4_.refs_3_, ...), custom_call_target="tpu_custom_call" | custom-call | flops 1000000 | bytes 1000000 | tf_op jit(solution)/shard_map/near_x_step/pallas_call | solution.py:79
  86.0 4.2 %all-to-all-done.1.refs_0_ = f32[8,16,256]{2,1,0:T(8,128)S(1)} async-done(((f32[8,16,256]{2,1,0:T(8,128)}), f32[8,16,256]{2,1,0:T(8,128)S(1)}, u32[]{:S(2)}, u32[]{:S(2)}) %all-to-all-start.1) | async-done | bytes 131104 | tf_op jit(solution)/shard_map/all_to_all | solution.py:405
  90.2 0.0 copy-done.3
  90.2 0.0 copy-done.4
  90.3 0.0 copy-done.5
  90.3 0.0 copy-done.6
  90.3 1.6 %last_step.1 = f32[16,32,128]{2,1,0:T(8,128)} custom-call(f32[8,16,256]{2,1,0:T(8,128)S(1)} %all-to-all-done.1.refs_0_, f32[16,2048]{1,0:T(8,128)S(1)} %get-tuple-element.29.refs_5_.refs_1_, f32[16,32,128]{2,1,0:T(8,128)S(1)} %get-tuple-element.45.refs_2_, f32[11,24,128]{2,1,0:T(8,128)S(1)} %get-tuple-element.46.refs_3_, bf16[24,16]{1,0:T(8,128)(2,1)S(1)} %copy-done.6, ...), custom_call_target="tpu_custom_call" | custom-call | flops 1000000 | bytes 1000000 | tf_op jit(solution)/shard_map/last_step/pallas_call | solution.py:79
Async XLA Ops:
  0.0 0.9 copy-start
  0.9 26.2 %copy-start.1 = (bf16[16,32,128]{2,1,0:T(8,128)(2,1)S(1)}, bf16[16,32,128]{2,1,0:T(8,128)(2,1)}, u32[]{:S(2)}) copy-start(bf16[16,32,128]{2,1,0:T(8,128)(2,1)} %refs_0_.8) | copy-start | bytes 393220
  1.0 20.8 %copy-start.7 = (f32[2,17]{1,0:T(2,128)S(1)}, f32[2,17]{1,0:T(2,128)}, u32[]{:S(2)}) copy-start(f32[2,17]{1,0:T(2,128)} %refs_0_.9) | copy-start | bytes 412
  1.0 26.2 %collective-permute-start = (bf16[352,128]{1,0:T(8,128)(2,1)S(1)}, bf16[352,128]{1,0:T(8,128)(2,1)S(1)}, u32[]{:S(2)}, u32[]{:S(2)}) collective-permute-start(bf16[352,128]{1,0:T(8,128)(2,1)S(1)} %get-tuple-element.26), channel_id=1, source_target_pairs={{8,16},{16,8},{24,32},{32,24},{40,48},{48,40},{56,0},{0,56},{9,17}... | collective-permute-start | bytes 270344 | tf_op jit(solution)/shard_map/ppermute | solution.py:368
  19.8 7.3 %collective-permute-start.1 = (bf16[352,128]{1,0:T(8,128)(2,1)S(1)}, bf16[352,128]{1,0:T(8,128)(2,1)S(1)}, u32[]{:S(2)}, u32[]{:S(2)}) collective-permute-start(bf16[352,128]{1,0:T(8,128)(2,1)S(1)} %get-tuple-element.27), channel_id=1, source_target_pairs={{0,8},{8,0},{16,24},{24,16},{32,40},{40,32},{48,56},{56,48},{1,9},... | collective-permute-start | bytes 270344 | tf_op jit(solution)/shard_map/ppermute | solution.py:369
  23.3 0.7 copy-start.10
  23.3 0.7 copy-start.8
  23.3 0.7 copy-start.9
  27.2 12.4 %copy-start.2 = (f32[256,128]{1,0:T(8,128)S(1)}, f32[256,128]{1,0:T(8,128)}, u32[]{:S(2)}) copy-start(f32[256,128]{1,0:T(8,128)} %constant.10.clone.refs_3_) | copy-start | bytes 393220
  27.7 11.8 %collective-permute-start.2 = (f32[144,128]{1,0:T(8,128)S(1)}, f32[144,128]{1,0:T(8,128)S(1)}, u32[]{:S(2)}, u32[]{:S(2)}) collective-permute-start(f32[144,128]{1,0:T(8,128)S(1)} %get-tuple-element.31), channel_id=1, source_target_pairs={{1,2},{2,1},{3,4},{4,3},{5,6},{6,5},{7,0},{0,7},{9,10},{10,9},{11,... | collective-permute-start | bytes 221192 | tf_op jit(solution)/shard_map/ppermute | solution.py:383
  31.4 8.1 %collective-permute-start.3 = (f32[144,128]{1,0:T(8,128)S(1)}, f32[144,128]{1,0:T(8,128)S(1)}, u32[]{:S(2)}, u32[]{:S(2)}) collective-permute-start(f32[144,128]{1,0:T(8,128)S(1)} %get-tuple-element.32), channel_id=1, source_target_pairs={{0,1},{1,0},{2,3},{3,2},{4,5},{5,4},{6,7},{7,6},{8,9},{9,8},{10,11... | collective-permute-start | bytes 221192 | tf_op jit(solution)/shard_map/ppermute | solution.py:384
  39.8 3.8 %collective-permute-start.4 = (f32[32,128]{1,0:T(8,128)S(1)}, f32[32,128]{1,0:T(8,128)S(1)}, u32[]{:S(2)}, u32[]{:S(2)}) collective-permute-start(f32[32,128]{1,0:T(8,128)S(1)} %q3_z_step.1.refs_1_), channel_id=1, source_target_pairs={{0,64},{64,128},{128,192},{192,256},{256,320},{320,384},{384,448},... | collective-permute-start | bytes 49160 | tf_op jit(solution)/shard_map/ppermute | solution.py:365
  42.8 3.2 %collective-permute-start.5 = (f32[32,128]{1,0:T(8,128)S(1)}, f32[32,128]{1,0:T(8,128)S(1)}, u32[]{:S(2)}, u32[]{:S(2)}) collective-permute-start(f32[32,128]{1,0:T(8,128)S(1)} %q3_z_step.1.refs_1_), channel_id=1, source_target_pairs={{0,448},{64,0},{128,64},{192,128},{256,192},{320,256},{384,320},{4... | collective-permute-start | bytes 49160 | tf_op jit(solution)/shard_map/ppermute | solution.py:365
  46.8 30.6 %all-to-all-start = ((bf16[64,8,128]{2,1,0:T(8,128)(2,1)}), bf16[64,8,128]{2,1,0:T(8,128)(2,1)S(1)}, u32[]{:S(2)}, u32[]{:S(2)}) async-start(bf16[64,8,128]{2,1,0:T(8,128)(2,1)} %bitcast.3), calls=%async_computation | async-start | bytes 262144 | tf_op jit(solution)/shard_map/all_to_all | solution.py:391
  62.7 8.6 %collective-permute-start.6 = (f32[520,128]{1,0:T(8,128)S(1)}, f32[520,128]{1,0:T(8,128)S(1)}, u32[]{:S(2)}, u32[]{:S(2)}) collective-permute-start(f32[520,128]{1,0:T(8,128)S(1)} %get-tuple-element.39), channel_id=1, source_target_pairs={{0,64},{64,128},{128,192},{192,256},{256,320},{320,384},{384,448},... | collective-permute-start | bytes 798728 | tf_op jit(solution)/shard_map/ppermute | solution.py:365
  63.0 8.3 %collective-permute-start.7 = (f32[520,128]{1,0:T(8,128)S(1)}, f32[520,128]{1,0:T(8,128)S(1)}, u32[]{:S(2)}, u32[]{:S(2)}) collective-permute-start(f32[520,128]{1,0:T(8,128)S(1)} %get-tuple-element.40), channel_id=1, source_target_pairs={{0,448},{64,0},{128,64},{192,128},{256,192},{320,256},{384,320},{4... | collective-permute-start | bytes 798728 | tf_op jit(solution)/shard_map/ppermute | solution.py:365
  63.2 7.0 %collective-permute-start.8 = (f32[72,128]{1,0:T(8,128)S(1)}, f32[72,128]{1,0:T(8,128)S(1)}, u32[]{:S(2)}, u32[]{:S(2)}) collective-permute-start(f32[72,128]{1,0:T(8,128)S(1)} %get-tuple-element.41), channel_id=1, source_target_pairs={{0,128},{64,192},{128,256},{192,320},{256,384},{320,448},{384,0},{... | collective-permute-start | bytes 110600 | tf_op jit(solution)/shard_map/ppermute | solution.py:365
  66.4 5.0 %collective-permute-start.9 = (f32[72,128]{1,0:T(8,128)S(1)}, f32[72,128]{1,0:T(8,128)S(1)}, u32[]{:S(2)}, u32[]{:S(2)}) collective-permute-start(f32[72,128]{1,0:T(8,128)S(1)} %get-tuple-element.42), channel_id=1, source_target_pairs={{0,384},{64,448},{128,0},{192,64},{256,128},{320,192},{384,256},{4... | collective-permute-start | bytes 110600 | tf_op jit(solution)/shard_map/ppermute | solution.py:365
  78.5 11.7 %all-to-all-start.1 = ((f32[8,16,256]{2,1,0:T(8,128)}), f32[8,16,256]{2,1,0:T(8,128)S(1)}, u32[]{:S(2)}, u32[]{:S(2)}) async-start(f32[8,16,256]{2,1,0:T(8,128)} %top_step.1.refs_7_), calls=%async_computation.1 | async-start | bytes 262144 | tf_op jit(solution)/shard_map/all_to_all | solution.py:405
  85.0 5.3 %copy-start.3 = (bf16[128,128]{1,0:T(8,128)(2,1)S(1)}, bf16[128,128]{1,0:T(8,128)(2,1)}, u32[]{:S(2)}) copy-start(bf16[128,128]{1,0:T(8,128)(2,1)} %constant.12.clone.refs_5_) | copy-start | bytes 98308
  85.0 5.3 %copy-start.4 = (bf16[128,128]{1,0:T(8,128)(2,1)S(1)}, bf16[128,128]{1,0:T(8,128)(2,1)}, u32[]{:S(2)}) copy-start(bf16[128,128]{1,0:T(8,128)(2,1)} %constant.14.clone.refs_7_) | copy-start | bytes 98308
  85.0 5.3 %copy-start.5 = (bf16[32,24]{1,0:T(8,128)(2,1)S(1)}, bf16[32,24]{1,0:T(8,128)(2,1)}, u32[]{:S(2)}) copy-start(bf16[32,24]{1,0:T(8,128)(2,1)} %constant.13.clone.refs_6_) | copy-start | bytes 4612
  85.0 5.3 %copy-start.6 = (bf16[24,16]{1,0:T(8,128)(2,1)S(1)}, bf16[24,16]{1,0:T(8,128)(2,1)}, u32[]{:S(2)}) copy-start(bf16[24,16]{1,0:T(8,128)(2,1)} %constant.11.clone.refs_4_) | copy-start | bytes 2308

commit v4 on v3

--- a/solution.py
+++ b/solution.py
@@ -290,7 +290,7 @@
             to_high2[24 * (j - 7) : 24 * (j - 7) + 24] = share
 
 
-def near_x_step(taps, n1, n2, low, high, low2, high2, n1_out, n2_out):
+def near_x_step(taps, n1, n2, low2, high2, low, high, n1_out, n2_out):
     for t in range(4):
         f = {}
         for i in range(8):
@@ -396,12 +396,12 @@
         [((16, 32, 128), f32), ((11, 24, 128), f32)] + [((520, 128), f32)] * 2 + [((72, 128), f32)] * 2,
         [n1, n2, from_odd, from_even, mz1, mz2], after=[message],
     )
-    halos = [shift(to_high, 1), shift(to_low, -1), shift(to_high2, 2), shift(to_low2, -2)]
-    (message,) = call(top_step, [((8, 16, 256), f32)], [gathered, wz1, wz2, ty], after=halos)
+    halos = [shift(to_high2, 2), shift(to_low2, -2), shift(to_high, 1), shift(to_low, -1)]
     n1, n2 = call(
         near_x_step, [((16, 32, 128), f32), ((11, 24, 128), f32)],
-        [kernel_taps, n1, n2, *halos], smem=(0,), after=[message],
-    )
+        [kernel_taps, n1, n2, *halos], smem=(0,),
+    )
+    (message,) = call(top_step, [((8, 16, 256), f32)], [gathered, wz1, wz2, ty], after=[n1])
     top = lax.all_to_all(message, "gx", split_axis=0, concat_axis=0, tiled=True)
     (result,) = call(
         last_step, [((16, 32, 128), f32)],

time: 92.3 us -> 91.2 us (0.988)
  blocking collectives: 0 us -> 11.2 us
  starting transfers between devices: 57.9 us -> 51.4 us
  waiting for transfers between devices: 23.7 us -> 18.5 us
    all_to_all x0 -> x1, blocking collectives: none -> 11.2 us  [per_device(): top = lax.all_to_all(message, 'gx', split_axis=0, concat_axis=0, tiled=True)]
    all_to_all x1 -> x0, starting transfers between devices: 6.46 us -> none  [per_device(): top = lax.all_to_all(message, 'gx', split_axis=0, concat_axis=0, tiled=True)]
    all_to_all x1 -> x0, waiting for transfers between devices: 4.23 us -> none  [per_device(): top = lax.all_to_all(message, 'gx', split_axis=0, concat_axis=0, tiled=True)]
    all_to_all x1, waiting for transfers between devices: 5.98 us -> 4.97 us  [per_device(): lax.all_to_all(message.reshape(64, 8, 128), ('gy', 'gz'), split_axis=0, c...]
  transfers between devices with their start and end apart: 12 -> 11, of which waited for: 8 -> 7; matrix products, arithmetic and copies ran while one was open for 0% -> 0% of each run, Pallas kernels for 4% -> 4%
where the time goes in v4:
time: 91.2 us; the launch traced here: 90.7 us
  starting transfers between devices  51.4 us (56%)
  waiting for transfers between devices  18.5 us (20%)
  blocking collectives  11.2 us (12%)
  Pallas kernels  7.85 us (9%)
  local copies, waits for them, and re-layouts  1.63 us (2%)
    ppermute x1, starting transfers between devices, per_device(): from_odd = lax.ppermute(to_odd, 'gy', swap_odd)  18.9 us
    all_to_all x1, starting transfers between devices, per_device(): lax.all_to_all(message.reshape(64, 8, 128), ('gy', 'gz'), split_axis=0, c...  15 us
    all_to_all x1, blocking collectives, per_device(): top = lax.all_to_all(message, 'gx', split_axis=0, concat_axis=0, tiled=True)  11.2 us
    ppermute x6, starting transfers between devices, shift(): return lax.ppermute(block, 'gx', [(i, (i + by) % 8) for i in range(8)])  9.97 us
    pallas_call x11, Pallas kernels, call(): pl.pallas_call(kernel, out_shape=[jax.ShapeDtypeStruct(s, d) for s, d in...  7.85 us
    ppermute x1, waiting for transfers between devices, per_device(): from_odd = lax.ppermute(to_odd, 'gz', swap_odd)  6.14 us
    all_to_all x1, waiting for transfers between devices, per_device(): lax.all_to_all(message.reshape(64, 8, 128), ('gy', 'gz'), split_axis=0, c...  4.97 us
    ppermute x6, waiting for transfers between devices, shift(): return lax.ppermute(block, 'gx', [(i, (i + by) % 8) for i in range(8)])  4.77 us
  transfers between devices with their start and end apart: 11, of which 7 were waited for; matrix products, arithmetic and copies ran while one was open for 0% of the time, Pallas kernels for 4%

profile of v4, /device:TPU:1, one launch (start us, length us, event | category | flops | bytes accessed | tf_op | source)
XLA Modules:
  0.0 90.7 jit_solution(3567762394682976712)
XLA Ops:
  0.0 0.0 copy-start
  0.0 0.9 copy-done
  0.9 0.0 copy-start.1
  0.9 0.1 y_send.1
  1.0 0.0 copy-start.7
  1.0 18.9 %collective-permute-start = (bf16[352,128]{1,0:T(8,128)(2,1)S(1)}, bf16[352,128]{1,0:T(8,128)(2,1)S(1)}, u32[]{:S(2)}, u32[]{:S(2)}) collective-permute-start(bf16[352,128]{1,0:T(8,128)(2,1)S(1)} %get-tuple-element.26), channel_id=1, source_target_pairs={{8,16},{16,8},{24,32},{32,24},{40,48},{48,40},{56,0},{0,56},{9,17}... | collective-permute-start | bytes 270344 | tf_op jit(solution)/shard_map/ppermute | solution.py:368
  19.8 1.9 %collective-permute-start.1 = (bf16[352,128]{1,0:T(8,128)(2,1)S(1)}, bf16[352,128]{1,0:T(8,128)(2,1)S(1)}, u32[]{:S(2)}, u32[]{:S(2)}) collective-permute-start(bf16[352,128]{1,0:T(8,128)(2,1)S(1)} %get-tuple-element.27), channel_id=1, source_target_pairs={{0,8},{8,0},{16,24},{24,16},{32,40},{40,32},{48,56},{56,48},{1,9},... | collective-permute-start | bytes 270344 | tf_op jit(solution)/shard_map/ppermute | solution.py:369
  21.8 0.0 copy-done.7
  21.8 0.9 prep_z.1
  22.7 0.6 prep_y.1.refs_3_
  23.3 0.0 copy-start.10
  23.3 0.0 copy-start.8
  23.3 0.0 copy-start.9
  23.3 0.6 copy-done.10
  24.0 0.0 copy-done.8
  24.0 0.0 copy-done.9
  24.0 0.6 prep_top.1
  24.6 2.6 %collective-permute-done.refs_1_ = bf16[352,128]{1,0:T(8,128)(2,1)S(1)} collective-permute-done((bf16[352,128]{1,0:T(8,128)(2,1)S(1)}, bf16[352,128]{1,0:T(8,128)(2,1)S(1)}, u32[]{:S(2)}, u32[]{:S(2)}) %collective-permute-start) | collective-permute-done | bytes 90144 | tf_op jit(solution)/shard_map/ppermute | solution.py:368
  27.1 0.0 collective-permute-done.1.refs_2_
  27.2 0.0 copy-done.1
  27.2 0.0 copy-start.2
  27.2 0.5 y_step.1
  27.7 3.8 %collective-permute-start.2 = (f32[144,128]{1,0:T(8,128)S(1)}, f32[144,128]{1,0:T(8,128)S(1)}, u32[]{:S(2)}, u32[]{:S(2)}) collective-permute-start(f32[144,128]{1,0:T(8,128)S(1)} %get-tuple-element.31), channel_id=1, source_target_pairs={{1,2},{2,1},{3,4},{4,3},{5,6},{6,5},{7,0},{0,7},{9,10},{10,9},{11,... | collective-permute-start | bytes 221192 | tf_op jit(solution)/shard_map/ppermute | solution.py:383
  31.4 1.9 %collective-permute-start.3 = (f32[144,128]{1,0:T(8,128)S(1)}, f32[144,128]{1,0:T(8,128)S(1)}, u32[]{:S(2)}, u32[]{:S(2)}) collective-permute-start(f32[144,128]{1,0:T(8,128)S(1)} %get-tuple-element.32), channel_id=1, source_target_pairs={{0,1},{1,0},{2,3},{3,2},{4,5},{5,4},{6,7},{7,6},{8,9},{9,8},{10,11... | collective-permute-start | bytes 221192 | tf_op jit(solution)/shard_map/ppermute | solution.py:384
  33.4 6.1 %collective-permute-done.2.refs_1_.refs_2_ = f32[144,128]{1,0:T(8,128)S(1)} collective-permute-done((f32[144,128]{1,0:T(8,128)S(1)}, f32[144,128]{1,0:T(8,128)S(1)}, u32[]{:S(2)}, u32[]{:S(2)}) %collective-permute-start.2) | collective-permute-done | bytes 73760 | tf_op jit(solution)/shard_map/ppermute | solution.py:383
  39.5 0.0 collective-permute-done.3.refs_2_.refs_3_
  39.5 0.0 copy-done.2
  39.5 0.3 q3_z_step.1.refs_1_
  39.8 3.0 %collective-permute-start.4 = (f32[32,128]{1,0:T(8,128)S(1)}, f32[32,128]{1,0:T(8,128)S(1)}, u32[]{:S(2)}, u32[]{:S(2)}) collective-permute-start(f32[32,128]{1,0:T(8,128)S(1)} %q3_z_step.1.refs_1_), channel_id=1, source_target_pairs={{0,64},{64,128},{128,192},{192,256},{256,320},{320,384},{384,448},... | collective-permute-start | bytes 49160 | tf_op jit(solution)/shard_map/ppermute | solution.py:365
  42.8 0.0 collective-permute-start.5
  42.8 0.9 collective-permute-done.4.refs_0_
  43.7 2.3 %collective-permute-done.5.refs_2_ = f32[32,128]{1,0:T(8,128)S(1)} collective-permute-done((f32[32,128]{1,0:T(8,128)S(1)}, f32[32,128]{1,0:T(8,128)S(1)}, u32[]{:S(2)}, u32[]{:S(2)}) %collective-permute-start.5) | collective-permute-done | bytes 16416 | tf_op jit(solution)/shard_map/ppermute | solution.py:365
  46.0 0.8 q3_x_step.1.refs_6_
  46.8 15.0 %all-to-all-start = ((bf16[64,8,128]{2,1,0:T(8,128)(2,1)}), bf16[64,8,128]{2,1,0:T(8,128)(2,1)S(1)}, u32[]{:S(2)}, u32[]{:S(2)}) async-start(bf16[64,8,128]{2,1,0:T(8,128)(2,1)} %bitcast.3), calls=%async_computation | async-start | bytes 262144 | tf_op jit(solution)/shard_map/all_to_all | solution.py:391
  61.8 1.0 %near_z_step.1 = (f32[16,32,128]{2,1,0:T(8,128)S(1)}, f32[11,24,128]{2,1,0:T(8,128)S(1)}, f32[520,128]{1,0:T(8,128)S(1)}, f32[520,128]{1,0:T(8,128)S(1)}, f32[72,128]{1,0:T(8,128)S(1)}, /*index=5*/f32[72,128]{1,0:T(8,128)S(1)}) custom-call(f32[16,32,128]{2,1,0:T(8,128)S(1)} %get-tuple-element.36.refs_0_, f32[16,24,128]{2,1,0:T(8,128)S(1)} %get-tuple-element.37.refs_1_, ...), custom_call_target="tpu_custom_call" | custom-call | flops 1000000 | bytes 1000000 | tf_op jit(solution)/shard_map/near_z_step/pallas_call | solution.py:79
  62.7 0.3 collective-permute-start.8
  63.0 0.2 collective-permute-start.9
  63.2 3.1 %collective-permute-start.6 = (f32[72,128]{1,0:T(8,128)S(1)}, f32[72,128]{1,0:T(8,128)S(1)}, u32[]{:S(2)}, u32[]{:S(2)}) collective-permute-start(f32[72,128]{1,0:T(8,128)S(1)} %get-tuple-element.41), channel_id=1, source_target_pairs={{0,128},{64,192},{128,256},{192,320},{256,384},{320,448},{384,0},{... | collective-permute-start | bytes 110600 | tf_op jit(solution)/shard_map/ppermute | solution.py:365
  66.4 3.4 %collective-permute-start.7 = (f32[72,128]{1,0:T(8,128)S(1)}, f32[72,128]{1,0:T(8,128)S(1)}, u32[]{:S(2)}, u32[]{:S(2)}) collective-permute-start(f32[72,128]{1,0:T(8,128)S(1)} %get-tuple-element.42), channel_id=1, source_target_pairs={{0,384},{64,448},{128,0},{192,64},{256,128},{320,192},{384,256},{4... | collective-permute-start | bytes 110600 | tf_op jit(solution)/shard_map/ppermute | solution.py:365
  69.8 0.5 collective-permute-done.6.refs_3_
  70.2 1.1 %collective-permute-done.7.refs_4_ = f32[72,128]{1,0:T(8,128)S(1)} collective-permute-done((f32[72,128]{1,0:T(8,128)S(1)}, f32[72,128]{1,0:T(8,128)S(1)}, u32[]{:S(2)}, u32[]{:S(2)}) %collective-permute-start.7) | collective-permute-done | bytes 36896 | tf_op jit(solution)/shard_map/ppermute | solution.py:365
  71.4 0.0 collective-permute-done.8.refs_5_
  71.4 0.0 collective-permute-done.9.refs_6_
  71.4 1.0 %near_x_step.1 = (f32[16,32,128]{2,1,0:T(8,128)S(1)}, f32[11,24,128]{2,1,0:T(8,128)S(1)}) custom-call(f32[2,17]{1,0:T(2,128)S(1)} %copy-done.7, f32[16,32,128]{2,1,0:T(8,128)S(1)} %get-tuple-element.39.refs_1_, f32[11,24,128]{2,1,0:T(8,128)S(1)} %get-tuple-element.40.refs_2_, f32[72,128]{1,0:T(8,128)S(1)} %collective-permute-done.6.refs_3_, ...), custom_call_target="tpu_custom_call" | custom-call | flops 1000000 | bytes 1000000 | tf_op jit(solution)/shard_map/near_x_step/pallas_call | solution.py:79
  72.4 5.0 %all-to-all-done.refs_0_ = bf16[64,8,128]{2,1,0:T(8,128)(2,1)S(1)} async-done(((bf16[64,8,128]{2,1,0:T(8,128)(2,1)}), bf16[64,8,128]{2,1,0:T(8,128)(2,1)S(1)}, u32[]{:S(2)}, u32[]{:S(2)}) %all-to-all-start) | async-done | bytes 131104 | tf_op jit(solution)/shard_map/all_to_all | solution.py:391
  77.4 0.5 top_step.1
  77.9 0.0 copy-start.3
  77.9 0.0 copy-start.4
  77.9 0.0 copy-start.5
  77.9 0.0 copy-start.6
  77.9 11.2 %all_to_all.10.refs_0_ = f32[8,16,256]{2,1,0:T(8,128)S(1)} all-to-all(f32[8,16,256]{2,1,0:T(8,128)S(1)} %top_step.1), channel_id=1, replica_groups=mesh['gx'=8,'gy'=8,'gz'=8] {'gx'}, dimensions={0} | all-to-all | bytes 262144 | tf_op jit(solution)/shard_map/all_to_all | solution.py:405
  89.1 0.0 copy-done.3
  89.1 0.0 copy-done.4
  89.1 0.0 copy-done.5
  89.1 0.0 copy-done.6
  89.2 1.6 %last_step.1 = f32[16,32,128]{2,1,0:T(8,128)} custom-call(f32[8,16,256]{2,1,0:T(8,128)S(1)} %all_to_all.10.refs_0_, f32[16,2048]{1,0:T(8,128)S(1)} %get-tuple-element.29.refs_5_.refs_1_, f32[16,32,128]{2,1,0:T(8,128)S(1)} %get-tuple-element.45.refs_4_.refs_2_, f32[11,24,128]{2,1,0:T(8,128)S(1)} %get-tuple-element.46.refs_3_, bf16[24,16]{1,0:T(8,128)(2,1)S(1)} %copy-done.6, ...), custom_call_target="tpu_custom_call" | custom-call | flops 1000000 | bytes 1000000 | tf_op jit(solution)/shard_map/last_step/pallas_call | solution.py:79
Async XLA Ops:
  0.0 0.9 copy-start
  0.9 26.2 %copy-start.1 = (bf16[16,32,128]{2,1,0:T(8,128)(2,1)S(1)}, bf16[16,32,128]{2,1,0:T(8,128)(2,1)}, u32[]{:S(2)}) copy-start(bf16[16,32,128]{2,1,0:T(8,128)(2,1)} %refs_0_.8) | copy-start | bytes 393220
  1.0 20.8 %copy-start.7 = (f32[2,17]{1,0:T(2,128)S(1)}, f32[2,17]{1,0:T(2,128)}, u32[]{:S(2)}) copy-start(f32[2,17]{1,0:T(2,128)} %refs_0_.9) | copy-start | bytes 412
  1.0 26.2 %collective-permute-start = (bf16[352,128]{1,0:T(8,128)(2,1)S(1)}, bf16[352,128]{1,0:T(8,128)(2,1)S(1)}, u32[]{:S(2)}, u32[]{:S(2)}) collective-permute-start(bf16[352,128]{1,0:T(8,128)(2,1)S(1)} %get-tuple-element.26), channel_id=1, source_target_pairs={{8,16},{16,8},{24,32},{32,24},{40,48},{48,40},{56,0},{0,56},{9,17}... | collective-permute-start | bytes 270344 | tf_op jit(solution)/shard_map/ppermute | solution.py:368
  19.8 7.3 %collective-permute-start.1 = (bf16[352,128]{1,0:T(8,128)(2,1)S(1)}, bf16[352,128]{1,0:T(8,128)(2,1)S(1)}, u32[]{:S(2)}, u32[]{:S(2)}) collective-permute-start(bf16[352,128]{1,0:T(8,128)(2,1)S(1)} %get-tuple-element.27), channel_id=1, source_target_pairs={{0,8},{8,0},{16,24},{24,16},{32,40},{40,32},{48,56},{56,48},{1,9},... | collective-permute-start | bytes 270344 | tf_op jit(solution)/shard_map/ppermute | solution.py:369
  23.3 0.7 copy-start.10
  23.3 0.7 copy-start.8
  23.3 0.7 copy-start.9
  27.2 12.4 %copy-start.2 = (f32[256,128]{1,0:T(8,128)S(1)}, f32[256,128]{1,0:T(8,128)}, u32[]{:S(2)}) copy-start(f32[256,128]{1,0:T(8,128)} %constant.10.clone.refs_3_) | copy-start | bytes 393220
  27.7 11.8 %collective-permute-start.2 = (f32[144,128]{1,0:T(8,128)S(1)}, f32[144,128]{1,0:T(8,128)S(1)}, u32[]{:S(2)}, u32[]{:S(2)}) collective-permute-start(f32[144,128]{1,0:T(8,128)S(1)} %get-tuple-element.31), channel_id=1, source_target_pairs={{1,2},{2,1},{3,4},{4,3},{5,6},{6,5},{7,0},{0,7},{9,10},{10,9},{11,... | collective-permute-start | bytes 221192 | tf_op jit(solution)/shard_map/ppermute | solution.py:383
  31.4 8.1 %collective-permute-start.3 = (f32[144,128]{1,0:T(8,128)S(1)}, f32[144,128]{1,0:T(8,128)S(1)}, u32[]{:S(2)}, u32[]{:S(2)}) collective-permute-start(f32[144,128]{1,0:T(8,128)S(1)} %get-tuple-element.32), channel_id=1, source_target_pairs={{0,1},{1,0},{2,3},{3,2},{4,5},{5,4},{6,7},{7,6},{8,9},{9,8},{10,11... | collective-permute-start | bytes 221192 | tf_op jit(solution)/shard_map/ppermute | solution.py:384
  39.8 3.8 %collective-permute-start.4 = (f32[32,128]{1,0:T(8,128)S(1)}, f32[32,128]{1,0:T(8,128)S(1)}, u32[]{:S(2)}, u32[]{:S(2)}) collective-permute-start(f32[32,128]{1,0:T(8,128)S(1)} %q3_z_step.1.refs_1_), channel_id=1, source_target_pairs={{0,64},{64,128},{128,192},{192,256},{256,320},{320,384},{384,448},... | collective-permute-start | bytes 49160 | tf_op jit(solution)/shard_map/ppermute | solution.py:365
  42.8 3.2 %collective-permute-start.5 = (f32[32,128]{1,0:T(8,128)S(1)}, f32[32,128]{1,0:T(8,128)S(1)}, u32[]{:S(2)}, u32[]{:S(2)}) collective-permute-start(f32[32,128]{1,0:T(8,128)S(1)} %q3_z_step.1.refs_1_), channel_id=1, source_target_pairs={{0,448},{64,0},{128,64},{192,128},{256,192},{320,256},{384,320},{4... | collective-permute-start | bytes 49160 | tf_op jit(solution)/shard_map/ppermute | solution.py:365
  46.8 30.6 %all-to-all-start = ((bf16[64,8,128]{2,1,0:T(8,128)(2,1)}), bf16[64,8,128]{2,1,0:T(8,128)(2,1)S(1)}, u32[]{:S(2)}, u32[]{:S(2)}) async-start(bf16[64,8,128]{2,1,0:T(8,128)(2,1)} %bitcast.3), calls=%async_computation | async-start | bytes 262144 | tf_op jit(solution)/shard_map/all_to_all | solution.py:391
  62.7 8.6 %collective-permute-start.8 = (f32[520,128]{1,0:T(8,128)S(1)}, f32[520,128]{1,0:T(8,128)S(1)}, u32[]{:S(2)}, u32[]{:S(2)}) collective-permute-start(f32[520,128]{1,0:T(8,128)S(1)} %get-tuple-element.43), channel_id=1, source_target_pairs={{0,64},{64,128},{128,192},{192,256},{256,320},{320,384},{384,448},... | collective-permute-start | bytes 798728 | tf_op jit(solution)/shard_map/ppermute | solution.py:365
  63.0 8.3 %collective-permute-start.9 = (f32[520,128]{1,0:T(8,128)S(1)}, f32[520,128]{1,0:T(8,128)S(1)}, u32[]{:S(2)}, u32[]{:S(2)}) collective-permute-start(f32[520,128]{1,0:T(8,128)S(1)} %get-tuple-element.44), channel_id=1, source_target_pairs={{0,448},{64,0},{128,64},{192,128},{256,192},{320,256},{384,320},{4... | collective-permute-start | bytes 798728 | tf_op jit(solution)/shard_map/ppermute | solution.py:365
  63.2 7.0 %collective-permute-start.6 = (f32[72,128]{1,0:T(8,128)S(1)}, f32[72,128]{1,0:T(8,128)S(1)}, u32[]{:S(2)}, u32[]{:S(2)}) collective-permute-start(f32[72,128]{1,0:T(8,128)S(1)} %get-tuple-element.41), channel_id=1, source_target_pairs={{0,128},{64,192},{128,256},{192,320},{256,384},{320,448},{384,0},{... | collective-permute-start | bytes 110600 | tf_op jit(solution)/shard_map/ppermute | solution.py:365
  66.4 5.0 %collective-permute-start.7 = (f32[72,128]{1,0:T(8,128)S(1)}, f32[72,128]{1,0:T(8,128)S(1)}, u32[]{:S(2)}, u32[]{:S(2)}) collective-permute-start(f32[72,128]{1,0:T(8,128)S(1)} %get-tuple-element.42), channel_id=1, source_target_pairs={{0,384},{64,448},{128,0},{192,64},{256,128},{320,192},{384,256},{4... | collective-permute-start | bytes 110600 | tf_op jit(solution)/shard_map/ppermute | solution.py:365
  77.9 11.3 %copy-start.3 = (bf16[128,128]{1,0:T(8,128)(2,1)S(1)}, bf16[128,128]{1,0:T(8,128)(2,1)}, u32[]{:S(2)}) copy-start(bf16[128,128]{1,0:T(8,128)(2,1)} %constant.12.clone.refs_5_) | copy-start | bytes 98308
  77.9 11.3 %copy-start.4 = (bf16[128,128]{1,0:T(8,128)(2,1)S(1)}, bf16[128,128]{1,0:T(8,128)(2,1)}, u32[]{:S(2)}) copy-start(bf16[128,128]{1,0:T(8,128)(2,1)} %constant.14.clone.refs_7_) | copy-start | bytes 98308
  77.9 11.3 %copy-start.5 = (bf16[32,24]{1,0:T(8,128)(2,1)S(1)}, bf16[32,24]{1,0:T(8,128)(2,1)}, u32[]{:S(2)}) copy-start(bf16[32,24]{1,0:T(8,128)(2,1)} %constant.13.clone.refs_6_) | copy-start | bytes 4612
  77.9 11.2 %copy-start.6 = (bf16[24,16]{1,0:T(8,128)(2,1)S(1)}, bf16[24,16]{1,0:T(8,128)(2,1)}, u32[]{:S(2)}) copy-start(bf16[24,16]{1,0:T(8,128)(2,1)} %constant.11.clone.refs_4_) | copy-start | bytes 2308

commit v5 on v4

--- a/solution.py
+++ b/solution.py
@@ -24,22 +24,32 @@
     return np.array([[entry(r, c) for c in range(cols)] for r in range(rows)], np.float32)
 
 
-def z_cell(row, width):
-    if row < 128:
-        return row
-    if row < 128 + width:
-        return row - 128 - width
-    if row < 128 + 2 * width:
-        return row - width
-    return None
-
-
-def z_twice16(row, col):
-    cell = z_cell(row, 16)
-    return 0.0 if cell is None else twice.get(cell - 4 * (col % 32), 0.0)
-
-
-z_twice_matrix = table(256, 128, z_twice16)
+def restrict(cell, coarse):
+    return weight.get(cell - 2 * coarse, 0.0)
+
+
+z_level2 = [*range(66), -1]
+z_top = [*range(35), -2, -1]
+z_first = table(128, 128, lambda r, c: restrict(r, z_level2[c]) if c < 67 else 0.0)
+z_second = table(128, 128, lambda r, c: restrict(z_level2[r], z_top[c]) if r < 67 and c < 37 else 0.0)
+
+
+def y_source(row, col):
+    coarse = row - 9
+    if row >= 35:
+        return 0.0
+    if col < 32:
+        return restrict(col, coarse)
+    if col < 40:
+        return restrict(col - 40, coarse) if -2 <= coarse <= 1 else 0.0
+    if col < 48:
+        return restrict(col - 8, coarse) if 15 <= coarse <= 18 else 0.0
+    if col < 56:
+        return 1.0 if coarse == col - 57 and col < 55 else 0.0
+    return 1.0 if coarse == col - 37 and col < 63 else 0.0
+
+
+y_sources = table(40, 64, y_source)
 y_raise_top = table(24, 16, lambda r, c: weight.get((r - 1) - 2 * (c - 2), 0.0) if r < 19 and c < 13 else 0.0)
 z_raise_top = table(128, 128, lambda r, c: weight.get((c - 1) - 2 * (r - 2), 0.0) if r < 37 and c < 67 else 0.0)
 y_raise = table(32, 24, lambda r, c: weight.get(r - 2 * (c - 1), 0.0) if c < 19 else 0.0)
@@ -50,17 +60,20 @@
     return jnp.dot(a, b, precision=highest, preferred_element_type=f32)
 
 
-def halves(x):
-    first = x.astype(bf16)
-    return first, (x - first.astype(f32)).astype(bf16)
-
-
-def from_left(m, x):
-    return sum(jnp.dot(m[...], term, preferred_element_type=f32) for term in halves(x))
-
-
-def from_right(x, m):
-    return sum(jnp.dot(term, m[...], preferred_element_type=f32) for term in halves(x))
+def split(x, count):
+    terms = []
+    for _ in range(count):
+        terms.append(x.astype(bf16))
+        x = x - terms[-1].astype(f32)
+    return terms
+
+
+def from_left(m, x, count=2):
+    return sum(jnp.dot(m[...], term, preferred_element_type=f32) for term in split(x, count))
+
+
+def from_right(x, m, count=2):
+    return sum(jnp.dot(term, m[...], preferred_element_type=f32) for term in split(x, count))
 
 
 def lanes(parts):
@@ -93,14 +106,6 @@
     )(*args, *after)
 
 
-def pair_taps(taps):
-    merged = {}
-    for b in range(-8, 9):
-        for d, w in weight.items():
-            merged.setdefault(2 * b + d, []).append(w * taps[1, b + 8])
-    return {m: sum(terms[1:], terms[0]) for m, terms in merged.items()}
-
-
 def fill(gap, values):
     out = jnp.zeros(gap.shape, f32)
     for m, value in values.items():
@@ -108,34 +113,28 @@
     return out
 
 
-def prep_y(taps, my):
-    def gap(rows, first, step):
-        column = iota((rows, 76), 1)
-        cell = jnp.where(column < 32, column, jnp.where(column < 54, column - 54, column - 22))
-        return cell - step * (iota((rows, 76), 0) + first)
-
-    single = {m: taps[0, m + 8] for m in range(-8, 9)}
-    part = jnp.concatenate(
-        [fill(gap(32, 0, 1), single), fill(gap(24, -1, 2), pair_taps(taps)), fill(gap(8, 0, 4), twice)], axis=0
-    )
-    first = part.astype(bf16)
-    rest = part - first.astype(f32)
-    second = rest.astype(bf16)
-    third = (rest - second.astype(f32)).astype(bf16)
-    my[...] = jnp.concatenate([first.astype(f32), second.astype(f32), third.astype(f32)], axis=0).astype(bf16)
+def prep_y(taps, sources, my1, my2):
+    column = iota((32, 48), 1)
+    cell = jnp.where(column < 32, column, jnp.where(column < 40, column - 40, column - 8))
+    terms = split(fill(cell - iota((32, 48), 0), {m: taps[0, m + 8] for m in range(-8, 9)}), 3)
+    my1[...] = jnp.concatenate([term.astype(f32) for term in terms], axis=0).astype(bf16)
+    coarse = iota((24, 40), 1) - 9
+    near = fill(coarse - (iota((24, 40), 0) - 1), {m: taps[1, m + 8] for m in range(-8, 9)})
+    top = fill(iota((8, 40), 1) - 9 - 2 * iota((8, 40), 0), weight)
+    my2[...] = dot(jnp.concatenate([near, top], axis=0), sources[...])
 
 
 def prep_z(taps, mz1, mz2):
     far_off = 1 << 20
-
-    def z_cells(width):
-        row = iota((256, 128), 0)
-        cell = jnp.where(row < 128, row, jnp.where(row < 128 + width, row - 128 - width, row - width))
-        return jnp.where(row < 128 + 2 * width, cell, far_off)
-
-    single = {m: taps[0, m + 8] for m in range(-8, 9)}
-    mz1[...] = fill(z_cells(8) - iota((256, 128), 1), single)
-    mz2[...] = fill(z_cells(32) - 2 * (iota((256, 128), 1) - 1), pair_taps(taps))
+    row = iota((256, 128), 0)
+    cell = jnp.where(row < 128, row, jnp.where(row < 136, row - 136, row - 8))
+    cell = jnp.where(row < 144, cell, far_off)
+    mz1[...] = fill(cell - iota((256, 128), 1), {m: taps[0, m + 8] for m in range(-8, 9)})
+    own = jnp.where(row < 66, row, jnp.where(row == 66, -1, far_off))
+    below = jnp.where(row < 139, row - 137, far_off)
+    above = jnp.where(row < 154, row - 80, jnp.where(row == 154, 63, far_off))
+    cell = jnp.where(row < 128, own, jnp.where(row < 144, below, above))
+    mz2[...] = fill(cell - (iota((256, 128), 1) - 1), {m: taps[1, m + 8] for m in range(-8, 9)})
 
 
 def toeplitz(profile, shift, size):
@@ -153,7 +152,7 @@
         for a in range(4):
             rows = pl.ds(128 * g + 32 * a, 32)
             part = blocks[a][32 * g : 32 * g + 32]
-            wz1[rows, :], wz2[rows, :] = halves(part)
+            wz1[rows, :], wz2[rows, :] = split(part, 2)
     ty = toeplitz(lanes([top_y[...]] * 2), lax.rem(130 - 8 * gy, 128), 128)
     my[...] = ty.T[0:16, 0:64]
     tx = toeplitz(lanes([top_x[...]] * 4), lax.rem(130 - 4 * gx, 128), 128)
@@ -169,51 +168,97 @@
     return jnp.where(is_odd, low, high), jnp.where(is_odd, high, low)
 
 
+def level2_rows(cells):
+    return [
+        sum(w * cells[2 * j + d] for d, w in weight.items() if 0 <= 2 * j + d < 16) for j in range(-1, 10)
+    ]
+
+
 def y_send(own, out_even, out_odd):
-    is_odd = odd_place("gy")
+    row, column = iota((16, 32), 0), iota((16, 32), 1)
+    y_matrix = fill(column - 2 * jnp.where(row < 8, row + 3, row - 1), weight).astype(bf16)
+    row, column = iota((128, 128), 0), iota((128, 128), 1)
+    z_matrix = jnp.where(column < 67, fill(row - 2 * jnp.where(column < 66, column, -1), weight), 0.0).astype(bf16)
     cells = own[...].astype(f32)
-    low = jnp.concatenate([cells[i, 0:22] for i in range(16)], axis=0)
-    high = jnp.concatenate([cells[i, 10:32] for i in range(16)], axis=0)
-    even, odd = choose(is_odd, low, high)
+    wide = from_left(y_matrix, lanes(level2_rows(cells)), 3)
+    tall = jnp.concatenate([wide[:, 128 * j : 128 * j + 128] for j in range(11)], axis=0)
+    tall = from_right(tall, z_matrix, 3)
+    lane = iota((8, 128), 1)
+
+    def message(raw_at, share_at):
+        rows, more = [cells[i, raw_at : raw_at + 8] for i in range(16)], jnp.zeros((8, 128), f32)
+        for j in range(11):
+            part = tall[16 * j + share_at : 16 * j + share_at + 8]
+            first = part.astype(bf16).astype(f32)
+            second = part - first
+            rows.append(jnp.where(lane < 64, first, pltpu.roll(second, 64, 1)))
+            beyond = jnp.where(lane % 8 < 4, pltpu.roll(first, (64 + 8 * j) % 128, 1), pltpu.roll(second, (68 + 8 * j) % 128, 1))
+            more = jnp.where(lane // 8 == j, beyond, more)
+        return jnp.concatenate([*rows, more], axis=0)
+
+    even, odd = choose(odd_place("gy"), message(0, 0), message(24, 8))
     out_even[...] = even.astype(bf16)
     out_odd[...] = odd.astype(bf16)
 
 
-def y_step(own, from_odd, from_even, my, n1, n2, q3, out_even, out_odd):
-    low, high = arrived("gy", from_even, from_odd, pl.ds(0, 352))
+def own_step(own, z_matrix, out):
+    rows = level2_rows(own[...].astype(f32))
+    out[...] = from_right(jnp.concatenate(rows, axis=0), z_matrix, 3).reshape(11, 32, 128)
+
+
+def pack(parts, width, shift):
+    slot = iota(parts[0].shape, 1) // width
+    out = jnp.zeros(parts[0].shape, f32)
+    for s, part in enumerate(parts):
+        by = (width * s + shift) % 128
+        moved = part if by == 0 else pltpu.roll(part, by, 1)
+        out = jnp.where(slot == s, moved, out)
+    return out
+
+
+def y_step(own, from_odd, from_even, own_share, my1, my2, z_matrix, z_next, n1, n2, q3, out_even, out_odd):
+    low, high = arrived("gy", from_even, from_odd, pl.ds(0, 224))
     low, high = low.astype(f32), high.astype(f32)
     cells = own[...].astype(f32)
-    columns = lanes([
-        jnp.concatenate([cells[i], low[22 * i : 22 * i + 22], high[22 * i : 22 * i + 22]], axis=0)
-        for i in range(16)
-    ])
-    terms = jnp.dot(my[...], columns.astype(bf16), preferred_element_type=f32)
-    done = terms[0:64] + (terms[64:128] + terms[128:192])
-    parts = [done[:, 128 * i : 128 * i + 128] for i in range(16)]
-    parts1 = [part[0:32] for part in parts]
-    parts2 = [part[32:56] for part in parts]
-    parts3 = [part[56:64] for part in parts]
+    raw = [[part[8 * i : 8 * i + 8] for i in range(16)] for part in (low, high)]
+    columns = lanes([jnp.concatenate([cells[i], raw[0][i], raw[1][i]], axis=0) for i in range(16)])
+    terms = jnp.dot(my1[...], columns.astype(bf16), preferred_element_type=f32)
+    done = terms[0:32] + (terms[32:64] + terms[64:96])
+    parts1 = [done[:, 128 * i : 128 * i + 128] for i in range(16)]
+
+    sides = [level2_rows(part) for part in raw]
+    tall = jnp.concatenate([part for j in range(11) for part in (sides[0][j], sides[1][j])], axis=0)
+    tall = from_right(tall, z_matrix, 3)
+    lane = iota((8, 128), 1)
+    columns = []
+    for j in range(11):
+        stack = [own_share[j], tall[16 * j : 16 * j + 16]]
+        for part in (low, high):
+            body = part[128 + 8 * j : 136 + 8 * j]
+            more = part[216:224] if j == 0 else pltpu.roll(part[216:224], 128 - 8 * j, 1)
+            more = pltpu.roll(more + pltpu.roll(more, 124, 1), 64, 1)
+            stack.append(jnp.where(lane < 64, body + pltpu.roll(body, 64, 1), jnp.where(lane < 67, more, 0.0)))
+        columns.append(jnp.concatenate(stack, axis=0))
+    done = dot(my2[...], lanes(columns))
+    parts2 = [done[0:24, 128 * j : 128 * j + 128] for j in range(11)]
+    half = {j - 1: done[24:32, 128 * j : 128 * j + 128] for j in range(11)}
+    rows = [sum(w * half[2 * j + d] for d, w in weight.items() if 2 * j + d in half) for j in range(-2, 7)]
+    tall = from_right(jnp.concatenate(rows, axis=0), z_next, 3)
+    parts3 = [tall[8 * j : 8 * j + 8] for j in range(9)]
     for i in range(16):
         n1[i] = parts1[i]
-        n2[i] = parts2[i]
-        q3[i] = parts3[i]
-
-    def pack(parts, width, high):
-        lane = iota(parts[0].shape, 1) // width
-        out = jnp.zeros(parts[0].shape, f32)
-        for s, part in enumerate(parts):
-            shift = (width * s + (width if high else 0)) % 128
-            moved = part if shift == 0 else pltpu.roll(part, shift, 1)
-            out = jnp.where(lane == s, moved, out)
-        return out
-
-    def packed(high):
-        groups = [pack(parts1, 8, high)]
-        groups += [pack(parts2[4 * g : 4 * g + 4], 32, high) for g in range(4)]
-        groups += [pack(parts3[8 * g : 8 * g + 8], 16, high) for g in range(2)]
-        return jnp.concatenate(groups, axis=0)
-
-    out_even[...], out_odd[...] = choose(odd_place("gz"), packed(False), packed(True))
+    for j in range(11):
+        n2[j] = parts2[j]
+    for j in range(9):
+        q3[j] = parts3[j]
+
+    lane = iota((24, 128), 1)
+    edge = [jnp.where(lane < 10, part, pltpu.roll(part, 72, 1)) for part in parts2]
+    to_low = [pack(parts1, 8, 0), pack(edge[0:8], 16, 0), pack(edge[8:11], 16, 0), pack(parts3, 8, -35)]
+    to_high = [pack(parts1, 8, 8), pack(parts2[0:8], 16, -55), pack(parts2[8:11], 16, -55), pack(parts3, 8, -32)]
+    out_even[...], out_odd[...] = choose(
+        odd_place("gz"), jnp.concatenate(to_low, axis=0), jnp.concatenate(to_high, axis=0)
+    )
 
 
 def arrived(axis, from_even, from_odd, rows):
@@ -230,35 +275,22 @@
     return jnp.where(iota(low.shape, 1) < width, low, high)
 
 
-def q3_z_step(q3, from_odd, from_even, mz3, out):
+def q3_z_step(q3, from_odd, from_even, out, to_low, to_high):
+    low, high = arrived("gz", from_even, from_odd, pl.ds(80, 8))
+    lane = iota((8, 128), 1)
     rows = []
-    for g in range(2):
-        low, high = arrived("gz", from_even, from_odd, pl.ds(128 + 8 * g, 8))
-        rows += [lanes([q3[8 * g + s], windows(low, high, s, 16)]) for s in range(8)]
-    full = dot(jnp.concatenate(rows, axis=0), mz3[...])
-    slot = iota((8, 128), 1) // 32
-    for g in range(4):
-        block = full[32 * g : 32 * g + 8]
-        for s in range(1, 4):
-            block = jnp.where(slot == s, full[32 * g + 8 * s : 32 * g + 8 * s + 8], block)
-        out[8 * g : 8 * g + 8] = block
+    for j in range(9):
+        below = low if j == 0 else pltpu.roll(low, 128 - 8 * j, 1)
+        above = pltpu.roll(high, (158 - 8 * j) % 128, 1)
+        edge = jnp.where(lane < 3, below, jnp.where(lane >= 30, above, 0.0))
+        rows.append(jnp.where(lane < 32, q3[j] + edge, 0.0))
+    out[...] = pack(rows[2:6], 32, 0)
+    to_low[...] = pack([jnp.zeros((8, 128), f32)] * 2 + rows[0:2], 32, 0)
+    to_high[...] = pack(rows[6:9], 32, 0)
 
 
 def q3_x_step(low, own, high, out):
-    groups = {}
-    for first, ref in ((-4, low), (0, own), (4, high)):
-        for g in range(4):
-            groups[first + g] = ref[8 * g : 8 * g + 8]
-    slot = iota((8, 128), 1) // 32
-    block = jnp.zeros((8, 128), f32)
-    for j in range(4):
-        total = jnp.zeros((8, 128), f32)
-        for q in range(-3, 3):
-            factor = fill(slot, {s: twice.get(4 * q + s, 0.0) for s in range(4)})
-            total = total + factor * groups[j + q]
-        total = total + pltpu.roll(total, 64, 1)
-        total = total + pltpu.roll(total, 32, 1)
-        block = jnp.where(slot == j, total, block)
+    block = own[...] + low[...] + high[...]
     pair = jnp.concatenate([block, block], axis=0).astype(bf16)
     out[...] = jnp.broadcast_to(pair[None], (32, 16, 128))
 
@@ -269,25 +301,17 @@
     done1 = dot(rows, mz1[...])
     n1_out[...] = done1.reshape(16, 32, 128)
     rows = []
-    for g in range(4):
+    for g in range(2):
         low, high = arrived("gz", from_even, from_odd, pl.ds(32 + 24 * g, 24))
-        rows += [lanes([n2[4 * g + s], windows(low, high, s, 32)]) for s in range(4)]
+        rows += [lanes([n2[j], windows(low, high, j % 8, 16)]) for j in range(8 * g, min(8 * g + 8, 11))]
     done2 = dot(jnp.concatenate(rows, axis=0), mz2[...])
+    n2_out[...] = done2.reshape(11, 24, 128)
     to_low[0:256] = done1[0:256]
     to_high[0:256] = done1[256:512]
-    for j in range(-1, 10):
-        share = jnp.zeros((24, 128), f32)
-        for d, w in weight.items():
-            if 0 <= 2 * j + d < 16:
-                share = share + w * done2[24 * (2 * j + d) : 24 * (2 * j + d) + 24]
-        at = 256 + 24 * (j + 1)
-        n2_out[j + 1] = share
-        to_low[at : at + 24] = share
-        to_high[at : at + 24] = share
-        if j < 2:
-            to_low2[24 * (j + 1) : 24 * (j + 1) + 24] = share
-        if j > 6:
-            to_high2[24 * (j - 7) : 24 * (j - 7) + 24] = share
+    to_low[256:520] = done2
+    to_high[256:520] = done2
+    to_low2[...] = done2[0:72]
+    to_high2[...] = done2[192:264]
 
 
 def near_x_step(taps, n1, n2, low2, high2, low, high, n1_out, n2_out):
@@ -364,11 +388,15 @@
     def shift(block, by):
         return lax.ppermute(block, "gx", [(i, (i + by) % 8) for i in range(8)])
 
-    to_even, to_odd = call(y_send, [((352, 128), bf16)] * 2, [charge])
+    z_matrix = jnp.asarray(z_first, bf16)
+    to_even, to_odd = call(y_send, [((224, 128), bf16)] * 2, [charge])
     from_odd = lax.ppermute(to_odd, "gy", swap_odd)
     from_even = lax.ppermute(to_even, "gy", swap_even)
-    (my,) = call(prep_y, [((192, 76), bf16)], [kernel_taps], smem=(0,))
+    my1, my2 = call(
+        prep_y, [((96, 48), bf16), ((32, 64), f32)], [kernel_taps, jnp.asarray(y_sources)], smem=(0,)
+    )
     mz1, mz2 = call(prep_z, [((256, 128), f32)] * 2, [kernel_taps], smem=(0,))
+    (own_share,) = call(own_step, [((11, 32, 128), f32)], [charge, z_matrix], after=[to_odd])
     wz1, wz2, ty, wx = call(
         prep_top,
         [((1024, 256), bf16)] * 2 + [((16, 64), f32), ((16, 2048), f32)],
@@ -377,17 +405,15 @@
 
     n1, n2, q3, to_even, to_odd = call(
         y_step,
-        [((16, 32, 128), f32), ((16, 24, 128), f32), ((16, 8, 128), f32), ((144, 128), f32), ((144, 128), f32)],
-        [charge, from_odd, from_even, my], after=[mz1, wx],
+        [((16, 32, 128), f32), ((11, 24, 128), f32), ((9, 8, 128), f32), ((88, 128), f32), ((88, 128), f32)],
+        [charge, from_odd, from_even, own_share, my1, my2, z_matrix, jnp.asarray(z_second, bf16)],
+        after=[mz1, wx],
     )
     from_odd = lax.ppermute(to_odd, "gz", swap_odd)
     from_even = lax.ppermute(to_even, "gz", swap_even)
 
-    (q3,) = call(
-        q3_z_step, [((32, 128), f32)],
-        [q3, from_odd, from_even, jnp.asarray(z_twice_matrix)],
-    )
-    (message,) = call(q3_x_step, [((32, 16, 128), bf16)], [shift(q3, 1), q3, shift(q3, -1)])
+    q3, to_low, to_high = call(q3_z_step, [((8, 128), f32)] * 3, [q3, from_odd, from_even])
+    (message,) = call(q3_x_step, [((32, 16, 128), bf16)], [shift(to_high, 1), q3, shift(to_low, -1)])
     gathered = lax.all_to_all(
         message.reshape(64, 8, 128), ("gy", "gz"), split_axis=0, concat_axis=0, tiled=True
     )

time: 91.2 us -> 88.2 us (0.967)
  waiting for transfers between devices: 18.5 us -> 14.3 us
    ppermute x1, waiting for transfers between devices: 2.56 us -> 0.01 us  [per_device(): from_odd = lax.ppermute(to_odd, 'gy', swap_odd)]
    all_to_all x1, starting transfers between devices: 15 us -> 12.5 us  [per_device(): lax.all_to_all(message.reshape(64, 8, 128), ('gy', 'gz'), split_axis=0, c...]
    ppermute x1, waiting for transfers between devices: 6.14 us -> 3.94 us  [per_device(): from_odd = lax.ppermute(to_odd, 'gz', swap_odd)]
    ppermute x1, starting transfers between devices: 3.77 us -> 5.67 us  [per_device(): from_odd = lax.ppermute(to_odd, 'gz', swap_odd)]
    ppermute x6, starting transfers between devices: 9.97 us -> 11.2 us  [shift(): return lax.ppermute(block, 'gx', [(i, (i + by) % 8) for i in range(8)])]
    pallas_call x11 -> x12, Pallas kernels: 7.85 us -> 8.44 us  [call(): pl.pallas_call(kernel, out_shape=[jax.ShapeDtypeStruct(s, d) for s, d in...]
  transfers between devices with their start and end apart: 11 -> 11, of which waited for: 7 -> 7; matrix products, arithmetic and copies ran while one was open for 0% -> 0% of each run, Pallas kernels for 4% -> 5%
where the time goes in v5:
time: 88.2 us; the launch traced here: 87.7 us
  starting transfers between devices  52.1 us (59%)
  waiting for transfers between devices  14.3 us (16%)
  blocking collectives  11.7 us (13%)
  Pallas kernels  8.44 us (10%)
  local copies, waits for them, and re-layouts  0.99 us (1%)
    ppermute x1, starting transfers between devices, per_device(): from_odd = lax.ppermute(to_odd, 'gy', swap_odd)  18.7 us
    all_to_all x1, starting transfers between devices, per_device(): lax.all_to_all(message.reshape(64, 8, 128), ('gy', 'gz'), split_axis=0, c...  12.5 us
    all_to_all x1, blocking collectives, per_device(): top = lax.all_to_all(message, 'gx', split_axis=0, concat_axis=0, tiled=True)  11.7 us
    ppermute x6, starting transfers between devices, shift(): return lax.ppermute(block, 'gx', [(i, (i + by) % 8) for i in range(8)])  11.2 us
    pallas_call x12, Pallas kernels, call(): pl.pallas_call(kernel, out_shape=[jax.ShapeDtypeStruct(s, d) for s, d in...  8.44 us
    ppermute x1, starting transfers between devices, per_device(): from_odd = lax.ppermute(to_odd, 'gz', swap_odd)  5.67 us
    all_to_all x1, waiting for transfers between devices, per_device(): lax.all_to_all(message.reshape(64, 8, 128), ('gy', 'gz'), split_axis=0, c...  5.09 us
    ppermute x6, waiting for transfers between devices, shift(): return lax.ppermute(block, 'gx', [(i, (i + by) % 8) for i in range(8)])  4.63 us
  transfers between devices with their start and end apart: 11, of which 7 were waited for; matrix products, arithmetic and copies ran while one was open for 0% of the time, Pallas kernels for 5%

profile of v5, /device:TPU:1, one launch (start us, length us, event | category | flops | bytes accessed | tf_op | source)
XLA Modules:
  0.0 87.7 jit_solution(6282404921560037786)
XLA Ops:
  0.0 0.0 copy-start
  0.0 0.9 %copy-done = bf16[16,32,128]{2,1,0:T(8,128)(2,1)S(1)} copy-done((bf16[16,32,128]{2,1,0:T(8,128)(2,1)S(1)}, bf16[16,32,128]{2,1,0:T(8,128)(2,1)}, u32[]{:S(2)}) %copy-start) | copy-done | bytes 131096
  0.9 0.0 copy-start.2
  0.9 0.5 y_send.1
  1.4 18.7 %collective-permute-start = (bf16[224,128]{1,0:T(8,128)(2,1)S(1)}, bf16[224,128]{1,0:T(8,128)(2,1)S(1)}, u32[]{:S(2)}, u32[]{:S(2)}) collective-permute-start(bf16[224,128]{1,0:T(8,128)(2,1)S(1)} %get-tuple-element.31.refs_2_), channel_id=1, source_target_pairs={{8,16},{16,8},{24,32},{32,24},{40,48},{48,40},{56,0},{0,56},{9,17}... | collective-permute-start | bytes 172040 | tf_op jit(solution)/shard_map/ppermute | solution.py:393
  20.1 0.0 copy-start.9
  20.1 0.0 copy-start.6
  20.2 0.0 copy-start.1
  20.2 2.1 %collective-permute-start.1 = (bf16[224,128]{1,0:T(8,128)(2,1)S(1)}, bf16[224,128]{1,0:T(8,128)(2,1)S(1)}, u32[]{:S(2)}, u32[]{:S(2)}) collective-permute-start(bf16[224,128]{1,0:T(8,128)(2,1)S(1)} %get-tuple-element.32), channel_id=1, source_target_pairs={{0,8},{8,0},{16,24},{24,16},{32,40},{40,32},{48,56},{56,48},{1,9},... | collective-permute-start | bytes 172040 | tf_op jit(solution)/shard_map/ppermute | solution.py:394
  22.2 0.0 copy-done.2
  22.2 0.0 copy-start.10
  22.3 0.0 copy-start.11
  22.3 0.0 copy-start.12
  22.3 0.2 own_step.1.refs_3_
  22.5 0.0 copy-done.9
  22.5 0.0 copy-start.5
  22.5 0.7 prep_z.1
  23.2 0.0 copy-done.6
  23.3 0.7 prep_y.1
  24.0 0.0 copy-done.10
  24.0 0.0 copy-done.11
  24.0 0.0 copy-done.12
  24.0 0.6 prep_top.1
  24.6 0.0 collective-permute-done.refs_1_
  24.6 0.6 collective-permute-done.1.refs_2_
  25.2 0.0 copy-done.1
  25.2 0.0 copy-done.5
  25.2 0.9 %y_step.1 = (f32[16,32,128]{2,1,0:T(8,128)S(1)}, f32[11,24,128]{2,1,0:T(8,128)S(1)}, f32[9,8,128]{2,1,0:T(8,128)S(1)}, f32[88,128]{1,0:T(8,128)S(1)}, f32[88,128]{1,0:T(8,128)S(1)}) custom-call(bf16[16,32,128]{2,1,0:T(8,128)(2,1)S(1)} %copy-done.1, bf16[224,128]{1,0:T(8,128)(2,1)S(1)} %collective-permute-done.refs_1_, ...), custom_call_target="tpu_custom_call" | custom-call | flops 1000000 | bytes 1000000 | tf_op jit(solution)/shard_map/y_step/pallas_call | solution.py:92
  26.2 5.7 %collective-permute-start.2 = (f32[88,128]{1,0:T(8,128)S(1)}, f32[88,128]{1,0:T(8,128)S(1)}, u32[]{:S(2)}, u32[]{:S(2)}) collective-permute-start(f32[88,128]{1,0:T(8,128)S(1)} %get-tuple-element.38), channel_id=1, source_target_pairs={{1,2},{2,1},{3,4},{4,3},{5,6},{6,5},{7,0},{0,7},{9,10},{10,9},{11,... | collective-permute-start | bytes 135176 | tf_op jit(solution)/shard_map/ppermute | solution.py:412
  31.9 1.9 %collective-permute-start.3 = (f32[88,128]{1,0:T(8,128)S(1)}, f32[88,128]{1,0:T(8,128)S(1)}, u32[]{:S(2)}, u32[]{:S(2)}) collective-permute-start(f32[88,128]{1,0:T(8,128)S(1)} %get-tuple-element.39), channel_id=1, source_target_pairs={{0,1},{1,0},{2,3},{3,2},{4,5},{5,4},{6,7},{7,6},{8,9},{9,8},{10,11... | collective-permute-start | bytes 135176 | tf_op jit(solution)/shard_map/ppermute | solution.py:413
  33.8 3.9 %collective-permute-done.2.refs_1_.refs_2_ = f32[88,128]{1,0:T(8,128)S(1)} collective-permute-done((f32[88,128]{1,0:T(8,128)S(1)}, f32[88,128]{1,0:T(8,128)S(1)}, u32[]{:S(2)}, u32[]{:S(2)}) %collective-permute-start.2) | collective-permute-done | bytes 45088 | tf_op jit(solution)/shard_map/ppermute | solution.py:412
  37.7 0.0 collective-permute-done.3.refs_2_.refs_3_
  37.7 0.2 q3_z_step.1
  37.9 4.2 %collective-permute-start.4 = (f32[8,128]{1,0:T(8,128)S(1)}, f32[8,128]{1,0:T(8,128)S(1)}, u32[]{:S(2)}, u32[]{:S(2)}) collective-permute-start(f32[8,128]{1,0:T(8,128)S(1)} %get-tuple-element.40), channel_id=1, source_target_pairs={{0,64},{64,128},{128,192},{192,256},{256,320},{320,384},{384,448},... | collective-permute-start | bytes 12296 | tf_op jit(solution)/shard_map/ppermute | solution.py:389
  42.1 0.0 collective-permute-start.5
  42.1 0.8 collective-permute-done.4.refs_0_
  42.9 2.3 %collective-permute-done.5.refs_2_ = f32[8,128]{1,0:T(8,128)S(1)} collective-permute-done((f32[8,128]{1,0:T(8,128)S(1)}, f32[8,128]{1,0:T(8,128)S(1)}, u32[]{:S(2)}, u32[]{:S(2)}) %collective-permute-start.5) | collective-permute-done | bytes 4128 | tf_op jit(solution)/shard_map/ppermute | solution.py:389
  45.1 0.7 q3_x_step.1.refs_6_
  45.8 12.5 %all-to-all-start = ((bf16[64,8,128]{2,1,0:T(8,128)(2,1)}), bf16[64,8,128]{2,1,0:T(8,128)(2,1)S(1)}, u32[]{:S(2)}, u32[]{:S(2)}) async-start(bf16[64,8,128]{2,1,0:T(8,128)(2,1)} %bitcast.3), calls=%async_computation | async-start | bytes 262144 | tf_op jit(solution)/shard_map/all_to_all | solution.py:417
  58.3 0.8 near_z_step.1
  59.2 0.3 collective-permute-start.8
  59.5 0.2 collective-permute-start.9
  59.7 3.1 %collective-permute-start.6 = (f32[72,128]{1,0:T(8,128)S(1)}, f32[72,128]{1,0:T(8,128)S(1)}, u32[]{:S(2)}, u32[]{:S(2)}) collective-permute-start(f32[72,128]{1,0:T(8,128)S(1)} %get-tuple-element.51), channel_id=1, source_target_pairs={{0,128},{64,192},{128,256},{192,320},{256,384},{320,448},{384,0},{... | collective-permute-start | bytes 110600 | tf_op jit(solution)/shard_map/ppermute | solution.py:389
  62.8 3.4 %collective-permute-start.7 = (f32[72,128]{1,0:T(8,128)S(1)}, f32[72,128]{1,0:T(8,128)S(1)}, u32[]{:S(2)}, u32[]{:S(2)}) collective-permute-start(f32[72,128]{1,0:T(8,128)S(1)} %get-tuple-element.52), channel_id=1, source_target_pairs={{0,384},{64,448},{128,0},{192,64},{256,128},{320,192},{384,256},{4... | collective-permute-start | bytes 110600 | tf_op jit(solution)/shard_map/ppermute | solution.py:389
  66.2 0.5 collective-permute-done.6.refs_3_
  66.7 1.1 %collective-permute-done.7.refs_4_ = f32[72,128]{1,0:T(8,128)S(1)} collective-permute-done((f32[72,128]{1,0:T(8,128)S(1)}, f32[72,128]{1,0:T(8,128)S(1)}, u32[]{:S(2)}, u32[]{:S(2)}) %collective-permute-start.7) | collective-permute-done | bytes 36896 | tf_op jit(solution)/shard_map/ppermute | solution.py:389
  67.8 0.0 collective-permute-done.8.refs_5_
  67.8 0.0 collective-permute-done.9.refs_6_
  67.8 1.0 %near_x_step.1 = (f32[16,32,128]{2,1,0:T(8,128)S(1)}, f32[11,24,128]{2,1,0:T(8,128)S(1)}) custom-call(f32[2,17]{1,0:T(2,128)S(1)} %copy-done.9, f32[16,32,128]{2,1,0:T(8,128)S(1)} %get-tuple-element.49.refs_1_, f32[11,24,128]{2,1,0:T(8,128)S(1)} %get-tuple-element.50.refs_2_, f32[72,128]{1,0:T(8,128)S(1)} %collective-permute-done.6.refs_3_, ...), custom_call_target="tpu_custom_call" | custom-call | flops 1000000 | bytes 1000000 | tf_op jit(solution)/shard_map/near_x_step/pallas_call | solution.py:92
  68.8 5.1 %all-to-all-done.refs_0_ = bf16[64,8,128]{2,1,0:T(8,128)(2,1)S(1)} async-done(((bf16[64,8,128]{2,1,0:T(8,128)(2,1)}), bf16[64,8,128]{2,1,0:T(8,128)(2,1)S(1)}, u32[]{:S(2)}, u32[]{:S(2)}) %all-to-all-start) | async-done | bytes 131104 | tf_op jit(solution)/shard_map/all_to_all | solution.py:417
  73.9 0.5 top_step.1
  74.4 0.0 copy-start.3
  74.4 0.0 copy-start.4
  74.5 0.0 copy-start.7
  74.5 0.0 copy-start.8
  74.5 11.7 %all_to_all.10.refs_0_ = f32[8,16,256]{2,1,0:T(8,128)S(1)} all-to-all(f32[8,16,256]{2,1,0:T(8,128)S(1)} %top_step.1), channel_id=1, replica_groups=mesh['gx'=8,'gy'=8,'gz'=8] {'gx'}, dimensions={0} | all-to-all | bytes 262144 | tf_op jit(solution)/shard_map/all_to_all | solution.py:431
  86.1 0.0 copy-done.3
  86.1 0.0 copy-done.4
  86.1 0.0 copy-done.7
  86.1 0.0 copy-done.8
  86.2 1.6 %last_step.1 = f32[16,32,128]{2,1,0:T(8,128)} custom-call(f32[8,16,256]{2,1,0:T(8,128)S(1)} %all_to_all.10.refs_0_, f32[16,2048]{1,0:T(8,128)S(1)} %get-tuple-element.36.refs_9_.refs_1_, f32[16,32,128]{2,1,0:T(8,128)S(1)} %get-tuple-element.55.refs_4_.refs_2_, f32[11,24,128]{2,1,0:T(8,128)S(1)} %get-tuple-element.56.refs_3_, bf16[24,16]{1,0:T(8,128)(2,1)S(1)} %copy-done.8, ...), custom_call_target="tpu_custom_call" | custom-call | flops 1000000 | bytes 1000000 | tf_op jit(solution)/shard_map/last_step/pallas_call | solution.py:92
Async XLA Ops:
  0.0 0.9 %copy-start = (bf16[16,32,128]{2,1,0:T(8,128)(2,1)S(1)}, bf16[16,32,128]{2,1,0:T(8,128)(2,1)}, u32[]{:S(2)}) copy-start(bf16[16,32,128]{2,1,0:T(8,128)(2,1)} %refs_0_.10) | copy-start | bytes 393220
  0.9 21.3 %copy-start.2 = (bf16[128,128]{1,0:T(8,128)(2,1)S(1)}, bf16[128,128]{1,0:T(8,128)(2,1)}, u32[]{:S(2)}) copy-start(bf16[128,128]{1,0:T(8,128)(2,1)} %constant.14.clone.refs_1_.refs_6_) | copy-start | bytes 98308
  1.4 23.2 %collective-permute-start = (bf16[224,128]{1,0:T(8,128)(2,1)S(1)}, bf16[224,128]{1,0:T(8,128)(2,1)S(1)}, u32[]{:S(2)}, u32[]{:S(2)}) collective-permute-start(bf16[224,128]{1,0:T(8,128)(2,1)S(1)} %get-tuple-element.31.refs_2_), channel_id=1, source_target_pairs={{8,16},{16,8},{24,32},{32,24},{40,48},{48,40},{56,0},{0,56},{9,17}... | collective-permute-start | bytes 172040 | tf_op jit(solution)/shard_map/ppermute | solution.py:393
  20.1 2.4 %copy-start.9 = (f32[2,17]{1,0:T(2,128)S(1)}, f32[2,17]{1,0:T(2,128)}, u32[]{:S(2)}) copy-start(f32[2,17]{1,0:T(2,128)} %refs_0_.11) | copy-start | bytes 412
  20.1 3.1 %copy-start.6 = (f32[40,64]{1,0:T(8,128)S(1)}, f32[40,64]{1,0:T(8,128)}, u32[]{:S(2)}) copy-start(f32[40,64]{1,0:T(8,128)} %constant.15.clone.refs_1_) | copy-start | bytes 30724
  20.2 5.1 %copy-start.1 = (bf16[16,32,128]{2,1,0:T(8,128)(2,1)S(1)}, bf16[16,32,128]{2,1,0:T(8,128)(2,1)}, u32[]{:S(2)}) copy-start(bf16[16,32,128]{2,1,0:T(8,128)(2,1)} %refs_0_.10) | copy-start | bytes 393220
  20.2 5.1 %collective-permute-start.1 = (bf16[224,128]{1,0:T(8,128)(2,1)S(1)}, bf16[224,128]{1,0:T(8,128)(2,1)S(1)}, u32[]{:S(2)}, u32[]{:S(2)}) collective-permute-start(bf16[224,128]{1,0:T(8,128)(2,1)S(1)} %get-tuple-element.32), channel_id=1, source_target_pairs={{0,8},{8,0},{16,24},{24,16},{32,40},{40,32},{48,56},{56,48},{1,9},... | collective-permute-start | bytes 172040 | tf_op jit(solution)/shard_map/ppermute | solution.py:394
  22.2 1.7 %copy-start.10 = (f32[256]{0:T(256)S(1)}, f32[256]{0:T(256)}, u32[]{:S(2)}) copy-start(f32[256]{0:T(256)} %param.16) | copy-start | bytes 3076
  22.3 1.7 %copy-start.11 = (f32[32]{0:T(128)S(1)}, f32[32]{0:T(128)}, u32[]{:S(2)}) copy-start(f32[32]{0:T(128)} %param.14) | copy-start | bytes 388
  22.3 1.7 %copy-start.12 = (f32[64]{0:T(128)S(1)}, f32[64]{0:T(128)}, u32[]{:S(2)}) copy-start(f32[64]{0:T(128)} %param.15) | copy-start | bytes 772
  22.5 2.7 %copy-start.5 = (bf16[128,128]{1,0:T(8,128)(2,1)S(1)}, bf16[128,128]{1,0:T(8,128)(2,1)}, u32[]{:S(2)}) copy-start(bf16[128,128]{1,0:T(8,128)(2,1)} %constant.16.clone.refs_7_) | copy-start | bytes 98308
  26.2 11.6 %collective-permute-start.2 = (f32[88,128]{1,0:T(8,128)S(1)}, f32[88,128]{1,0:T(8,128)S(1)}, u32[]{:S(2)}, u32[]{:S(2)}) collective-permute-start(f32[88,128]{1,0:T(8,128)S(1)} %get-tuple-element.38), channel_id=1, source_target_pairs={{1,2},{2,1},{3,4},{4,3},{5,6},{6,5},{7,0},{0,7},{9,10},{10,9},{11,... | collective-permute-start | bytes 135176 | tf_op jit(solution)/shard_map/ppermute | solution.py:412
  31.9 5.9 %collective-permute-start.3 = (f32[88,128]{1,0:T(8,128)S(1)}, f32[88,128]{1,0:T(8,128)S(1)}, u32[]{:S(2)}, u32[]{:S(2)}) collective-permute-start(f32[88,128]{1,0:T(8,128)S(1)} %get-tuple-element.39), channel_id=1, source_target_pairs={{0,1},{1,0},{2,3},{3,2},{4,5},{5,4},{6,7},{7,6},{8,9},{9,8},{10,11... | collective-permute-start | bytes 135176 | tf_op jit(solution)/shard_map/ppermute | solution.py:413
  37.9 5.0 %collective-permute-start.4 = (f32[8,128]{1,0:T(8,128)S(1)}, f32[8,128]{1,0:T(8,128)S(1)}, u32[]{:S(2)}, u32[]{:S(2)}) collective-permute-start(f32[8,128]{1,0:T(8,128)S(1)} %get-tuple-element.40), channel_id=1, source_target_pairs={{0,64},{64,128},{128,192},{192,256},{256,320},{320,384},{384,448},... | collective-permute-start | bytes 12296 | tf_op jit(solution)/shard_map/ppermute | solution.py:389
  42.1 3.0 %collective-permute-start.5 = (f32[8,128]{1,0:T(8,128)S(1)}, f32[8,128]{1,0:T(8,128)S(1)}, u32[]{:S(2)}, u32[]{:S(2)}) collective-permute-start(f32[8,128]{1,0:T(8,128)S(1)} %get-tuple-element.42), channel_id=1, source_target_pairs={{0,448},{64,0},{128,64},{192,128},{256,192},{320,256},{384,320},{4... | collective-permute-start | bytes 12296 | tf_op jit(solution)/shard_map/ppermute | solution.py:389
  45.8 28.1 %all-to-all-start = ((bf16[64,8,128]{2,1,0:T(8,128)(2,1)}), bf16[64,8,128]{2,1,0:T(8,128)(2,1)S(1)}, u32[]{:S(2)}, u32[]{:S(2)}) async-start(bf16[64,8,128]{2,1,0:T(8,128)(2,1)} %bitcast.3), calls=%async_computation | async-start | bytes 262144 | tf_op jit(solution)/shard_map/all_to_all | solution.py:417
  59.2 8.6 %collective-permute-start.8 = (f32[520,128]{1,0:T(8,128)S(1)}, f32[520,128]{1,0:T(8,128)S(1)}, u32[]{:S(2)}, u32[]{:S(2)}) collective-permute-start(f32[520,128]{1,0:T(8,128)S(1)} %get-tuple-element.53), channel_id=1, source_target_pairs={{0,64},{64,128},{128,192},{192,256},{256,320},{320,384},{384,448},... | collective-permute-start | bytes 798728 | tf_op jit(solution)/shard_map/ppermute | solution.py:389
  59.5 8.3 %collective-permute-start.9 = (f32[520,128]{1,0:T(8,128)S(1)}, f32[520,128]{1,0:T(8,128)S(1)}, u32[]{:S(2)}, u32[]{:S(2)}) collective-permute-start(f32[520,128]{1,0:T(8,128)S(1)} %get-tuple-element.54), channel_id=1, source_target_pairs={{0,448},{64,0},{128,64},{192,128},{256,192},{320,256},{384,320},{4... | collective-permute-start | bytes 798728 | tf_op jit(solution)/shard_map/ppermute | solution.py:389
  59.7 7.0 %collective-permute-start.6 = (f32[72,128]{1,0:T(8,128)S(1)}, f32[72,128]{1,0:T(8,128)S(1)}, u32[]{:S(2)}, u32[]{:S(2)}) collective-permute-start(f32[72,128]{1,0:T(8,128)S(1)} %get-tuple-element.51), channel_id=1, source_target_pairs={{0,128},{64,192},{128,256},{192,320},{256,384},{320,448},{384,0},{... | collective-permute-start | bytes 110600 | tf_op jit(solution)/shard_map/ppermute | solution.py:389
  62.8 5.0 %collective-permute-start.7 = (f32[72,128]{1,0:T(8,128)S(1)}, f32[72,128]{1,0:T(8,128)S(1)}, u32[]{:S(2)}, u32[]{:S(2)}) collective-permute-start(f32[72,128]{1,0:T(8,128)S(1)} %get-tuple-element.52), channel_id=1, source_target_pairs={{0,384},{64,448},{128,0},{192,64},{256,128},{320,192},{384,256},{4... | collective-permute-start | bytes 110600 | tf_op jit(solution)/shard_map/ppermute | solution.py:389
  74.4 11.7 %copy-start.3 = (bf16[128,128]{1,0:T(8,128)(2,1)S(1)}, bf16[128,128]{1,0:T(8,128)(2,1)}, u32[]{:S(2)}) copy-start(bf16[128,128]{1,0:T(8,128)(2,1)} %constant.18.clone.refs_5_) | copy-start | bytes 98308
  74.4 11.7 %copy-start.4 = (bf16[128,128]{1,0:T(8,128)(2,1)S(1)}, bf16[128,128]{1,0:T(8,128)(2,1)}, u32[]{:S(2)}) copy-start(bf16[128,128]{1,0:T(8,128)(2,1)} %constant.20.clone.refs_7_) | copy-start | bytes 98308
  74.5 11.7 %copy-start.7 = (bf16[32,24]{1,0:T(8,128)(2,1)S(1)}, bf16[32,24]{1,0:T(8,128)(2,1)}, u32[]{:S(2)}) copy-start(bf16[32,24]{1,0:T(8,128)(2,1)} %constant.19.clone.refs_6_) | copy-start | bytes 4612
  74.5 11.7 %copy-start.8 = (bf16[24,16]{1,0:T(8,128)(2,1)S(1)}, bf16[24,16]{1,0:T(8,128)(2,1)}, u32[]{:S(2)}) copy-start(bf16[24,16]{1,0:T(8,128)(2,1)} %constant.17.clone.refs_4_) | copy-start | bytes 2308

commit v6 on v5

--- a/solution.py
+++ b/solution.py
@@ -51,7 +51,11 @@
 
 y_sources = table(40, 64, y_source)
 y_raise_top = table(24, 16, lambda r, c: weight.get((r - 1) - 2 * (c - 2), 0.0) if r < 19 and c < 13 else 0.0)
-z_raise_top = table(128, 128, lambda r, c: weight.get((c - 1) - 2 * (r - 2), 0.0) if r < 37 and c < 67 else 0.0)
+z_raise_top = table(
+    128,
+    128,
+    lambda r, c: weight.get((c - 1) - 2 * ((r if r < 32 else 32 + (r - 32) % 5) - 2), 0.0) if r < 57 and c < 67 else 0.0,
+)
 y_raise = table(32, 24, lambda r, c: weight.get(r - 2 * (c - 1), 0.0) if c < 19 else 0.0)
 z_raise = table(128, 128, lambda r, c: weight.get(c - 2 * (r - 1), 0.0) if r < 67 else 0.0)
 
@@ -116,7 +120,7 @@
 def prep_y(taps, sources, my1, my2):
     column = iota((32, 48), 1)
     cell = jnp.where(column < 32, column, jnp.where(column < 40, column - 40, column - 8))
-    terms = split(fill(cell - iota((32, 48), 0), {m: taps[0, m + 8] for m in range(-8, 9)}), 3)
+    terms = split(fill(cell - iota((32, 48), 0), {m: taps[0, m + 8] for m in range(-8, 9)}), 2)
     my1[...] = jnp.concatenate([term.astype(f32) for term in terms], axis=0).astype(bf16)
     coarse = iota((24, 40), 1) - 9
     near = fill(coarse - (iota((24, 40), 0) - 1), {m: taps[1, m + 8] for m in range(-8, 9)})
@@ -145,18 +149,20 @@
 def prep_top(top_x, top_y, top_z, wz1, wz2, my, wx):
     gx, gy, gz = lax.axis_index("gx"), lax.axis_index("gy"), lax.axis_index("gz")
     tz = toeplitz(top_z[...], lax.rem(258 - 32 * gz, 256), 256)
-    lane = iota((256, 256), 1)
-    near = jnp.where(lane < 64, tz, 0.0)
-    blocks = [near] + [pltpu.roll(near, 64 * a, 1) for a in range(1, 4)]
-    for g in range(8):
-        for a in range(4):
+    lane = iota((256, 128), 1)
+    near, past = tz[:, 0:128], jnp.zeros((256, 128), f32)
+    for t in range(5):
+        past = jnp.where(lane // 5 == t, pltpu.roll(near, 96 + 5 * t, 1), past)
+    near, past = jnp.where(lane < 32, near, 0.0), jnp.where(lane < 25, past, 0.0)
+    for a in range(4):
+        both = lanes([pltpu.roll(part, 32 * a, 1) if a else part for part in (near, past)])
+        for g in range(8):
             rows = pl.ds(128 * g + 32 * a, 32)
-            part = blocks[a][32 * g : 32 * g + 32]
-            wz1[rows, :], wz2[rows, :] = split(part, 2)
+            wz1[rows, :], wz2[rows, :] = split(both[32 * g : 32 * g + 32], 2)
     ty = toeplitz(lanes([top_y[...]] * 2), lax.rem(130 - 8 * gy, 128), 128)
     my[...] = ty.T[0:16, 0:64]
     tx = toeplitz(lanes([top_x[...]] * 4), lax.rem(130 - 4 * gx, 128), 128)
-    spread = jnp.where(iota((32, 2048), 1) // 64 == iota((32, 2048), 0), 1.0, 0.0)
+    spread = jnp.where(iota((32, 1024), 1) // 32 == iota((32, 1024), 0), 1.0, 0.0)
     wx[...] = dot(tx.T[0:16, 0:32], spread)
 
 
@@ -223,7 +229,7 @@
     raw = [[part[8 * i : 8 * i + 8] for i in range(16)] for part in (low, high)]
     columns = lanes([jnp.concatenate([cells[i], raw[0][i], raw[1][i]], axis=0) for i in range(16)])
     terms = jnp.dot(my1[...], columns.astype(bf16), preferred_element_type=f32)
-    done = terms[0:32] + (terms[32:64] + terms[64:96])
+    done = terms[0:32] + terms[32:64]
     parts1 = [done[:, 128 * i : 128 * i + 128] for i in range(16)]
 
     sides = [level2_rows(part) for part in raw]
@@ -295,7 +301,7 @@
     out[...] = jnp.broadcast_to(pair[None], (32, 16, 128))
 
 
-def near_z_step(n1, n2, from_odd, from_even, mz1, mz2, n1_out, n2_out, to_low, to_high, to_low2, to_high2):
+def near_z_step(n1, n2, from_odd, from_even, mz1, mz2, n1_out, n2_out, to_low, to_high, to_even, to_odd):
     low, high = arrived("gz", from_even, from_odd, pl.ds(0, 32))
     rows = jnp.concatenate([lanes([n1[i], windows(low, high, i, 8)]) for i in range(16)], axis=0)
     done1 = dot(rows, mz1[...])
@@ -310,11 +316,14 @@
     to_high[0:256] = done1[256:512]
     to_low[256:520] = done2
     to_high[256:520] = done2
-    to_low2[...] = done2[0:72]
-    to_high2[...] = done2[192:264]
-
-
-def near_x_step(taps, n1, n2, low2, high2, low, high, n1_out, n2_out):
+    odd_chip = lax.rem(lax.axis_index("gx") // 2, 2) == 1
+    to_even[...], to_odd[...] = choose(odd_chip, done2[0:72], done2[192:264])
+
+
+def near_x_step(taps, n1, n2, even2, odd2, low, high, n1_out, n2_out):
+    odd_chip = lax.rem(lax.axis_index("gx") // 2, 2) == 1
+    low2 = jnp.where(odd_chip, even2[...], odd2[...])
+    high2 = jnp.where(odd_chip, odd2[...], even2[...])
     for t in range(4):
         f = {}
         for i in range(8):
@@ -349,7 +358,13 @@
     rows = lanes([whole[:, g].reshape(64, 128) for g in range(8)]).astype(bf16)
     along_z = jnp.dot(rows, wz1[...], preferred_element_type=f32)
     along_z = along_z + jnp.dot(rows, wz2[...], preferred_element_type=f32)
-    out[...] = jnp.broadcast_to(dot(my[...], along_z)[None], (8, 16, 256))
+    done = dot(my[...], along_z)
+    row = iota((16, 128), 0)
+    block, past = done[:, 0:128], jnp.where(iota((16, 128), 1) % 32 // 5 == row % 5, done[:, 128:256], 0.0)
+    for t in range(3):
+        mine = (row // 5 == t) & (row < 13)
+        block = jnp.where(row == 13 + t, jnp.sum(jnp.where(mine, past, 0.0), axis=0, keepdims=True), block)
+    out[...] = jnp.broadcast_to(block[None], (8, 16, 128))
 
 
 def raise_rows(rows, first, last):
@@ -365,14 +380,17 @@
 
 def last_step(top, wx, n1, n2, y1, z1, y2, z2, out):
     e3 = {}
+    row, lane = iota((16, 128), 0), iota((16, 128), 1)
+    here = (lane >= 32) & (lane < 57) & (lane % 32 // 5 == row % 5)
     for i in range(9):
         total = None
         for g in range(8):
-            for h in range(2):
-                at = 256 * g + 128 * h
-                term = wx[i : i + 1, at : at + 128] * top[g, :, 128 * h : 128 * h + 128]
-                total = term if total is None else total + term
-        e3[i - 2] = total + pltpu.roll(total, 64, 1)
+            term = wx[i : i + 1, 128 * g : 128 * g + 128] * top[g]
+            total = term if total is None else total + term
+        total = total + pltpu.roll(total, 64, 1)
+        total = total + pltpu.roll(total, 32, 1)
+        past = jnp.where(row < 5, total[13:14], jnp.where(row < 10, total[14:15], total[15:16]))
+        e3[i - 2] = jnp.where(lane < 32, total, jnp.where(here, past, 0.0))
     e2 = raise_rows(e3, -1, 9)
     wide = from_left(y1, lanes([e2[i] for i in range(-1, 10)]))
     tall = jnp.concatenate([wide[:, 128 * i : 128 * i + 128] for i in range(11)], axis=0)
@@ -393,13 +411,13 @@
     from_odd = lax.ppermute(to_odd, "gy", swap_odd)
     from_even = lax.ppermute(to_even, "gy", swap_even)
     my1, my2 = call(
-        prep_y, [((96, 48), bf16), ((32, 64), f32)], [kernel_taps, jnp.asarray(y_sources)], smem=(0,)
+        prep_y, [((64, 48), bf16), ((32, 64), f32)], [kernel_taps, jnp.asarray(y_sources)], smem=(0,)
     )
     mz1, mz2 = call(prep_z, [((256, 128), f32)] * 2, [kernel_taps], smem=(0,))
     (own_share,) = call(own_step, [((11, 32, 128), f32)], [charge, z_matrix], after=[to_odd])
     wz1, wz2, ty, wx = call(
         prep_top,
-        [((1024, 256), bf16)] * 2 + [((16, 64), f32), ((16, 2048), f32)],
+        [((1024, 256), bf16)] * 2 + [((16, 64), f32), ((16, 1024), f32)],
         [top_x[None], top_y[None], top_z[None]],
     )
 
@@ -417,17 +435,22 @@
     gathered = lax.all_to_all(
         message.reshape(64, 8, 128), ("gy", "gz"), split_axis=0, concat_axis=0, tiled=True
     )
-    n1, n2, to_low, to_high, to_low2, to_high2 = call(
+    n1, n2, to_low, to_high, to_even, to_odd = call(
         near_z_step,
         [((16, 32, 128), f32), ((11, 24, 128), f32)] + [((520, 128), f32)] * 2 + [((72, 128), f32)] * 2,
         [n1, n2, from_odd, from_even, mz1, mz2], after=[message],
     )
-    halos = [shift(to_high2, 2), shift(to_low2, -2), shift(to_high, 1), shift(to_low, -1)]
+    halos = [
+        lax.ppermute(to_even, "gx", [(0, 2), (2, 0), (1, 3), (3, 1), (4, 6), (6, 4), (5, 7), (7, 5)]),
+        lax.ppermute(to_odd, "gx", [(2, 4), (4, 2), (3, 5), (5, 3), (6, 0), (0, 6), (7, 1), (1, 7)]),
+        shift(to_high, 1),
+        shift(to_low, -1),
+    ]
     n1, n2 = call(
         near_x_step, [((16, 32, 128), f32), ((11, 24, 128), f32)],
         [kernel_taps, n1, n2, *halos], smem=(0,),
     )
-    (message,) = call(top_step, [((8, 16, 256), f32)], [gathered, wz1, wz2, ty], after=[n1])
+    (message,) = call(top_step, [((8, 16, 128), f32)], [gathered, wz1, wz2, ty], after=[n1])
     top = lax.all_to_all(message, "gx", split_axis=0, concat_axis=0, tiled=True)
     (result,) = call(
         last_step, [((16, 32, 128), f32)],

time: 88.2 us -> 87.8 us (level)
    ppermute x0 -> x2, starting transfers between devices: none -> 6.54 us  [the longest x1 3.43 us: per_device(): lax.ppermute(to_odd, 'gx', [(2, 4), (4, 2), (3, 5), (5, 3), (6, 0), (0, 6...]
    ppermute x6 -> x4, starting transfers between devices: 11.2 us -> 4.72 us  [shift(): return lax.ppermute(block, 'gx', [(i, (i + by) % 8) for i in range(8)])]
    ppermute x0 -> x2, waiting for transfers between devices: none -> 2.76 us  [the longest x1 2.76 us: per_device(): lax.ppermute(to_odd, 'gx', [(2, 4), (4, 2), (3, 5), (5, 3), (6, 0), (0, 6...]
    ppermute x6 -> x4, waiting for transfers between devices: 4.63 us -> 3.03 us  [shift(): return lax.ppermute(block, 'gx', [(i, (i + by) % 8) for i in range(8)])]
    all_to_all x1, waiting for transfers between devices: 5.09 us -> 3.85 us  [per_device(): lax.all_to_all(message.reshape(64, 8, 128), ('gy', 'gz'), split_axis=0, c...]
  transfers between devices with their start and end apart: 11 -> 11, of which waited for: 7 -> 6; matrix products, arithmetic and copies ran while one was open for 0% -> 0% of each run, Pallas kernels for 5% -> 5%
where the time goes in v6:
time: 87.8 us; the launch traced here: 87.3 us
  starting transfers between devices  52.2 us (59%)
  waiting for transfers between devices  14 us (16%)
  blocking collectives  11.2 us (13%)
  Pallas kernels  8.72 us (10%)
  local copies, waits for them, and re-layouts  0.98 us (1%)
    ppermute x1, starting transfers between devices, per_device(): from_odd = lax.ppermute(to_odd, 'gy', swap_odd)  18.7 us
    all_to_all x1, starting transfers between devices, per_device(): lax.all_to_all(message.reshape(64, 8, 128), ('gy', 'gz'), split_axis=0, c...  12.5 us
    all_to_all x1, blocking collectives, per_device(): top = lax.all_to_all(message, 'gx', split_axis=0, concat_axis=0, tiled=True)  11.2 us
    pallas_call x12, Pallas kernels, call(): pl.pallas_call(kernel, out_shape=[jax.ShapeDtypeStruct(s, d) for s, d in...  8.72 us
    ppermute x1, starting transfers between devices, per_device(): from_odd = lax.ppermute(to_odd, 'gz', swap_odd)  5.67 us
    ppermute x4, starting transfers between devices, shift(): return lax.ppermute(block, 'gx', [(i, (i + by) % 8) for i in range(8)])  4.72 us
    ppermute x1, waiting for transfers between devices, per_device(): from_odd = lax.ppermute(to_odd, 'gz', swap_odd)  3.94 us
    all_to_all x1, waiting for transfers between devices, per_device(): lax.all_to_all(message.reshape(64, 8, 128), ('gy', 'gz'), split_axis=0, c...  3.85 us
  transfers between devices with their start and end apart: 11, of which 6 were waited for; matrix products, arithmetic and copies ran while one was open for 0% of the time, Pallas kernels for 5%

profile of v6, /device:TPU:1, one launch (start us, length us, event | category | flops | bytes accessed | tf_op | source)
XLA Modules:
  0.0 87.3 jit_solution(16148496048258096999)
XLA Ops:
  0.0 0.0 copy-start
  0.0 0.9 %copy-done = bf16[16,32,128]{2,1,0:T(8,128)(2,1)S(1)} copy-done((bf16[16,32,128]{2,1,0:T(8,128)(2,1)S(1)}, bf16[16,32,128]{2,1,0:T(8,128)(2,1)}, u32[]{:S(2)}) %copy-start) | copy-done | bytes 131096
  0.9 0.0 copy-start.2
  0.9 0.5 y_send.1
  1.4 18.7 %collective-permute-start = (bf16[224,128]{1,0:T(8,128)(2,1)S(1)}, bf16[224,128]{1,0:T(8,128)(2,1)S(1)}, u32[]{:S(2)}, u32[]{:S(2)}) collective-permute-start(bf16[224,128]{1,0:T(8,128)(2,1)S(1)} %get-tuple-element.31.refs_2_), channel_id=1, source_target_pairs={{8,16},{16,8},{24,32},{32,24},{40,48},{48,40},{56,0},{0,56},{9,17}... | collective-permute-start | bytes 172040 | tf_op jit(solution)/shard_map/ppermute | solution.py:411
  20.1 0.0 copy-start.9
  20.1 0.0 copy-start.6
  20.2 0.0 copy-start.1
  20.2 2.1 %collective-permute-start.1 = (bf16[224,128]{1,0:T(8,128)(2,1)S(1)}, bf16[224,128]{1,0:T(8,128)(2,1)S(1)}, u32[]{:S(2)}, u32[]{:S(2)}) collective-permute-start(bf16[224,128]{1,0:T(8,128)(2,1)S(1)} %get-tuple-element.32), channel_id=1, source_target_pairs={{0,8},{8,0},{16,24},{24,16},{32,40},{40,32},{48,56},{56,48},{1,9},... | collective-permute-start | bytes 172040 | tf_op jit(solution)/shard_map/ppermute | solution.py:412
  22.2 0.0 copy-done.2
  22.2 0.0 copy-start.10
  22.3 0.0 copy-start.11
  22.3 0.0 copy-start.12
  22.3 0.2 own_step.1.refs_3_
  22.5 0.0 copy-done.9
  22.5 0.0 copy-start.3
  22.5 0.7 prep_z.1
  23.2 0.0 copy-done.6
  23.3 0.7 prep_y.1
  24.0 0.0 copy-done.10
  24.0 0.0 copy-done.11
  24.0 0.0 copy-done.12
  24.0 0.8 prep_top.1
  24.9 0.0 collective-permute-done.refs_1_
  24.9 0.4 collective-permute-done.1.refs_2_
  25.2 0.0 copy-done.1
  25.2 0.0 copy-done.3
  25.2 0.9 %y_step.1 = (f32[16,32,128]{2,1,0:T(8,128)S(1)}, f32[11,24,128]{2,1,0:T(8,128)S(1)}, f32[9,8,128]{2,1,0:T(8,128)S(1)}, f32[88,128]{1,0:T(8,128)S(1)}, f32[88,128]{1,0:T(8,128)S(1)}) custom-call(bf16[16,32,128]{2,1,0:T(8,128)(2,1)S(1)} %copy-done.1, bf16[224,128]{1,0:T(8,128)(2,1)S(1)} %collective-permute-done.refs_1_, ...), custom_call_target="tpu_custom_call" | custom-call | flops 1000000 | bytes 1000000 | tf_op jit(solution)/shard_map/y_step/pallas_call | solution.py:96
  26.1 5.7 %collective-permute-start.2 = (f32[88,128]{1,0:T(8,128)S(1)}, f32[88,128]{1,0:T(8,128)S(1)}, u32[]{:S(2)}, u32[]{:S(2)}) collective-permute-start(f32[88,128]{1,0:T(8,128)S(1)} %get-tuple-element.38), channel_id=1, source_target_pairs={{1,2},{2,1},{3,4},{4,3},{5,6},{6,5},{7,0},{0,7},{9,10},{10,9},{11,... | collective-permute-start | bytes 135176 | tf_op jit(solution)/shard_map/ppermute | solution.py:430
  31.8 1.9 %collective-permute-start.3 = (f32[88,128]{1,0:T(8,128)S(1)}, f32[88,128]{1,0:T(8,128)S(1)}, u32[]{:S(2)}, u32[]{:S(2)}) collective-permute-start(f32[88,128]{1,0:T(8,128)S(1)} %get-tuple-element.39), channel_id=1, source_target_pairs={{0,1},{1,0},{2,3},{3,2},{4,5},{5,4},{6,7},{7,6},{8,9},{9,8},{10,11... | collective-permute-start | bytes 135176 | tf_op jit(solution)/shard_map/ppermute | solution.py:431
  33.7 3.9 %collective-permute-done.2.refs_1_.refs_2_ = f32[88,128]{1,0:T(8,128)S(1)} collective-permute-done((f32[88,128]{1,0:T(8,128)S(1)}, f32[88,128]{1,0:T(8,128)S(1)}, u32[]{:S(2)}, u32[]{:S(2)}) %collective-permute-start.2) | collective-permute-done | bytes 45088 | tf_op jit(solution)/shard_map/ppermute | solution.py:430
  37.7 0.0 collective-permute-done.3.refs_2_.refs_3_
  37.7 0.2 q3_z_step.1
  37.8 4.2 %collective-permute-start.4 = (f32[8,128]{1,0:T(8,128)S(1)}, f32[8,128]{1,0:T(8,128)S(1)}, u32[]{:S(2)}, u32[]{:S(2)}) collective-permute-start(f32[8,128]{1,0:T(8,128)S(1)} %get-tuple-element.40), channel_id=1, source_target_pairs={{0,64},{64,128},{128,192},{192,256},{256,320},{320,384},{384,448},... | collective-permute-start | bytes 12296 | tf_op jit(solution)/shard_map/ppermute | solution.py:407
  42.0 0.0 collective-permute-start.5
  42.1 0.8 collective-permute-done.4.refs_0_
  42.8 2.3 %collective-permute-done.5.refs_2_ = f32[8,128]{1,0:T(8,128)S(1)} collective-permute-done((f32[8,128]{1,0:T(8,128)S(1)}, f32[8,128]{1,0:T(8,128)S(1)}, u32[]{:S(2)}, u32[]{:S(2)}) %collective-permute-start.5) | collective-permute-done | bytes 4128 | tf_op jit(solution)/shard_map/ppermute | solution.py:407
  45.1 0.7 q3_x_step.1.refs_6_
  45.7 12.5 %all-to-all-start = ((bf16[64,8,128]{2,1,0:T(8,128)(2,1)}), bf16[64,8,128]{2,1,0:T(8,128)(2,1)S(1)}, u32[]{:S(2)}, u32[]{:S(2)}) async-start(bf16[64,8,128]{2,1,0:T(8,128)(2,1)} %bitcast.3), calls=%async_computation | async-start | bytes 262144 | tf_op jit(solution)/shard_map/all_to_all | solution.py:435
  58.3 0.9 near_z_step.1
  59.1 0.3 collective-permute-start.8
  59.5 0.2 collective-permute-start.9
  59.7 3.1 %collective-permute-start.6 = (f32[72,128]{1,0:T(8,128)S(1)}, f32[72,128]{1,0:T(8,128)S(1)}, u32[]{:S(2)}, u32[]{:S(2)}) collective-permute-start(f32[72,128]{1,0:T(8,128)S(1)} %get-tuple-element.51), channel_id=1, source_target_pairs={{0,128},{128,0},{64,192},{192,64},{256,384},{384,256},{320,448},{4... | collective-permute-start | bytes 110600 | tf_op jit(solution)/shard_map/ppermute | solution.py:444
  62.8 3.4 %collective-permute-start.7 = (f32[72,128]{1,0:T(8,128)S(1)}, f32[72,128]{1,0:T(8,128)S(1)}, u32[]{:S(2)}, u32[]{:S(2)}) collective-permute-start(f32[72,128]{1,0:T(8,128)S(1)} %get-tuple-element.52), channel_id=1, source_target_pairs={{128,256},{256,128},{192,320},{320,192},{384,0},{0,384},{448,64},{... | collective-permute-start | bytes 110600 | tf_op jit(solution)/shard_map/ppermute | solution.py:445
  66.2 0.0 collective-permute-done.6.refs_3_
  66.2 2.8 %collective-permute-done.7.refs_4_ = f32[72,128]{1,0:T(8,128)S(1)} collective-permute-done((f32[72,128]{1,0:T(8,128)S(1)}, f32[72,128]{1,0:T(8,128)S(1)}, u32[]{:S(2)}, u32[]{:S(2)}) %collective-permute-start.7) | collective-permute-done | bytes 36896 | tf_op jit(solution)/shard_map/ppermute | solution.py:445
  69.0 0.0 collective-permute-done.8.refs_5_
  69.0 0.0 collective-permute-done.9.refs_6_
  69.0 1.0 %near_x_step.1 = (f32[16,32,128]{2,1,0:T(8,128)S(1)}, f32[11,24,128]{2,1,0:T(8,128)S(1)}) custom-call(f32[2,17]{1,0:T(2,128)S(1)} %copy-done.9, f32[16,32,128]{2,1,0:T(8,128)S(1)} %get-tuple-element.49.refs_1_, f32[11,24,128]{2,1,0:T(8,128)S(1)} %get-tuple-element.50.refs_2_, f32[72,128]{1,0:T(8,128)S(1)} %collective-permute-done.6.refs_3_, ...), custom_call_target="tpu_custom_call" | custom-call | flops 1000000 | bytes 1000000 | tf_op jit(solution)/shard_map/near_x_step/pallas_call | solution.py:96
  70.0 3.9 %all-to-all-done.refs_0_ = bf16[64,8,128]{2,1,0:T(8,128)(2,1)S(1)} async-done(((bf16[64,8,128]{2,1,0:T(8,128)(2,1)}), bf16[64,8,128]{2,1,0:T(8,128)(2,1)S(1)}, u32[]{:S(2)}, u32[]{:S(2)}) %all-to-all-start) | async-done | bytes 131104 | tf_op jit(solution)/shard_map/all_to_all | solution.py:435
  73.9 0.5 top_step.1
  74.4 0.0 copy-start.4
  74.4 0.0 copy-start.5
  74.4 0.0 copy-start.7
  74.4 0.0 copy-start.8
  74.4 11.2 %all_to_all.10.refs_0_ = f32[8,16,128]{2,1,0:T(8,128)S(1)} all-to-all(f32[8,16,128]{2,1,0:T(8,128)S(1)} %top_step.1), channel_id=1, replica_groups=mesh['gx'=8,'gy'=8,'gz'=8] {'gx'}, dimensions={0} | all-to-all | bytes 131072 | tf_op jit(solution)/shard_map/all_to_all | solution.py:454
  85.7 0.0 copy-done.4
  85.7 0.0 copy-done.5
  85.7 0.0 copy-done.7
  85.7 0.0 copy-done.8
  85.7 1.6 %last_step.1 = f32[16,32,128]{2,1,0:T(8,128)} custom-call(f32[8,16,128]{2,1,0:T(8,128)S(1)} %all_to_all.10.refs_0_, f32[16,1024]{1,0:T(8,128)S(1)} %get-tuple-element.36.refs_9_.refs_1_, f32[16,32,128]{2,1,0:T(8,128)S(1)} %get-tuple-element.55.refs_4_.refs_2_, f32[11,24,128]{2,1,0:T(8,128)S(1)} %get-tuple-element.56.refs_3_, bf16[24,16]{1,0:T(8,128)(2,1)S(1)} %copy-done.8, ...), custom_call_target="tpu_custom_call" | custom-call | flops 1000000 | bytes 1000000 | tf_op jit(solution)/shard_map/last_step/pallas_call | solution.py:96
Async XLA Ops:
  0.0 0.9 %copy-start = (bf16[16,32,128]{2,1,0:T(8,128)(2,1)S(1)}, bf16[16,32,128]{2,1,0:T(8,128)(2,1)}, u32[]{:S(2)}) copy-start(bf16[16,32,128]{2,1,0:T(8,128)(2,1)} %refs_0_.10) | copy-start | bytes 393220
  0.9 21.3 %copy-start.2 = (bf16[128,128]{1,0:T(8,128)(2,1)S(1)}, bf16[128,128]{1,0:T(8,128)(2,1)}, u32[]{:S(2)}) copy-start(bf16[128,128]{1,0:T(8,128)(2,1)} %constant.14.clone.refs_1_.refs_6_) | copy-start | bytes 98308
  1.4 23.5 %collective-permute-start = (bf16[224,128]{1,0:T(8,128)(2,1)S(1)}, bf16[224,128]{1,0:T(8,128)(2,1)S(1)}, u32[]{:S(2)}, u32[]{:S(2)}) collective-permute-start(bf16[224,128]{1,0:T(8,128)(2,1)S(1)} %get-tuple-element.31.refs_2_), channel_id=1, source_target_pairs={{8,16},{16,8},{24,32},{32,24},{40,48},{48,40},{56,0},{0,56},{9,17}... | collective-permute-start | bytes 172040 | tf_op jit(solution)/shard_map/ppermute | solution.py:411
  20.1 2.4 %copy-start.9 = (f32[2,17]{1,0:T(2,128)S(1)}, f32[2,17]{1,0:T(2,128)}, u32[]{:S(2)}) copy-start(f32[2,17]{1,0:T(2,128)} %refs_0_.11) | copy-start | bytes 412
  20.1 3.1 %copy-start.6 = (f32[40,64]{1,0:T(8,128)S(1)}, f32[40,64]{1,0:T(8,128)}, u32[]{:S(2)}) copy-start(f32[40,64]{1,0:T(8,128)} %constant.15.clone.refs_1_) | copy-start | bytes 30724
  20.2 5.1 %copy-start.1 = (bf16[16,32,128]{2,1,0:T(8,128)(2,1)S(1)}, bf16[16,32,128]{2,1,0:T(8,128)(2,1)}, u32[]{:S(2)}) copy-start(bf16[16,32,128]{2,1,0:T(8,128)(2,1)} %refs_0_.10) | copy-start | bytes 393220
  20.2 5.1 %collective-permute-start.1 = (bf16[224,128]{1,0:T(8,128)(2,1)S(1)}, bf16[224,128]{1,0:T(8,128)(2,1)S(1)}, u32[]{:S(2)}, u32[]{:S(2)}) collective-permute-start(bf16[224,128]{1,0:T(8,128)(2,1)S(1)} %get-tuple-element.32), channel_id=1, source_target_pairs={{0,8},{8,0},{16,24},{24,16},{32,40},{40,32},{48,56},{56,48},{1,9},... | collective-permute-start | bytes 172040 | tf_op jit(solution)/shard_map/ppermute | solution.py:412
  22.2 1.7 %copy-start.10 = (f32[256]{0:T(256)S(1)}, f32[256]{0:T(256)}, u32[]{:S(2)}) copy-start(f32[256]{0:T(256)} %param.16) | copy-start | bytes 3076
  22.3 1.7 %copy-start.11 = (f32[32]{0:T(128)S(1)}, f32[32]{0:T(128)}, u32[]{:S(2)}) copy-start(f32[32]{0:T(128)} %param.14) | copy-start | bytes 388
  22.3 1.7 %copy-start.12 = (f32[64]{0:T(128)S(1)}, f32[64]{0:T(128)}, u32[]{:S(2)}) copy-start(f32[64]{0:T(128)} %param.15) | copy-start | bytes 772
  22.5 2.7 %copy-start.3 = (bf16[128,128]{1,0:T(8,128)(2,1)S(1)}, bf16[128,128]{1,0:T(8,128)(2,1)}, u32[]{:S(2)}) copy-start(bf16[128,128]{1,0:T(8,128)(2,1)} %constant.16.clone.refs_7_) | copy-start | bytes 98308
  26.1 11.5 %collective-permute-start.2 = (f32[88,128]{1,0:T(8,128)S(1)}, f32[88,128]{1,0:T(8,128)S(1)}, u32[]{:S(2)}, u32[]{:S(2)}) collective-permute-start(f32[88,128]{1,0:T(8,128)S(1)} %get-tuple-element.38), channel_id=1, source_target_pairs={{1,2},{2,1},{3,4},{4,3},{5,6},{6,5},{7,0},{0,7},{9,10},{10,9},{11,... | collective-permute-start | bytes 135176 | tf_op jit(solution)/shard_map/ppermute | solution.py:430
  31.8 5.9 %collective-permute-start.3 = (f32[88,128]{1,0:T(8,128)S(1)}, f32[88,128]{1,0:T(8,128)S(1)}, u32[]{:S(2)}, u32[]{:S(2)}) collective-permute-start(f32[88,128]{1,0:T(8,128)S(1)} %get-tuple-element.39), channel_id=1, source_target_pairs={{0,1},{1,0},{2,3},{3,2},{4,5},{5,4},{6,7},{7,6},{8,9},{9,8},{10,11... | collective-permute-start | bytes 135176 | tf_op jit(solution)/shard_map/ppermute | solution.py:431
  37.8 5.0 %collective-permute-start.4 = (f32[8,128]{1,0:T(8,128)S(1)}, f32[8,128]{1,0:T(8,128)S(1)}, u32[]{:S(2)}, u32[]{:S(2)}) collective-permute-start(f32[8,128]{1,0:T(8,128)S(1)} %get-tuple-element.40), channel_id=1, source_target_pairs={{0,64},{64,128},{128,192},{192,256},{256,320},{320,384},{384,448},... | collective-permute-start | bytes 12296 | tf_op jit(solution)/shard_map/ppermute | solution.py:407
  42.0 3.0 %collective-permute-start.5 = (f32[8,128]{1,0:T(8,128)S(1)}, f32[8,128]{1,0:T(8,128)S(1)}, u32[]{:S(2)}, u32[]{:S(2)}) collective-permute-start(f32[8,128]{1,0:T(8,128)S(1)} %get-tuple-element.42), channel_id=1, source_target_pairs={{0,448},{64,0},{128,64},{192,128},{256,192},{320,256},{384,320},{4... | collective-permute-start | bytes 12296 | tf_op jit(solution)/shard_map/ppermute | solution.py:407
  45.7 28.1 %all-to-all-start = ((bf16[64,8,128]{2,1,0:T(8,128)(2,1)}), bf16[64,8,128]{2,1,0:T(8,128)(2,1)S(1)}, u32[]{:S(2)}, u32[]{:S(2)}) async-start(bf16[64,8,128]{2,1,0:T(8,128)(2,1)} %bitcast.3), calls=%async_computation | async-start | bytes 262144 | tf_op jit(solution)/shard_map/all_to_all | solution.py:435
  59.1 9.8 %collective-permute-start.8 = (f32[520,128]{1,0:T(8,128)S(1)}, f32[520,128]{1,0:T(8,128)S(1)}, u32[]{:S(2)}, u32[]{:S(2)}) collective-permute-start(f32[520,128]{1,0:T(8,128)S(1)} %get-tuple-element.53), channel_id=1, source_target_pairs={{0,64},{64,128},{128,192},{192,256},{256,320},{320,384},{384,448},... | collective-permute-start | bytes 798728 | tf_op jit(solution)/shard_map/ppermute | solution.py:407
  59.5 9.5 %collective-permute-start.9 = (f32[520,128]{1,0:T(8,128)S(1)}, f32[520,128]{1,0:T(8,128)S(1)}, u32[]{:S(2)}, u32[]{:S(2)}) collective-permute-start(f32[520,128]{1,0:T(8,128)S(1)} %get-tuple-element.54), channel_id=1, source_target_pairs={{0,448},{64,0},{128,64},{192,128},{256,192},{320,256},{384,320},{4... | collective-permute-start | bytes 798728 | tf_op jit(solution)/shard_map/ppermute | solution.py:407
  59.7 6.6 %collective-permute-start.6 = (f32[72,128]{1,0:T(8,128)S(1)}, f32[72,128]{1,0:T(8,128)S(1)}, u32[]{:S(2)}, u32[]{:S(2)}) collective-permute-start(f32[72,128]{1,0:T(8,128)S(1)} %get-tuple-element.51), channel_id=1, source_target_pairs={{0,128},{128,0},{64,192},{192,64},{256,384},{384,256},{320,448},{4... | collective-permute-start | bytes 110600 | tf_op jit(solution)/shard_map/ppermute | solution.py:444
  62.8 6.2 %collective-permute-start.7 = (f32[72,128]{1,0:T(8,128)S(1)}, f32[72,128]{1,0:T(8,128)S(1)}, u32[]{:S(2)}, u32[]{:S(2)}) collective-permute-start(f32[72,128]{1,0:T(8,128)S(1)} %get-tuple-element.52), channel_id=1, source_target_pairs={{128,256},{256,128},{192,320},{320,192},{384,0},{0,384},{448,64},{... | collective-permute-start | bytes 110600 | tf_op jit(solution)/shard_map/ppermute | solution.py:445
  74.4 11.3 %copy-start.4 = (bf16[128,128]{1,0:T(8,128)(2,1)S(1)}, bf16[128,128]{1,0:T(8,128)(2,1)}, u32[]{:S(2)}) copy-start(bf16[128,128]{1,0:T(8,128)(2,1)} %constant.18.clone.refs_5_) | copy-start | bytes 98308
  74.4 11.3 %copy-start.5 = (bf16[128,128]{1,0:T(8,128)(2,1)S(1)}, bf16[128,128]{1,0:T(8,128)(2,1)}, u32[]{:S(2)}) copy-start(bf16[128,128]{1,0:T(8,128)(2,1)} %constant.20.clone.refs_7_) | copy-start | bytes 98308
  74.4 11.3 %copy-start.7 = (bf16[32,24]{1,0:T(8,128)(2,1)S(1)}, bf16[32,24]{1,0:T(8,128)(2,1)}, u32[]{:S(2)}) copy-start(bf16[32,24]{1,0:T(8,128)(2,1)} %constant.19.clone.refs_6_) | copy-start | bytes 4612
  74.4 11.3 %copy-start.8 = (bf16[24,16]{1,0:T(8,128)(2,1)S(1)}, bf16[24,16]{1,0:T(8,128)(2,1)}, u32[]{:S(2)}) copy-start(bf16[24,16]{1,0:T(8,128)(2,1)} %constant.17.clone.refs_4_) | copy-start | bytes 2308

commit v7 on v6

--- a/solution.py
+++ b/solution.py
@@ -245,7 +245,16 @@
             more = pltpu.roll(more + pltpu.roll(more, 124, 1), 64, 1)
             stack.append(jnp.where(lane < 64, body + pltpu.roll(body, 64, 1), jnp.where(lane < 67, more, 0.0)))
         columns.append(jnp.concatenate(stack, axis=0))
-    done = dot(my2[...], lanes(columns))
+    wide = lanes(columns)
+    data = split(wide, 3)
+    first = my2[...].astype(bf16)
+    rest = (my2[...] - first.astype(f32)).astype(bf16)
+    both = jnp.dot(
+        jnp.concatenate([first.astype(f32), rest.astype(f32)], axis=0).astype(bf16), data[0], preferred_element_type=f32
+    )
+    done = both[0:32] + both[32:64]
+    for term in data[1:]:
+        done = done + jnp.dot(first, term, preferred_element_type=f32)
     parts2 = [done[0:24, 128 * j : 128 * j + 128] for j in range(11)]
     half = {j - 1: done[24:32, 128 * j : 128 * j + 128] for j in range(11)}
     rows = [sum(w * half[2 * j + d] for d, w in weight.items() if 2 * j + d in half) for j in range(-2, 7)]
@@ -320,7 +329,7 @@
     to_even[...], to_odd[...] = choose(odd_chip, done2[0:72], done2[192:264])
 
 
-def near_x_step(taps, n1, n2, even2, odd2, low, high, n1_out, n2_out):
+def near_x_step(taps, n1, n2, even2, odd2, high, low, n1_out, n2_out):
     odd_chip = lax.rem(lax.axis_index("gx") // 2, 2) == 1
     low2 = jnp.where(odd_chip, even2[...], odd2[...])
     high2 = jnp.where(odd_chip, odd2[...], even2[...])
@@ -431,7 +440,7 @@
     from_even = lax.ppermute(to_even, "gz", swap_even)
 
     q3, to_low, to_high = call(q3_z_step, [((8, 128), f32)] * 3, [q3, from_odd, from_even])
-    (message,) = call(q3_x_step, [((32, 16, 128), bf16)], [shift(to_high, 1), q3, shift(to_low, -1)])
+    (message,) = call(q3_x_step, [((32, 16, 128), bf16)], [shift(to_low, -1), q3, shift(to_high, 1)])
     gathered = lax.all_to_all(
         message.reshape(64, 8, 128), ("gy", "gz"), split_axis=0, concat_axis=0, tiled=True
     )
@@ -443,8 +452,8 @@
     halos = [
         lax.ppermute(to_even, "gx", [(0, 2), (2, 0), (1, 3), (3, 1), (4, 6), (6, 4), (5, 7), (7, 5)]),
         lax.ppermute(to_odd, "gx", [(2, 4), (4, 2), (3, 5), (5, 3), (6, 0), (0, 6), (7, 1), (1, 7)]),
+        shift(to_low, -1),
         shift(to_high, 1),
-        shift(to_low, -1),
     ]
     n1, n2 = call(
         near_x_step, [((16, 32, 128), f32), ((11, 24, 128), f32)],

time: 87.8 us -> 86.7 us (0.987)
  waiting for transfers between devices: 14 us -> 8.98 us
  starting transfers between devices: 52.2 us -> 54.9 us
  blocking collectives: 11.2 us -> 12.5 us
    ppermute x4, starting transfers between devices: 4.72 us -> 7.59 us  [shift(): return lax.ppermute(block, 'gx', [(i, (i + by) % 8) for i in range(8)])]
    all_to_all x1, waiting for transfers between devices: 3.85 us -> 1.68 us  [per_device(): lax.all_to_all(message.reshape(64, 8, 128), ('gy', 'gz'), split_axis=0, c...]
    ppermute x4, waiting for transfers between devices: 3.03 us -> 1.29 us  [shift(): return lax.ppermute(block, 'gx', [(i, (i + by) % 8) for i in range(8)])]
    all_to_all x1, blocking collectives: 11.2 us -> 12.5 us  [per_device(): top = lax.all_to_all(message, 'gx', split_axis=0, concat_axis=0, tiled=True)]
    ppermute x1, starting transfers between devices: 3.11 us -> 1.91 us  [per_device(): lax.ppermute(to_even, 'gx', [(0, 2), (2, 0), (1, 3), (3, 1), (4, 6), (6,...]
    ppermute x1, starting transfers between devices: 3.43 us -> 4.49 us  [per_device(): lax.ppermute(to_odd, 'gx', [(2, 4), (4, 2), (3, 5), (5, 3), (6, 0), (0, 6...]
    ppermute x1, waiting for transfers between devices: 2.76 us -> 1.7 us  [per_device(): lax.ppermute(to_odd, 'gx', [(2, 4), (4, 2), (3, 5), (5, 3), (6, 0), (0, 6...]
  transfers between devices with their start and end apart: 11 -> 11, of which waited for: 6 -> 5; matrix products, arithmetic and copies ran while one was open for 0% -> 0% of each run, Pallas kernels for 5% -> 5%
where the time goes in v7:
time: 86.7 us; the launch traced here: 86.3 us
  starting transfers between devices  54.9 us (63%)
  blocking collectives  12.5 us (14%)
  waiting for transfers between devices  8.98 us (10%)
  Pallas kernels  8.67 us (10%)
  local copies, waits for them, and re-layouts  0.98 us (1%)
    ppermute x1, starting transfers between devices, per_device(): from_odd = lax.ppermute(to_odd, 'gy', swap_odd)  18.7 us
    all_to_all x1, starting transfers between devices, per_device(): lax.all_to_all(message.reshape(64, 8, 128), ('gy', 'gz'), split_axis=0, c...  12.5 us
    all_to_all x1, blocking collectives, per_device(): top = lax.all_to_all(message, 'gx', split_axis=0, concat_axis=0, tiled=True)  12.5 us
    pallas_call x12, Pallas kernels, call(): pl.pallas_call(kernel, out_shape=[jax.ShapeDtypeStruct(s, d) for s, d in...  8.67 us
    ppermute x4, starting transfers between devices, shift(): return lax.ppermute(block, 'gx', [(i, (i + by) % 8) for i in range(8)])  7.59 us
    ppermute x1, starting transfers between devices, per_device(): from_odd = lax.ppermute(to_odd, 'gz', swap_odd)  5.67 us
    ppermute x1, starting transfers between devices, per_device(): lax.ppermute(to_odd, 'gx', [(2, 4), (4, 2), (3, 5), (5, 3), (6, 0), (0, 6...  4.49 us
    ppermute x1, waiting for transfers between devices, per_device(): from_odd = lax.ppermute(to_odd, 'gz', swap_odd)  3.94 us
  transfers between devices with their start and end apart: 11, of which 5 were waited for; matrix products, arithmetic and copies ran while one was open for 0% of the time, Pallas kernels for 5%

profile of v7, /device:TPU:1, one launch (start us, length us, event | category | flops | bytes accessed | tf_op | source)
XLA Modules:
  0.0 86.3 jit_solution(14341246360877378572)
XLA Ops:
  0.0 0.0 copy-start
  0.0 0.9 %copy-done = bf16[16,32,128]{2,1,0:T(8,128)(2,1)S(1)} copy-done((bf16[16,32,128]{2,1,0:T(8,128)(2,1)S(1)}, bf16[16,32,128]{2,1,0:T(8,128)(2,1)}, u32[]{:S(2)}) %copy-start) | copy-done | bytes 131096
  0.9 0.0 copy-start.2
  0.9 0.5 y_send.1
  1.4 18.7 %collective-permute-start = (bf16[224,128]{1,0:T(8,128)(2,1)S(1)}, bf16[224,128]{1,0:T(8,128)(2,1)S(1)}, u32[]{:S(2)}, u32[]{:S(2)}) collective-permute-start(bf16[224,128]{1,0:T(8,128)(2,1)S(1)} %get-tuple-element.31.refs_2_), channel_id=1, source_target_pairs={{8,16},{16,8},{24,32},{32,24},{40,48},{48,40},{56,0},{0,56},{9,17}... | collective-permute-start | bytes 172040 | tf_op jit(solution)/shard_map/ppermute | solution.py:420
  20.1 0.0 copy-start.9
  20.1 0.0 copy-start.6
  20.2 0.0 copy-start.1
  20.2 2.1 %collective-permute-start.1 = (bf16[224,128]{1,0:T(8,128)(2,1)S(1)}, bf16[224,128]{1,0:T(8,128)(2,1)S(1)}, u32[]{:S(2)}, u32[]{:S(2)}) collective-permute-start(bf16[224,128]{1,0:T(8,128)(2,1)S(1)} %get-tuple-element.32), channel_id=1, source_target_pairs={{0,8},{8,0},{16,24},{24,16},{32,40},{40,32},{48,56},{56,48},{1,9},... | collective-permute-start | bytes 172040 | tf_op jit(solution)/shard_map/ppermute | solution.py:421
  22.2 0.0 copy-done.2
  22.2 0.0 copy-start.10
  22.3 0.0 copy-start.11
  22.3 0.0 copy-start.12
  22.3 0.2 own_step.1.refs_3_
  22.5 0.0 copy-done.9
  22.5 0.0 copy-start.3
  22.5 0.7 prep_z.1
  23.2 0.0 copy-done.6
  23.3 0.7 prep_y.1
  24.0 0.0 copy-done.10
  24.0 0.0 copy-done.11
  24.0 0.0 copy-done.12
  24.0 0.8 prep_top.1
  24.9 0.0 collective-permute-done.refs_1_
  24.9 0.4 collective-permute-done.1.refs_2_
  25.2 0.0 copy-done.1
  25.2 0.0 copy-done.3
  25.2 0.8 y_step.1
  26.1 5.7 %collective-permute-start.2 = (f32[88,128]{1,0:T(8,128)S(1)}, f32[88,128]{1,0:T(8,128)S(1)}, u32[]{:S(2)}, u32[]{:S(2)}) collective-permute-start(f32[88,128]{1,0:T(8,128)S(1)} %get-tuple-element.38), channel_id=1, source_target_pairs={{1,2},{2,1},{3,4},{4,3},{5,6},{6,5},{7,0},{0,7},{9,10},{10,9},{11,... | collective-permute-start | bytes 135176 | tf_op jit(solution)/shard_map/ppermute | solution.py:439
  31.8 1.9 %collective-permute-start.3 = (f32[88,128]{1,0:T(8,128)S(1)}, f32[88,128]{1,0:T(8,128)S(1)}, u32[]{:S(2)}, u32[]{:S(2)}) collective-permute-start(f32[88,128]{1,0:T(8,128)S(1)} %get-tuple-element.39), channel_id=1, source_target_pairs={{0,1},{1,0},{2,3},{3,2},{4,5},{5,4},{6,7},{7,6},{8,9},{9,8},{10,11... | collective-permute-start | bytes 135176 | tf_op jit(solution)/shard_map/ppermute | solution.py:440
  33.7 3.9 %collective-permute-done.2.refs_1_.refs_2_ = f32[88,128]{1,0:T(8,128)S(1)} collective-permute-done((f32[88,128]{1,0:T(8,128)S(1)}, f32[88,128]{1,0:T(8,128)S(1)}, u32[]{:S(2)}, u32[]{:S(2)}) %collective-permute-start.2) | collective-permute-done | bytes 45088 | tf_op jit(solution)/shard_map/ppermute | solution.py:439
  37.6 0.0 collective-permute-done.3.refs_2_.refs_3_
  37.6 0.2 q3_z_step.1
  37.8 3.1 %collective-permute-start.4 = (f32[8,128]{1,0:T(8,128)S(1)}, f32[8,128]{1,0:T(8,128)S(1)}, u32[]{:S(2)}, u32[]{:S(2)}) collective-permute-start(f32[8,128]{1,0:T(8,128)S(1)} %get-tuple-element.40), channel_id=1, source_target_pairs={{0,448},{64,0},{128,64},{192,128},{256,192},{320,256},{384,320},{4... | collective-permute-start | bytes 12296 | tf_op jit(solution)/shard_map/ppermute | solution.py:416
  40.9 1.1 %collective-permute-start.5 = (f32[8,128]{1,0:T(8,128)S(1)}, f32[8,128]{1,0:T(8,128)S(1)}, u32[]{:S(2)}, u32[]{:S(2)}) collective-permute-start(f32[8,128]{1,0:T(8,128)S(1)} %get-tuple-element.42), channel_id=1, source_target_pairs={{0,64},{64,128},{128,192},{192,256},{256,320},{320,384},{384,448},... | collective-permute-start | bytes 12296 | tf_op jit(solution)/shard_map/ppermute | solution.py:416
  42.0 1.3 %collective-permute-done.4.refs_0_ = f32[8,128]{1,0:T(8,128)S(1)} collective-permute-done((f32[8,128]{1,0:T(8,128)S(1)}, f32[8,128]{1,0:T(8,128)S(1)}, u32[]{:S(2)}, u32[]{:S(2)}) %collective-permute-start.4) | collective-permute-done | bytes 4128 | tf_op jit(solution)/shard_map/ppermute | solution.py:416
  43.3 0.0 collective-permute-done.5.refs_2_
  43.3 0.7 q3_x_step.1.refs_6_
  44.0 12.5 %all-to-all-start = ((bf16[64,8,128]{2,1,0:T(8,128)(2,1)}), bf16[64,8,128]{2,1,0:T(8,128)(2,1)S(1)}, u32[]{:S(2)}, u32[]{:S(2)}) async-start(bf16[64,8,128]{2,1,0:T(8,128)(2,1)} %bitcast.3), calls=%async_computation | async-start | bytes 262144 | tf_op jit(solution)/shard_map/all_to_all | solution.py:444
  56.5 0.9 near_z_step.1
  57.4 3.4 %collective-permute-start.8 = (f32[520,128]{1,0:T(8,128)S(1)}, f32[520,128]{1,0:T(8,128)S(1)}, u32[]{:S(2)}, u32[]{:S(2)}) collective-permute-start(f32[520,128]{1,0:T(8,128)S(1)} %get-tuple-element.53), channel_id=1, source_target_pairs={{0,448},{64,0},{128,64},{192,128},{256,192},{320,256},{384,320},{4... | collective-permute-start | bytes 798728 | tf_op jit(solution)/shard_map/ppermute | solution.py:416
  60.7 0.0 collective-permute-start.9
  60.7 1.9 %collective-permute-start.6 = (f32[72,128]{1,0:T(8,128)S(1)}, f32[72,128]{1,0:T(8,128)S(1)}, u32[]{:S(2)}, u32[]{:S(2)}) collective-permute-start(f32[72,128]{1,0:T(8,128)S(1)} %get-tuple-element.51), channel_id=1, source_target_pairs={{0,128},{128,0},{64,192},{192,64},{256,384},{384,256},{320,448},{4... | collective-permute-start | bytes 110600 | tf_op jit(solution)/shard_map/ppermute | solution.py:453
  62.7 4.5 %collective-permute-start.7 = (f32[72,128]{1,0:T(8,128)S(1)}, f32[72,128]{1,0:T(8,128)S(1)}, u32[]{:S(2)}, u32[]{:S(2)}) collective-permute-start(f32[72,128]{1,0:T(8,128)S(1)} %get-tuple-element.52), channel_id=1, source_target_pairs={{128,256},{256,128},{192,320},{320,192},{384,0},{0,384},{448,64},{... | collective-permute-start | bytes 110600 | tf_op jit(solution)/shard_map/ppermute | solution.py:454
  67.2 0.0 collective-permute-done.6.refs_3_
  67.2 1.7 %collective-permute-done.7.refs_4_ = f32[72,128]{1,0:T(8,128)S(1)} collective-permute-done((f32[72,128]{1,0:T(8,128)S(1)}, f32[72,128]{1,0:T(8,128)S(1)}, u32[]{:S(2)}, u32[]{:S(2)}) %collective-permute-start.7) | collective-permute-done | bytes 36896 | tf_op jit(solution)/shard_map/ppermute | solution.py:454
  68.9 0.0 collective-permute-done.8.refs_5_
  68.9 0.0 collective-permute-done.9.refs_6_
  68.9 1.0 %near_x_step.1 = (f32[16,32,128]{2,1,0:T(8,128)S(1)}, f32[11,24,128]{2,1,0:T(8,128)S(1)}) custom-call(f32[2,17]{1,0:T(2,128)S(1)} %copy-done.9, f32[16,32,128]{2,1,0:T(8,128)S(1)} %get-tuple-element.49.refs_1_, f32[11,24,128]{2,1,0:T(8,128)S(1)} %get-tuple-element.50.refs_2_, f32[72,128]{1,0:T(8,128)S(1)} %collective-permute-done.6.refs_3_, ...), custom_call_target="tpu_custom_call" | custom-call | flops 1000000 | bytes 1000000 | tf_op jit(solution)/shard_map/near_x_step/pallas_call | solution.py:96
  69.9 1.7 %all-to-all-done.refs_0_ = bf16[64,8,128]{2,1,0:T(8,128)(2,1)S(1)} async-done(((bf16[64,8,128]{2,1,0:T(8,128)(2,1)}), bf16[64,8,128]{2,1,0:T(8,128)(2,1)S(1)}, u32[]{:S(2)}, u32[]{:S(2)}) %all-to-all-start) | async-done | bytes 131104 | tf_op jit(solution)/shard_map/all_to_all | solution.py:444
  71.6 0.5 top_step.1
  72.1 0.0 copy-start.4
  72.1 0.0 copy-start.5
  72.1 0.0 copy-start.7
  72.1 0.0 copy-start.8
  72.1 12.5 %all_to_all.10.refs_0_ = f32[8,16,128]{2,1,0:T(8,128)S(1)} all-to-all(f32[8,16,128]{2,1,0:T(8,128)S(1)} %top_step.1), channel_id=1, replica_groups=mesh['gx'=8,'gy'=8,'gz'=8] {'gx'}, dimensions={0} | all-to-all | bytes 131072 | tf_op jit(solution)/shard_map/all_to_all | solution.py:463
  84.6 0.0 copy-done.4
  84.6 0.0 copy-done.5
  84.6 0.0 copy-done.7
  84.6 0.0 copy-done.8
  84.6 1.6 %last_step.1 = f32[16,32,128]{2,1,0:T(8,128)} custom-call(f32[8,16,128]{2,1,0:T(8,128)S(1)} %all_to_all.10.refs_0_, f32[16,1024]{1,0:T(8,128)S(1)} %get-tuple-element.36.refs_9_.refs_1_, f32[16,32,128]{2,1,0:T(8,128)S(1)} %get-tuple-element.55.refs_4_.refs_2_, f32[11,24,128]{2,1,0:T(8,128)S(1)} %get-tuple-element.56.refs_3_, bf16[24,16]{1,0:T(8,128)(2,1)S(1)} %copy-done.8, ...), custom_call_target="tpu_custom_call" | custom-call | flops 1000000 | bytes 1000000 | tf_op jit(solution)/shard_map/last_step/pallas_call | solution.py:96
Async XLA Ops:
  0.0 0.9 %copy-start = (bf16[16,32,128]{2,1,0:T(8,128)(2,1)S(1)}, bf16[16,32,128]{2,1,0:T(8,128)(2,1)}, u32[]{:S(2)}) copy-start(bf16[16,32,128]{2,1,0:T(8,128)(2,1)} %refs_0_.10) | copy-start | bytes 393220
  0.9 21.3 %copy-start.2 = (bf16[128,128]{1,0:T(8,128)(2,1)S(1)}, bf16[128,128]{1,0:T(8,128)(2,1)}, u32[]{:S(2)}) copy-start(bf16[128,128]{1,0:T(8,128)(2,1)} %constant.14.clone.refs_1_.refs_6_) | copy-start | bytes 98308
  1.4 23.5 %collective-permute-start = (bf16[224,128]{1,0:T(8,128)(2,1)S(1)}, bf16[224,128]{1,0:T(8,128)(2,1)S(1)}, u32[]{:S(2)}, u32[]{:S(2)}) collective-permute-start(bf16[224,128]{1,0:T(8,128)(2,1)S(1)} %get-tuple-element.31.refs_2_), channel_id=1, source_target_pairs={{8,16},{16,8},{24,32},{32,24},{40,48},{48,40},{56,0},{0,56},{9,17}... | collective-permute-start | bytes 172040 | tf_op jit(solution)/shard_map/ppermute | solution.py:420
  20.1 2.4 %copy-start.9 = (f32[2,17]{1,0:T(2,128)S(1)}, f32[2,17]{1,0:T(2,128)}, u32[]{:S(2)}) copy-start(f32[2,17]{1,0:T(2,128)} %refs_0_.11) | copy-start | bytes 412
  20.1 3.1 %copy-start.6 = (f32[40,64]{1,0:T(8,128)S(1)}, f32[40,64]{1,0:T(8,128)}, u32[]{:S(2)}) copy-start(f32[40,64]{1,0:T(8,128)} %constant.15.clone.refs_1_) | copy-start | bytes 30724
  20.2 5.1 %copy-start.1 = (bf16[16,32,128]{2,1,0:T(8,128)(2,1)S(1)}, bf16[16,32,128]{2,1,0:T(8,128)(2,1)}, u32[]{:S(2)}) copy-start(bf16[16,32,128]{2,1,0:T(8,128)(2,1)} %refs_0_.10) | copy-start | bytes 393220
  20.2 5.1 %collective-permute-start.1 = (bf16[224,128]{1,0:T(8,128)(2,1)S(1)}, bf16[224,128]{1,0:T(8,128)(2,1)S(1)}, u32[]{:S(2)}, u32[]{:S(2)}) collective-permute-start(bf16[224,128]{1,0:T(8,128)(2,1)S(1)} %get-tuple-element.32), channel_id=1, source_target_pairs={{0,8},{8,0},{16,24},{24,16},{32,40},{40,32},{48,56},{56,48},{1,9},... | collective-permute-start | bytes 172040 | tf_op jit(solution)/shard_map/ppermute | solution.py:421
  22.2 1.7 %copy-start.10 = (f32[256]{0:T(256)S(1)}, f32[256]{0:T(256)}, u32[]{:S(2)}) copy-start(f32[256]{0:T(256)} %param.16) | copy-start | bytes 3076
  22.3 1.7 %copy-start.11 = (f32[32]{0:T(128)S(1)}, f32[32]{0:T(128)}, u32[]{:S(2)}) copy-start(f32[32]{0:T(128)} %param.14) | copy-start | bytes 388
  22.3 1.7 %copy-start.12 = (f32[64]{0:T(128)S(1)}, f32[64]{0:T(128)}, u32[]{:S(2)}) copy-start(f32[64]{0:T(128)} %param.15) | copy-start | bytes 772
  22.5 2.7 %copy-start.3 = (bf16[128,128]{1,0:T(8,128)(2,1)S(1)}, bf16[128,128]{1,0:T(8,128)(2,1)}, u32[]{:S(2)}) copy-start(bf16[128,128]{1,0:T(8,128)(2,1)} %constant.16.clone.refs_7_) | copy-start | bytes 98308
  26.1 11.5 %collective-permute-start.2 = (f32[88,128]{1,0:T(8,128)S(1)}, f32[88,128]{1,0:T(8,128)S(1)}, u32[]{:S(2)}, u32[]{:S(2)}) collective-permute-start(f32[88,128]{1,0:T(8,128)S(1)} %get-tuple-element.38), channel_id=1, source_target_pairs={{1,2},{2,1},{3,4},{4,3},{5,6},{6,5},{7,0},{0,7},{9,10},{10,9},{11,... | collective-permute-start | bytes 135176 | tf_op jit(solution)/shard_map/ppermute | solution.py:439
  31.8 5.9 %collective-permute-start.3 = (f32[88,128]{1,0:T(8,128)S(1)}, f32[88,128]{1,0:T(8,128)S(1)}, u32[]{:S(2)}, u32[]{:S(2)}) collective-permute-start(f32[88,128]{1,0:T(8,128)S(1)} %get-tuple-element.39), channel_id=1, source_target_pairs={{0,1},{1,0},{2,3},{3,2},{4,5},{5,4},{6,7},{7,6},{8,9},{9,8},{10,11... | collective-permute-start | bytes 135176 | tf_op jit(solution)/shard_map/ppermute | solution.py:440
  37.8 5.5 %collective-permute-start.4 = (f32[8,128]{1,0:T(8,128)S(1)}, f32[8,128]{1,0:T(8,128)S(1)}, u32[]{:S(2)}, u32[]{:S(2)}) collective-permute-start(f32[8,128]{1,0:T(8,128)S(1)} %get-tuple-element.40), channel_id=1, source_target_pairs={{0,448},{64,0},{128,64},{192,128},{256,192},{320,256},{384,320},{4... | collective-permute-start | bytes 12296 | tf_op jit(solution)/shard_map/ppermute | solution.py:416
  40.9 2.4 %collective-permute-start.5 = (f32[8,128]{1,0:T(8,128)S(1)}, f32[8,128]{1,0:T(8,128)S(1)}, u32[]{:S(2)}, u32[]{:S(2)}) collective-permute-start(f32[8,128]{1,0:T(8,128)S(1)} %get-tuple-element.42), channel_id=1, source_target_pairs={{0,64},{64,128},{128,192},{192,256},{256,320},{320,384},{384,448},... | collective-permute-start | bytes 12296 | tf_op jit(solution)/shard_map/ppermute | solution.py:416
  44.0 27.6 %all-to-all-start = ((bf16[64,8,128]{2,1,0:T(8,128)(2,1)}), bf16[64,8,128]{2,1,0:T(8,128)(2,1)S(1)}, u32[]{:S(2)}, u32[]{:S(2)}) async-start(bf16[64,8,128]{2,1,0:T(8,128)(2,1)} %bitcast.3), calls=%async_computation | async-start | bytes 262144 | tf_op jit(solution)/shard_map/all_to_all | solution.py:444
  57.4 11.5 %collective-permute-start.8 = (f32[520,128]{1,0:T(8,128)S(1)}, f32[520,128]{1,0:T(8,128)S(1)}, u32[]{:S(2)}, u32[]{:S(2)}) collective-permute-start(f32[520,128]{1,0:T(8,128)S(1)} %get-tuple-element.53), channel_id=1, source_target_pairs={{0,448},{64,0},{128,64},{192,128},{256,192},{320,256},{384,320},{4... | collective-permute-start | bytes 798728 | tf_op jit(solution)/shard_map/ppermute | solution.py:416
  60.7 8.1 %collective-permute-start.9 = (f32[520,128]{1,0:T(8,128)S(1)}, f32[520,128]{1,0:T(8,128)S(1)}, u32[]{:S(2)}, u32[]{:S(2)}) collective-permute-start(f32[520,128]{1,0:T(8,128)S(1)} %get-tuple-element.54), channel_id=1, source_target_pairs={{0,64},{64,128},{128,192},{192,256},{256,320},{320,384},{384,448},... | collective-permute-start | bytes 798728 | tf_op jit(solution)/shard_map/ppermute | solution.py:416
  60.7 6.4 %collective-permute-start.6 = (f32[72,128]{1,0:T(8,128)S(1)}, f32[72,128]{1,0:T(8,128)S(1)}, u32[]{:S(2)}, u32[]{:S(2)}) collective-permute-start(f32[72,128]{1,0:T(8,128)S(1)} %get-tuple-element.51), channel_id=1, source_target_pairs={{0,128},{128,0},{64,192},{192,64},{256,384},{384,256},{320,448},{4... | collective-permute-start | bytes 110600 | tf_op jit(solution)/shard_map/ppermute | solution.py:453
  62.7 6.2 %collective-permute-start.7 = (f32[72,128]{1,0:T(8,128)S(1)}, f32[72,128]{1,0:T(8,128)S(1)}, u32[]{:S(2)}, u32[]{:S(2)}) collective-permute-start(f32[72,128]{1,0:T(8,128)S(1)} %get-tuple-element.52), channel_id=1, source_target_pairs={{128,256},{256,128},{192,320},{320,192},{384,0},{0,384},{448,64},{... | collective-permute-start | bytes 110600 | tf_op jit(solution)/shard_map/ppermute | solution.py:454
  72.1 12.5 %copy-start.4 = (bf16[128,128]{1,0:T(8,128)(2,1)S(1)}, bf16[128,128]{1,0:T(8,128)(2,1)}, u32[]{:S(2)}) copy-start(bf16[128,128]{1,0:T(8,128)(2,1)} %constant.18.clone.refs_5_) | copy-start | bytes 98308
  72.1 12.5 %copy-start.5 = (bf16[128,128]{1,0:T(8,128)(2,1)S(1)}, bf16[128,128]{1,0:T(8,128)(2,1)}, u32[]{:S(2)}) copy-start(bf16[128,128]{1,0:T(8,128)(2,1)} %constant.20.clone.refs_7_) | copy-start | bytes 98308
  72.1 12.5 %copy-start.7 = (bf16[32,24]{1,0:T(8,128)(2,1)S(1)}, bf16[32,24]{1,0:T(8,128)(2,1)}, u32[]{:S(2)}) copy-start(bf16[32,24]{1,0:T(8,128)(2,1)} %constant.19.clone.refs_6_) | copy-start | bytes 4612
  72.1 12.5 %copy-start.8 = (bf16[24,16]{1,0:T(8,128)(2,1)S(1)}, bf16[24,16]{1,0:T(8,128)(2,1)}, u32[]{:S(2)}) copy-start(bf16[24,16]{1,0:T(8,128)(2,1)} %constant.17.clone.refs_4_) | copy-start | bytes 2308

commit v8 on v7

--- a/solution.py
+++ b/solution.py
@@ -58,6 +58,9 @@
 )
 y_raise = table(32, 24, lambda r, c: weight.get(r - 2 * (c - 1), 0.0) if c < 19 else 0.0)
 z_raise = table(128, 128, lambda r, c: weight.get(c - 2 * (r - 1), 0.0) if r < 67 else 0.0)
+
+y_raise_both = y_raise @ y_raise_top
+z_raise_both = z_raise_top @ z_raise
 
 
 def dot(a, b):
@@ -329,7 +332,7 @@
     to_even[...], to_odd[...] = choose(odd_chip, done2[0:72], done2[192:264])
 
 
-def near_x_step(taps, n1, n2, even2, odd2, high, low, n1_out, n2_out):
+def near_x_step(taps, n1, n2, even2, odd2, high, low, y2, z2, out):
     odd_chip = lax.rem(lax.axis_index("gx") // 2, 2) == 1
     low2 = jnp.where(odd_chip, even2[...], odd2[...])
     high2 = jnp.where(odd_chip, odd2[...], even2[...])
@@ -344,7 +347,8 @@
             total = taps[0, 0] * f[i - 8]
             for a in range(-7, 9):
                 total = total + taps[0, a + 8] * f[i + a]
-            n1_out[i, 8 * t : 8 * t + 8] = total
+            out[i, 8 * t : 8 * t + 8] = total
+    tiles = {}
     for t in range(3):
         half = {}
         for j in range(-1, 10):
@@ -359,7 +363,13 @@
             total = taps[1, 0] * half[i - 8]
             for a in range(-7, 9):
                 total = total + taps[1, a + 8] * half[i + a]
-            n2_out[i + 1, 8 * t : 8 * t + 8] = total
+            tiles[i, t] = total
+    tall = jnp.concatenate([tiles[i, t] for i in range(-1, 10) for t in range(3)], axis=0)
+    tall = from_right(tall, z2)
+    wide = from_left(y2, lanes([tall[24 * i : 24 * i + 24] for i in range(11)]))
+    rows = raise_rows({i - 1: wide[:, 128 * i : 128 * i + 128] for i in range(11)}, 0, 15)
+    for i in range(16):
+        out[i] = out[i] + rows[i]
 
 
 def top_step(gathered, wz1, wz2, my, out):
@@ -387,7 +397,7 @@
     return out
 
 
-def last_step(top, wx, n1, n2, y1, z1, y2, z2, out):
+def last_step(top, wx, near, y_both, z_both, out):
     e3 = {}
     row, lane = iota((16, 128), 0), iota((16, 128), 1)
     here = (lane >= 32) & (lane < 57) & (lane % 32 // 5 == row % 5)
@@ -400,15 +410,12 @@
         total = total + pltpu.roll(total, 32, 1)
         past = jnp.where(row < 5, total[13:14], jnp.where(row < 10, total[14:15], total[15:16]))
         e3[i - 2] = jnp.where(lane < 32, total, jnp.where(here, past, 0.0))
-    e2 = raise_rows(e3, -1, 9)
-    wide = from_left(y1, lanes([e2[i] for i in range(-1, 10)]))
-    tall = jnp.concatenate([wide[:, 128 * i : 128 * i + 128] for i in range(11)], axis=0)
-    tall = from_right(tall, z1) + n2[...].reshape(264, 128)
-    tall = from_right(tall, z2)
-    wide = from_left(y2, lanes([tall[24 * i : 24 * i + 24] for i in range(11)]))
-    rows = raise_rows({i - 1: wide[:, 128 * i : 128 * i + 128] for i in range(11)}, 0, 15)
+    tall = from_right(jnp.concatenate([e3[i] for i in range(-2, 7)], axis=0), z_both)
+    wide = from_left(y_both, lanes([tall[16 * i : 16 * i + 16] for i in range(9)]))
+    rows = raise_rows({i - 2: wide[:, 128 * i : 128 * i + 128] for i in range(9)}, -1, 9)
+    rows = raise_rows(rows, 0, 15)
     for i in range(16):
-        out[i] = rows[i] + n1[i]
+        out[i] = rows[i] + near[i]
 
 
 def per_device(charge, kernel_taps, top_x, top_y, top_z):
@@ -455,15 +462,15 @@
         shift(to_low, -1),
         shift(to_high, 1),
     ]
-    n1, n2 = call(
-        near_x_step, [((16, 32, 128), f32), ((11, 24, 128), f32)],
-        [kernel_taps, n1, n2, *halos], smem=(0,),
-    )
-    (message,) = call(top_step, [((8, 16, 128), f32)], [gathered, wz1, wz2, ty], after=[n1])
+    (near,) = call(
+        near_x_step, [((16, 32, 128), f32)],
+        [kernel_taps, n1, n2, *halos, jnp.asarray(y_raise, bf16), jnp.asarray(z_raise, bf16)], smem=(0,),
+    )
+    (message,) = call(top_step, [((8, 16, 128), f32)], [gathered, wz1, wz2, ty], after=[near])
     top = lax.all_to_all(message, "gx", split_axis=0, concat_axis=0, tiled=True)
     (result,) = call(
         last_step, [((16, 32, 128), f32)],
-        [top, wx, n1, n2, *(jnp.asarray(m, bf16) for m in (y_raise_top, z_raise_top, y_raise, z_raise))],
+        [top, wx, near, jnp.asarray(y_raise_both, bf16), jnp.asarray(z_raise_both, bf16)],
     )
     return result
 

time: 86.7 us -> 86.2 us (level)
  no operation moved by 1% of the time
where the time goes in v8:
time: 86.2 us; the launch traced here: 85.7 us
  starting transfers between devices  54.9 us (64%)
  blocking collectives  12.4 us (14%)
  waiting for transfers between devices  8.69 us (10%)
  Pallas kernels  8.54 us (10%)
  local copies, waits for them, and re-layouts  0.98 us (1%)
    ppermute x1, starting transfers between devices, per_device(): from_odd = lax.ppermute(to_odd, 'gy', swap_odd)  18.7 us
    all_to_all x1, starting transfers between devices, per_device(): lax.all_to_all(message.reshape(64, 8, 128), ('gy', 'gz'), split_axis=0, c...  12.5 us
    all_to_all x1, blocking collectives, per_device(): top = lax.all_to_all(message, 'gx', split_axis=0, concat_axis=0, tiled=True)  12.4 us
    pallas_call x12, Pallas kernels, call(): pl.pallas_call(kernel, out_shape=[jax.ShapeDtypeStruct(s, d) for s, d in...  8.54 us
    ppermute x4, starting transfers between devices, shift(): return lax.ppermute(block, 'gx', [(i, (i + by) % 8) for i in range(8)])  7.59 us
    ppermute x1, starting transfers between devices, per_device(): from_odd = lax.ppermute(to_odd, 'gz', swap_odd)  5.67 us
    ppermute x1, starting transfers between devices, per_device(): lax.ppermute(to_odd, 'gx', [(2, 4), (4, 2), (3, 5), (5, 3), (6, 0), (0, 6...  4.49 us
    ppermute x1, waiting for transfers between devices, per_device(): from_odd = lax.ppermute(to_odd, 'gz', swap_odd)  3.94 us
  transfers between devices with their start and end apart: 11, of which 5 were waited for; matrix products, arithmetic and copies ran while one was open for 0% of the time, Pallas kernels for 5%

profile of v8, /device:TPU:1, one launch (start us, length us, event | category | flops | bytes accessed | tf_op | source)
XLA Modules:
  0.0 85.7 jit_solution(11688968808560883605)
XLA Ops:
  0.0 0.0 copy-start
  0.0 0.9 %copy-done = bf16[16,32,128]{2,1,0:T(8,128)(2,1)S(1)} copy-done((bf16[16,32,128]{2,1,0:T(8,128)(2,1)S(1)}, bf16[16,32,128]{2,1,0:T(8,128)(2,1)}, u32[]{:S(2)}) %copy-start) | copy-done | bytes 131096
  0.9 0.0 copy-start.2
  0.9 0.5 y_send.1
  1.4 18.7 %collective-permute-start = (bf16[224,128]{1,0:T(8,128)(2,1)S(1)}, bf16[224,128]{1,0:T(8,128)(2,1)S(1)}, u32[]{:S(2)}, u32[]{:S(2)}) collective-permute-start(bf16[224,128]{1,0:T(8,128)(2,1)S(1)} %get-tuple-element.29.refs_2_), channel_id=1, source_target_pairs={{8,16},{16,8},{24,32},{32,24},{40,48},{48,40},{56,0},{0,56},{9,17}... | collective-permute-start | bytes 172040 | tf_op jit(solution)/shard_map/ppermute | solution.py:427
  20.1 0.0 copy-start.9
  20.1 0.0 copy-start.6
  20.2 0.0 copy-start.1
  20.2 2.1 %collective-permute-start.1 = (bf16[224,128]{1,0:T(8,128)(2,1)S(1)}, bf16[224,128]{1,0:T(8,128)(2,1)S(1)}, u32[]{:S(2)}, u32[]{:S(2)}) collective-permute-start(bf16[224,128]{1,0:T(8,128)(2,1)S(1)} %get-tuple-element.30), channel_id=1, source_target_pairs={{0,8},{8,0},{16,24},{24,16},{32,40},{40,32},{48,56},{56,48},{1,9},... | collective-permute-start | bytes 172040 | tf_op jit(solution)/shard_map/ppermute | solution.py:428
  22.2 0.0 copy-done.2
  22.2 0.0 copy-start.10
  22.3 0.0 copy-start.11
  22.3 0.0 copy-start.12
  22.3 0.2 own_step.1.refs_3_
  22.5 0.0 copy-done.9
  22.5 0.0 copy-start.5
  22.5 0.7 prep_z.1
  23.2 0.0 copy-done.6
  23.3 0.7 prep_y.1
  24.0 0.0 copy-done.10
  24.0 0.0 copy-done.11
  24.0 0.0 copy-done.12
  24.0 0.8 prep_top.1
  24.9 0.0 collective-permute-done.refs_1_
  24.9 0.4 collective-permute-done.1.refs_2_
  25.2 0.0 copy-done.1
  25.2 0.0 copy-done.5
  25.2 0.8 y_step.1
  26.1 5.7 %collective-permute-start.2 = (f32[88,128]{1,0:T(8,128)S(1)}, f32[88,128]{1,0:T(8,128)S(1)}, u32[]{:S(2)}, u32[]{:S(2)}) collective-permute-start(f32[88,128]{1,0:T(8,128)S(1)} %get-tuple-element.36), channel_id=1, source_target_pairs={{1,2},{2,1},{3,4},{4,3},{5,6},{6,5},{7,0},{0,7},{9,10},{10,9},{11,... | collective-permute-start | bytes 135176 | tf_op jit(solution)/shard_map/ppermute | solution.py:446
  31.8 1.9 %collective-permute-start.3 = (f32[88,128]{1,0:T(8,128)S(1)}, f32[88,128]{1,0:T(8,128)S(1)}, u32[]{:S(2)}, u32[]{:S(2)}) collective-permute-start(f32[88,128]{1,0:T(8,128)S(1)} %get-tuple-element.37), channel_id=1, source_target_pairs={{0,1},{1,0},{2,3},{3,2},{4,5},{5,4},{6,7},{7,6},{8,9},{9,8},{10,11... | collective-permute-start | bytes 135176 | tf_op jit(solution)/shard_map/ppermute | solution.py:447
  33.7 3.9 %collective-permute-done.2.refs_1_.refs_2_ = f32[88,128]{1,0:T(8,128)S(1)} collective-permute-done((f32[88,128]{1,0:T(8,128)S(1)}, f32[88,128]{1,0:T(8,128)S(1)}, u32[]{:S(2)}, u32[]{:S(2)}) %collective-permute-start.2) | collective-permute-done | bytes 45088 | tf_op jit(solution)/shard_map/ppermute | solution.py:446
  37.6 0.0 collective-permute-done.3.refs_2_.refs_3_
  37.6 0.2 q3_z_step.1
  37.8 3.1 %collective-permute-start.4 = (f32[8,128]{1,0:T(8,128)S(1)}, f32[8,128]{1,0:T(8,128)S(1)}, u32[]{:S(2)}, u32[]{:S(2)}) collective-permute-start(f32[8,128]{1,0:T(8,128)S(1)} %get-tuple-element.38), channel_id=1, source_target_pairs={{0,448},{64,0},{128,64},{192,128},{256,192},{320,256},{384,320},{4... | collective-permute-start | bytes 12296 | tf_op jit(solution)/shard_map/ppermute | solution.py:423
  40.9 1.1 %collective-permute-start.5 = (f32[8,128]{1,0:T(8,128)S(1)}, f32[8,128]{1,0:T(8,128)S(1)}, u32[]{:S(2)}, u32[]{:S(2)}) collective-permute-start(f32[8,128]{1,0:T(8,128)S(1)} %get-tuple-element.40), channel_id=1, source_target_pairs={{0,64},{64,128},{128,192},{192,256},{256,320},{320,384},{384,448},... | collective-permute-start | bytes 12296 | tf_op jit(solution)/shard_map/ppermute | solution.py:423
  42.0 1.3 %collective-permute-done.4.refs_0_ = f32[8,128]{1,0:T(8,128)S(1)} collective-permute-done((f32[8,128]{1,0:T(8,128)S(1)}, f32[8,128]{1,0:T(8,128)S(1)}, u32[]{:S(2)}, u32[]{:S(2)}) %collective-permute-start.4) | collective-permute-done | bytes 4128 | tf_op jit(solution)/shard_map/ppermute | solution.py:423
  43.3 0.0 collective-permute-done.5.refs_2_
  43.3 0.7 q3_x_step.1.refs_6_
  44.0 12.5 %all-to-all-start = ((bf16[64,8,128]{2,1,0:T(8,128)(2,1)}), bf16[64,8,128]{2,1,0:T(8,128)(2,1)S(1)}, u32[]{:S(2)}, u32[]{:S(2)}) async-start(bf16[64,8,128]{2,1,0:T(8,128)(2,1)} %bitcast.3), calls=%async_computation | async-start | bytes 262144 | tf_op jit(solution)/shard_map/all_to_all | solution.py:451
  56.5 0.0 copy-start.4
  56.5 0.9 near_z_step.1
  57.4 0.0 copy-start.8
  57.4 3.4 %collective-permute-start.8 = (f32[520,128]{1,0:T(8,128)S(1)}, f32[520,128]{1,0:T(8,128)S(1)}, u32[]{:S(2)}, u32[]{:S(2)}) collective-permute-start(f32[520,128]{1,0:T(8,128)S(1)} %get-tuple-element.51), channel_id=1, source_target_pairs={{0,448},{64,0},{128,64},{192,128},{256,192},{320,256},{384,320},{4... | collective-permute-start | bytes 798728 | tf_op jit(solution)/shard_map/ppermute | solution.py:423
  60.8 0.0 collective-permute-start.9
  60.8 1.9 %collective-permute-start.6 = (f32[72,128]{1,0:T(8,128)S(1)}, f32[72,128]{1,0:T(8,128)S(1)}, u32[]{:S(2)}, u32[]{:S(2)}) collective-permute-start(f32[72,128]{1,0:T(8,128)S(1)} %get-tuple-element.49), channel_id=1, source_target_pairs={{0,128},{128,0},{64,192},{192,64},{256,384},{384,256},{320,448},{4... | collective-permute-start | bytes 110600 | tf_op jit(solution)/shard_map/ppermute | solution.py:460
  62.7 4.5 %collective-permute-start.7 = (f32[72,128]{1,0:T(8,128)S(1)}, f32[72,128]{1,0:T(8,128)S(1)}, u32[]{:S(2)}, u32[]{:S(2)}) collective-permute-start(f32[72,128]{1,0:T(8,128)S(1)} %get-tuple-element.50), channel_id=1, source_target_pairs={{128,256},{256,128},{192,320},{320,192},{384,0},{0,384},{448,64},{... | collective-permute-start | bytes 110600 | tf_op jit(solution)/shard_map/ppermute | solution.py:461
  67.2 0.0 collective-permute-done.6.refs_3_
  67.2 1.7 %collective-permute-done.7.refs_4_ = f32[72,128]{1,0:T(8,128)S(1)} collective-permute-done((f32[72,128]{1,0:T(8,128)S(1)}, f32[72,128]{1,0:T(8,128)S(1)}, u32[]{:S(2)}, u32[]{:S(2)}) %collective-permute-start.7) | collective-permute-done | bytes 36896 | tf_op jit(solution)/shard_map/ppermute | solution.py:461
  68.9 0.0 collective-permute-done.8.refs_5_
  68.9 0.0 collective-permute-done.9.refs_6_
  68.9 0.0 copy-done.4
  68.9 0.0 copy-done.8
  68.9 1.3 %near_x_step.1.refs_4_.refs_2_ = f32[16,32,128]{2,1,0:T(8,128)S(1)} custom-call(f32[2,17]{1,0:T(2,128)S(1)} %copy-done.9, f32[16,32,128]{2,1,0:T(8,128)S(1)} %get-tuple-element.47.refs_1_, f32[11,24,128]{2,1,0:T(8,128)S(1)} %get-tuple-element.48.refs_2_, f32[72,128]{1,0:T(8,128)S(1)} %collective-permute-done.6.refs_3_, ...), custom_call_target="tpu_custom_call" | custom-call | flops 1000000 | bytes 1000000 | tf_op jit(solution)/shard_map/near_x_step/pallas_call | solution.py:99
  70.2 1.4 %all-to-all-done.refs_0_ = bf16[64,8,128]{2,1,0:T(8,128)(2,1)S(1)} async-done(((bf16[64,8,128]{2,1,0:T(8,128)(2,1)}), bf16[64,8,128]{2,1,0:T(8,128)(2,1)S(1)}, u32[]{:S(2)}, u32[]{:S(2)}) %all-to-all-start) | async-done | bytes 131104 | tf_op jit(solution)/shard_map/all_to_all | solution.py:451
  71.6 0.5 top_step.1
  72.1 0.0 copy-start.3
  72.1 0.0 copy-start.7
  72.1 12.4 %all_to_all.10.refs_0_ = f32[8,16,128]{2,1,0:T(8,128)S(1)} all-to-all(f32[8,16,128]{2,1,0:T(8,128)S(1)} %top_step.1), channel_id=1, replica_groups=mesh['gx'=8,'gy'=8,'gz'=8] {'gx'}, dimensions={0} | all-to-all | bytes 131072 | tf_op jit(solution)/shard_map/all_to_all | solution.py:470
  84.5 0.0 copy-done.3
  84.5 0.0 copy-done.7
  84.5 1.2 %last_step.1 = f32[16,32,128]{2,1,0:T(8,128)} custom-call(f32[8,16,128]{2,1,0:T(8,128)S(1)} %all_to_all.10.refs_0_, f32[16,1024]{1,0:T(8,128)S(1)} %get-tuple-element.34.refs_9_.refs_1_, f32[16,32,128]{2,1,0:T(8,128)S(1)} %near_x_step.1.refs_4_.refs_2_, bf16[32,16]{1,0:T(8,128)(2,1)S(1)} %copy-done.7, bf16[128,128]{1,0:T(8,128)(2,1)S(1)} %copy-done.3), custom_call_target="tpu_custom_call" | custom-call | flops 1000000 | bytes 1000000 | tf_op jit(solution)/shard_map/last_step/pallas_call | solution.py:99
Async XLA Ops:
  0.0 0.9 %copy-start = (bf16[16,32,128]{2,1,0:T(8,128)(2,1)S(1)}, bf16[16,32,128]{2,1,0:T(8,128)(2,1)}, u32[]{:S(2)}) copy-start(bf16[16,32,128]{2,1,0:T(8,128)(2,1)} %refs_0_.10) | copy-start | bytes 393220
  0.9 21.3 %copy-start.2 = (bf16[128,128]{1,0:T(8,128)(2,1)S(1)}, bf16[128,128]{1,0:T(8,128)(2,1)}, u32[]{:S(2)}) copy-start(bf16[128,128]{1,0:T(8,128)(2,1)} %constant.14.clone.refs_1_.refs_6_) | copy-start | bytes 98308
  1.4 23.5 %collective-permute-start = (bf16[224,128]{1,0:T(8,128)(2,1)S(1)}, bf16[224,128]{1,0:T(8,128)(2,1)S(1)}, u32[]{:S(2)}, u32[]{:S(2)}) collective-permute-start(bf16[224,128]{1,0:T(8,128)(2,1)S(1)} %get-tuple-element.29.refs_2_), channel_id=1, source_target_pairs={{8,16},{16,8},{24,32},{32,24},{40,48},{48,40},{56,0},{0,56},{9,17}... | collective-permute-start | bytes 172040 | tf_op jit(solution)/shard_map/ppermute | solution.py:427
  20.1 2.4 %copy-start.9 = (f32[2,17]{1,0:T(2,128)S(1)}, f32[2,17]{1,0:T(2,128)}, u32[]{:S(2)}) copy-start(f32[2,17]{1,0:T(2,128)} %refs_0_.11) | copy-start | bytes 412
  20.1 3.1 %copy-start.6 = (f32[40,64]{1,0:T(8,128)S(1)}, f32[40,64]{1,0:T(8,128)}, u32[]{:S(2)}) copy-start(f32[40,64]{1,0:T(8,128)} %constant.15.clone.refs_1_) | copy-start | bytes 30724
  20.2 5.1 %copy-start.1 = (bf16[16,32,128]{2,1,0:T(8,128)(2,1)S(1)}, bf16[16,32,128]{2,1,0:T(8,128)(2,1)}, u32[]{:S(2)}) copy-start(bf16[16,32,128]{2,1,0:T(8,128)(2,1)} %refs_0_.10) | copy-start | bytes 393220
  20.2 5.1 %collective-permute-start.1 = (bf16[224,128]{1,0:T(8,128)(2,1)S(1)}, bf16[224,128]{1,0:T(8,128)(2,1)S(1)}, u32[]{:S(2)}, u32[]{:S(2)}) collective-permute-start(bf16[224,128]{1,0:T(8,128)(2,1)S(1)} %get-tuple-element.30), channel_id=1, source_target_pairs={{0,8},{8,0},{16,24},{24,16},{32,40},{40,32},{48,56},{56,48},{1,9},... | collective-permute-start | bytes 172040 | tf_op jit(solution)/shard_map/ppermute | solution.py:428
  22.2 1.7 %copy-start.10 = (f32[256]{0:T(256)S(1)}, f32[256]{0:T(256)}, u32[]{:S(2)}) copy-start(f32[256]{0:T(256)} %param.16) | copy-start | bytes 3076
  22.3 1.7 %copy-start.11 = (f32[32]{0:T(128)S(1)}, f32[32]{0:T(128)}, u32[]{:S(2)}) copy-start(f32[32]{0:T(128)} %param.14) | copy-start | bytes 388
  22.3 1.7 %copy-start.12 = (f32[64]{0:T(128)S(1)}, f32[64]{0:T(128)}, u32[]{:S(2)}) copy-start(f32[64]{0:T(128)} %param.15) | copy-start | bytes 772
  22.5 2.7 %copy-start.5 = (bf16[128,128]{1,0:T(8,128)(2,1)S(1)}, bf16[128,128]{1,0:T(8,128)(2,1)}, u32[]{:S(2)}) copy-start(bf16[128,128]{1,0:T(8,128)(2,1)} %constant.16.clone.refs_7_) | copy-start | bytes 98308
  26.1 11.5 %collective-permute-start.2 = (f32[88,128]{1,0:T(8,128)S(1)}, f32[88,128]{1,0:T(8,128)S(1)}, u32[]{:S(2)}, u32[]{:S(2)}) collective-permute-start(f32[88,128]{1,0:T(8,128)S(1)} %get-tuple-element.36), channel_id=1, source_target_pairs={{1,2},{2,1},{3,4},{4,3},{5,6},{6,5},{7,0},{0,7},{9,10},{10,9},{11,... | collective-permute-start | bytes 135176 | tf_op jit(solution)/shard_map/ppermute | solution.py:446
  31.8 5.9 %collective-permute-start.3 = (f32[88,128]{1,0:T(8,128)S(1)}, f32[88,128]{1,0:T(8,128)S(1)}, u32[]{:S(2)}, u32[]{:S(2)}) collective-permute-start(f32[88,128]{1,0:T(8,128)S(1)} %get-tuple-element.37), channel_id=1, source_target_pairs={{0,1},{1,0},{2,3},{3,2},{4,5},{5,4},{6,7},{7,6},{8,9},{9,8},{10,11... | collective-permute-start | bytes 135176 | tf_op jit(solution)/shard_map/ppermute | solution.py:447
  37.8 5.5 %collective-permute-start.4 = (f32[8,128]{1,0:T(8,128)S(1)}, f32[8,128]{1,0:T(8,128)S(1)}, u32[]{:S(2)}, u32[]{:S(2)}) collective-permute-start(f32[8,128]{1,0:T(8,128)S(1)} %get-tuple-element.38), channel_id=1, source_target_pairs={{0,448},{64,0},{128,64},{192,128},{256,192},{320,256},{384,320},{4... | collective-permute-start | bytes 12296 | tf_op jit(solution)/shard_map/ppermute | solution.py:423
  40.9 2.4 %collective-permute-start.5 = (f32[8,128]{1,0:T(8,128)S(1)}, f32[8,128]{1,0:T(8,128)S(1)}, u32[]{:S(2)}, u32[]{:S(2)}) collective-permute-start(f32[8,128]{1,0:T(8,128)S(1)} %get-tuple-element.40), channel_id=1, source_target_pairs={{0,64},{64,128},{128,192},{192,256},{256,320},{320,384},{384,448},... | collective-permute-start | bytes 12296 | tf_op jit(solution)/shard_map/ppermute | solution.py:423
  44.0 27.6 %all-to-all-start = ((bf16[64,8,128]{2,1,0:T(8,128)(2,1)}), bf16[64,8,128]{2,1,0:T(8,128)(2,1)S(1)}, u32[]{:S(2)}, u32[]{:S(2)}) async-start(bf16[64,8,128]{2,1,0:T(8,128)(2,1)} %bitcast.3), calls=%async_computation | async-start | bytes 262144 | tf_op jit(solution)/shard_map/all_to_all | solution.py:451
  56.5 12.4 %copy-start.4 = (bf16[128,128]{1,0:T(8,128)(2,1)S(1)}, bf16[128,128]{1,0:T(8,128)(2,1)}, u32[]{:S(2)}) copy-start(bf16[128,128]{1,0:T(8,128)(2,1)} %constant.18.clone.refs_8_) | copy-start | bytes 98308
  57.4 11.5 %copy-start.8 = (bf16[32,24]{1,0:T(8,128)(2,1)S(1)}, bf16[32,24]{1,0:T(8,128)(2,1)}, u32[]{:S(2)}) copy-start(bf16[32,24]{1,0:T(8,128)(2,1)} %constant.17.clone.refs_7_) | copy-start | bytes 4612
  57.4 11.5 %collective-permute-start.8 = (f32[520,128]{1,0:T(8,128)S(1)}, f32[520,128]{1,0:T(8,128)S(1)}, u32[]{:S(2)}, u32[]{:S(2)}) collective-permute-start(f32[520,128]{1,0:T(8,128)S(1)} %get-tuple-element.51), channel_id=1, source_target_pairs={{0,448},{64,0},{128,64},{192,128},{256,192},{320,256},{384,320},{4... | collective-permute-start | bytes 798728 | tf_op jit(solution)/shard_map/ppermute | solution.py:423
  60.8 8.1 %collective-permute-start.9 = (f32[520,128]{1,0:T(8,128)S(1)}, f32[520,128]{1,0:T(8,128)S(1)}, u32[]{:S(2)}, u32[]{:S(2)}) collective-permute-start(f32[520,128]{1,0:T(8,128)S(1)} %get-tuple-element.52), channel_id=1, source_target_pairs={{0,64},{64,128},{128,192},{192,256},{256,320},{320,384},{384,448},... | collective-permute-start | bytes 798728 | tf_op jit(solution)/shard_map/ppermute | solution.py:423
  60.8 6.4 %collective-permute-start.6 = (f32[72,128]{1,0:T(8,128)S(1)}, f32[72,128]{1,0:T(8,128)S(1)}, u32[]{:S(2)}, u32[]{:S(2)}) collective-permute-start(f32[72,128]{1,0:T(8,128)S(1)} %get-tuple-element.49), channel_id=1, source_target_pairs={{0,128},{128,0},{64,192},{192,64},{256,384},{384,256},{320,448},{4... | collective-permute-start | bytes 110600 | tf_op jit(solution)/shard_map/ppermute | solution.py:460
  62.7 6.2 %collective-permute-start.7 = (f32[72,128]{1,0:T(8,128)S(1)}, f32[72,128]{1,0:T(8,128)S(1)}, u32[]{:S(2)}, u32[]{:S(2)}) collective-permute-start(f32[72,128]{1,0:T(8,128)S(1)} %get-tuple-element.50), channel_id=1, source_target_pairs={{128,256},{256,128},{192,320},{320,192},{384,0},{0,384},{448,64},{... | collective-permute-start | bytes 110600 | tf_op jit(solution)/shard_map/ppermute | solution.py:461
  72.1 12.4 %copy-start.3 = (bf16[128,128]{1,0:T(8,128)(2,1)S(1)}, bf16[128,128]{1,0:T(8,128)(2,1)}, u32[]{:S(2)}) copy-start(bf16[128,128]{1,0:T(8,128)(2,1)} %constant.20.clone.refs_4_) | copy-start | bytes 98308
  72.1 12.4 %copy-start.7 = (bf16[32,16]{1,0:T(8,128)(2,1)S(1)}, bf16[32,16]{1,0:T(8,128)(2,1)}, u32[]{:S(2)}) copy-start(bf16[32,16]{1,0:T(8,128)(2,1)} %constant.19.clone.refs_3_) | copy-start | bytes 3076

commit v9 on v8

--- a/solution.py
+++ b/solution.py
@@ -332,6 +332,21 @@
     to_even[...], to_odd[...] = choose(odd_chip, done2[0:72], done2[192:264])
 
 
+def near_own_step(taps, n1, n2, n1_out, n2_out):
+    for t in range(4):
+        f = [n1[i, 8 * t : 8 * t + 8] for i in range(16)]
+        for i in range(16):
+            n1_out[i, 8 * t : 8 * t + 8] = sum(
+                taps[0, a + 8] * f[i + a] for a in range(-8, 9) if 0 <= i + a < 16
+            )
+    for t in range(3):
+        half = {j: n2[j + 1, 8 * t : 8 * t + 8] for j in range(-1, 10)}
+        for i in range(-1, 10):
+            n2_out[i + 1, 8 * t : 8 * t + 8] = sum(
+                taps[1, a + 8] * half[i + a] for a in range(-8, 9) if i + a in half
+            )
+
+
 def near_x_step(taps, n1, n2, even2, odd2, high, low, y2, z2, out):
     odd_chip = lax.rem(lax.axis_index("gx") // 2, 2) == 1
     low2 = jnp.where(odd_chip, even2[...], odd2[...])
@@ -342,27 +357,23 @@
             f[i - 8] = low[32 * i + 8 * t : 32 * i + 8 * t + 8]
             f[i + 16] = high[32 * i + 8 * t : 32 * i + 8 * t + 8]
         for i in range(16):
-            f[i] = n1[i, 8 * t : 8 * t + 8]
-        for i in range(16):
-            total = taps[0, 0] * f[i - 8]
-            for a in range(-7, 9):
-                total = total + taps[0, a + 8] * f[i + a]
+            total = n1[i, 8 * t : 8 * t + 8] + sum(taps[0, a + 8] * f[i + a] for a in range(-8, 9) if i + a in f)
             out[i, 8 * t : 8 * t + 8] = total
     tiles = {}
     for t in range(3):
         half = {}
         for j in range(-1, 10):
             at = 256 + 24 * (j + 1) + 8 * t
-            for place, part in ((j - 8, low[at : at + 8]), (j, n2[j + 1, 8 * t : 8 * t + 8]), (j + 8, high[at : at + 8])):
+            for place, part in ((j - 8, low[at : at + 8]), (j + 8, high[at : at + 8])):
                 half[place] = half[place] + part if place in half else part
         for k in range(3):
             at = 24 * k + 8 * t
             half[k - 9] = half[k - 9] + low2[at : at + 8]
             half[k + 15] = half[k + 15] + high2[at : at + 8]
         for i in range(-1, 10):
-            total = taps[1, 0] * half[i - 8]
-            for a in range(-7, 9):
-                total = total + taps[1, a + 8] * half[i + a]
+            total = n2[i + 1, 8 * t : 8 * t + 8] + sum(
+                taps[1, a + 8] * half[i + a] for a in range(-8, 9) if i + a in half
+            )
             tiles[i, t] = total
     tall = jnp.concatenate([tiles[i, t] for i in range(-1, 10) for t in range(3)], axis=0)
     tall = from_right(tall, z2)
@@ -462,6 +473,9 @@
         shift(to_low, -1),
         shift(to_high, 1),
     ]
+    n1, n2 = call(
+        near_own_step, [((16, 32, 128), f32), ((11, 24, 128), f32)], [kernel_taps, n1, n2], smem=(0,)
+    )
     (near,) = call(
         near_x_step, [((16, 32, 128), f32)],
         [kernel_taps, n1, n2, *halos, jnp.asarray(y_raise, bf16), jnp.asarray(z_raise, bf16)], smem=(0,),

time: 86.2 us -> 86.2 us (level)
    ppermute x1, waiting for transfers between devices: 1.7 us -> 0.8 us  [per_device(): lax.ppermute(to_odd, 'gx', [(2, 4), (4, 2), (3, 5), (5, 3), (6, 0), (0, 6...]
    pallas_call x12 -> x13, Pallas kernels: 8.54 us -> 9.16 us  [call(): pl.pallas_call(kernel, out_shape=[jax.ShapeDtypeStruct(s, d) for s, d in...]
  transfers between devices with their start and end apart: 11 -> 11, of which waited for: 5 -> 5; matrix products, arithmetic and copies ran while one was open for 0% -> 0% of each run, Pallas kernels for 5% -> 6%
where the time goes in v9:
time: 86.2 us; the launch traced here: 85.7 us
  starting transfers between devices  54.9 us (64%)
  blocking collectives  12.4 us (14%)
  Pallas kernels  9.16 us (11%)
  waiting for transfers between devices  8.05 us (9%)
  local copies, waits for them, and re-layouts  0.98 us (1%)
    ppermute x1, starting transfers between devices, per_device(): from_odd = lax.ppermute(to_odd, 'gy', swap_odd)  18.7 us
    all_to_all x1, starting transfers between devices, per_device(): lax.all_to_all(message.reshape(64, 8, 128), ('gy', 'gz'), split_axis=0, c...  12.5 us
    all_to_all x1, blocking collectives, per_device(): top = lax.all_to_all(message, 'gx', split_axis=0, concat_axis=0, tiled=True)  12.4 us
    pallas_call x13, Pallas kernels, call(): pl.pallas_call(kernel, out_shape=[jax.ShapeDtypeStruct(s, d) for s, d in...  9.16 us
    ppermute x4, starting transfers between devices, shift(): return lax.ppermute(block, 'gx', [(i, (i + by) % 8) for i in range(8)])  7.59 us
    ppermute x1, starting transfers between devices, per_device(): from_odd = lax.ppermute(to_odd, 'gz', swap_odd)  5.67 us
    ppermute x1, starting transfers between devices, per_device(): lax.ppermute(to_odd, 'gx', [(2, 4), (4, 2), (3, 5), (5, 3), (6, 0), (0, 6...  4.49 us
    ppermute x1, waiting for transfers between devices, per_device(): from_odd = lax.ppermute(to_odd, 'gz', swap_odd)  3.94 us
  transfers between devices with their start and end apart: 11, of which 5 were waited for; matrix products, arithmetic and copies ran while one was open for 0% of the time, Pallas kernels for 6%

profile of v9, /device:TPU:1, one launch (start us, length us, event | category | flops | bytes accessed | tf_op | source)
XLA Modules:
  0.0 85.7 jit_solution(10890015920849380336)
XLA Ops:
  0.0 0.0 copy-start
  0.0 0.9 %copy-done = bf16[16,32,128]{2,1,0:T(8,128)(2,1)S(1)} copy-done((bf16[16,32,128]{2,1,0:T(8,128)(2,1)S(1)}, bf16[16,32,128]{2,1,0:T(8,128)(2,1)}, u32[]{:S(2)}) %copy-start) | copy-done | bytes 131096
  0.9 0.0 copy-start.2
  0.9 0.5 y_send.1
  1.4 18.7 %collective-permute-start = (bf16[224,128]{1,0:T(8,128)(2,1)S(1)}, bf16[224,128]{1,0:T(8,128)(2,1)S(1)}, u32[]{:S(2)}, u32[]{:S(2)}) collective-permute-start(bf16[224,128]{1,0:T(8,128)(2,1)S(1)} %get-tuple-element.31.refs_2_), channel_id=1, source_target_pairs={{8,16},{16,8},{24,32},{32,24},{40,48},{48,40},{56,0},{0,56},{9,17}... | collective-permute-start | bytes 172040 | tf_op jit(solution)/shard_map/ppermute | solution.py:438
  20.1 0.0 copy-start.7
  20.1 0.0 copy-start.6
  20.2 0.0 copy-start.1
  20.2 2.1 %collective-permute-start.1 = (bf16[224,128]{1,0:T(8,128)(2,1)S(1)}, bf16[224,128]{1,0:T(8,128)(2,1)S(1)}, u32[]{:S(2)}, u32[]{:S(2)}) collective-permute-start(bf16[224,128]{1,0:T(8,128)(2,1)S(1)} %get-tuple-element.32), channel_id=1, source_target_pairs={{0,8},{8,0},{16,24},{24,16},{32,40},{40,32},{48,56},{56,48},{1,9},... | collective-permute-start | bytes 172040 | tf_op jit(solution)/shard_map/ppermute | solution.py:439
  22.2 0.0 copy-done.2
  22.2 0.0 copy-start.10
  22.3 0.0 copy-start.11
  22.3 0.0 copy-start.12
  22.3 0.2 own_step.1.refs_3_
  22.5 0.0 copy-done.7
  22.5 0.0 copy-start.5
  22.5 0.7 prep_z.1
  23.2 0.0 copy-done.6
  23.3 0.7 prep_y.1
  24.0 0.0 copy-done.10
  24.0 0.0 copy-done.11
  24.0 0.0 copy-done.12
  24.0 0.8 prep_top.1
  24.9 0.0 collective-permute-done.refs_1_
  24.9 0.4 collective-permute-done.1.refs_2_
  25.2 0.0 copy-done.1
  25.2 0.0 copy-done.5
  25.2 0.8 y_step.1
  26.1 5.7 %collective-permute-start.2 = (f32[88,128]{1,0:T(8,128)S(1)}, f32[88,128]{1,0:T(8,128)S(1)}, u32[]{:S(2)}, u32[]{:S(2)}) collective-permute-start(f32[88,128]{1,0:T(8,128)S(1)} %get-tuple-element.38), channel_id=1, source_target_pairs={{1,2},{2,1},{3,4},{4,3},{5,6},{6,5},{7,0},{0,7},{9,10},{10,9},{11,... | collective-permute-start | bytes 135176 | tf_op jit(solution)/shard_map/ppermute | solution.py:457
  31.8 1.9 %collective-permute-start.3 = (f32[88,128]{1,0:T(8,128)S(1)}, f32[88,128]{1,0:T(8,128)S(1)}, u32[]{:S(2)}, u32[]{:S(2)}) collective-permute-start(f32[88,128]{1,0:T(8,128)S(1)} %get-tuple-element.39), channel_id=1, source_target_pairs={{0,1},{1,0},{2,3},{3,2},{4,5},{5,4},{6,7},{7,6},{8,9},{9,8},{10,11... | collective-permute-start | bytes 135176 | tf_op jit(solution)/shard_map/ppermute | solution.py:458
  33.7 3.9 %collective-permute-done.2.refs_1_.refs_2_ = f32[88,128]{1,0:T(8,128)S(1)} collective-permute-done((f32[88,128]{1,0:T(8,128)S(1)}, f32[88,128]{1,0:T(8,128)S(1)}, u32[]{:S(2)}, u32[]{:S(2)}) %collective-permute-start.2) | collective-permute-done | bytes 45088 | tf_op jit(solution)/shard_map/ppermute | solution.py:457
  37.6 0.0 collective-permute-done.3.refs_2_.refs_3_
  37.6 0.2 q3_z_step.1
  37.8 3.1 %collective-permute-start.4 = (f32[8,128]{1,0:T(8,128)S(1)}, f32[8,128]{1,0:T(8,128)S(1)}, u32[]{:S(2)}, u32[]{:S(2)}) collective-permute-start(f32[8,128]{1,0:T(8,128)S(1)} %get-tuple-element.40), channel_id=1, source_target_pairs={{0,448},{64,0},{128,64},{192,128},{256,192},{320,256},{384,320},{4... | collective-permute-start | bytes 12296 | tf_op jit(solution)/shard_map/ppermute | solution.py:434
  40.9 1.1 %collective-permute-start.5 = (f32[8,128]{1,0:T(8,128)S(1)}, f32[8,128]{1,0:T(8,128)S(1)}, u32[]{:S(2)}, u32[]{:S(2)}) collective-permute-start(f32[8,128]{1,0:T(8,128)S(1)} %get-tuple-element.42), channel_id=1, source_target_pairs={{0,64},{64,128},{128,192},{192,256},{256,320},{320,384},{384,448},... | collective-permute-start | bytes 12296 | tf_op jit(solution)/shard_map/ppermute | solution.py:434
  42.0 1.3 %collective-permute-done.4.refs_0_ = f32[8,128]{1,0:T(8,128)S(1)} collective-permute-done((f32[8,128]{1,0:T(8,128)S(1)}, f32[8,128]{1,0:T(8,128)S(1)}, u32[]{:S(2)}, u32[]{:S(2)}) %collective-permute-start.4) | collective-permute-done | bytes 4128 | tf_op jit(solution)/shard_map/ppermute | solution.py:434
  43.3 0.0 collective-permute-done.5.refs_2_
  43.3 0.7 q3_x_step.1.refs_6_
  44.0 12.5 %all-to-all-start = ((bf16[64,8,128]{2,1,0:T(8,128)(2,1)}), bf16[64,8,128]{2,1,0:T(8,128)(2,1)S(1)}, u32[]{:S(2)}, u32[]{:S(2)}) async-start(bf16[64,8,128]{2,1,0:T(8,128)(2,1)} %bitcast.3), calls=%async_computation | async-start | bytes 262144 | tf_op jit(solution)/shard_map/all_to_all | solution.py:462
  56.5 0.9 near_z_step.1
  57.4 3.4 %collective-permute-start.8 = (f32[520,128]{1,0:T(8,128)S(1)}, f32[520,128]{1,0:T(8,128)S(1)}, u32[]{:S(2)}, u32[]{:S(2)}) collective-permute-start(f32[520,128]{1,0:T(8,128)S(1)} %get-tuple-element.55), channel_id=1, source_target_pairs={{0,448},{64,0},{128,64},{192,128},{256,192},{320,256},{384,320},{4... | collective-permute-start | bytes 798728 | tf_op jit(solution)/shard_map/ppermute | solution.py:434
  60.7 0.0 collective-permute-start.9
  60.7 1.9 %collective-permute-start.6 = (f32[72,128]{1,0:T(8,128)S(1)}, f32[72,128]{1,0:T(8,128)S(1)}, u32[]{:S(2)}, u32[]{:S(2)}) collective-permute-start(f32[72,128]{1,0:T(8,128)S(1)} %get-tuple-element.53), channel_id=1, source_target_pairs={{0,128},{128,0},{64,192},{192,64},{256,384},{384,256},{320,448},{4... | collective-permute-start | bytes 110600 | tf_op jit(solution)/shard_map/ppermute | solution.py:471
  62.7 4.5 %collective-permute-start.7 = (f32[72,128]{1,0:T(8,128)S(1)}, f32[72,128]{1,0:T(8,128)S(1)}, u32[]{:S(2)}, u32[]{:S(2)}) collective-permute-start(f32[72,128]{1,0:T(8,128)S(1)} %get-tuple-element.54), channel_id=1, source_target_pairs={{128,256},{256,128},{192,320},{320,192},{384,0},{0,384},{448,64},{... | collective-permute-start | bytes 110600 | tf_op jit(solution)/shard_map/ppermute | solution.py:472
  67.2 0.0 copy-start.4
  67.2 0.0 copy-start.9
  67.2 0.9 %near_own_step.1 = (f32[16,32,128]{2,1,0:T(8,128)S(1)}, f32[11,24,128]{2,1,0:T(8,128)S(1)}) custom-call(f32[2,17]{1,0:T(2,128)S(1)} %copy-done.7, f32[16,32,128]{2,1,0:T(8,128)S(1)} %get-tuple-element.49.refs_1_, f32[11,24,128]{2,1,0:T(8,128)S(1)} %get-tuple-element.50.refs_2_), custom_call_target="tpu_custom_call" | custom-call | flops 1000000 | bytes 1000000 | tf_op jit(solution)/shard_map/near_own_step/pallas_call | solution.py:99
  68.0 0.0 collective-permute-done.6.refs_3_
  68.1 0.8 collective-permute-done.7.refs_4_
  68.9 0.0 collective-permute-done.8.refs_5_
  68.9 0.0 collective-permute-done.9.refs_6_
  68.9 0.0 copy-done.4
  68.9 0.0 copy-done.9
  68.9 1.0 %near_x_step.1.refs_4_.refs_2_ = f32[16,32,128]{2,1,0:T(8,128)S(1)} custom-call(f32[2,17]{1,0:T(2,128)S(1)} %copy-done.7, f32[16,32,128]{2,1,0:T(8,128)S(1)} %get-tuple-element.51.refs_1_, f32[11,24,128]{2,1,0:T(8,128)S(1)} %get-tuple-element.52.refs_2_, f32[72,128]{1,0:T(8,128)S(1)} %collective-permute-done.6.refs_3_, ...), custom_call_target="tpu_custom_call" | custom-call | flops 1000000 | bytes 1000000 | tf_op jit(solution)/shard_map/near_x_step/pallas_call | solution.py:99
  69.9 1.6 %all-to-all-done.refs_0_ = bf16[64,8,128]{2,1,0:T(8,128)(2,1)S(1)} async-done(((bf16[64,8,128]{2,1,0:T(8,128)(2,1)}), bf16[64,8,128]{2,1,0:T(8,128)(2,1)S(1)}, u32[]{:S(2)}, u32[]{:S(2)}) %all-to-all-start) | async-done | bytes 131104 | tf_op jit(solution)/shard_map/all_to_all | solution.py:462
  71.6 0.5 top_step.1
  72.1 0.0 copy-start.3
  72.1 0.0 copy-start.8
  72.1 12.4 %all_to_all.10.refs_0_ = f32[8,16,128]{2,1,0:T(8,128)S(1)} all-to-all(f32[8,16,128]{2,1,0:T(8,128)S(1)} %top_step.1), channel_id=1, replica_groups=mesh['gx'=8,'gy'=8,'gz'=8] {'gx'}, dimensions={0} | all-to-all | bytes 131072 | tf_op jit(solution)/shard_map/all_to_all | solution.py:484
  84.5 0.0 copy-done.3
  84.5 0.0 copy-done.8
  84.5 1.2 %last_step.1 = f32[16,32,128]{2,1,0:T(8,128)} custom-call(f32[8,16,128]{2,1,0:T(8,128)S(1)} %all_to_all.10.refs_0_, f32[16,1024]{1,0:T(8,128)S(1)} %get-tuple-element.36.refs_9_.refs_1_, f32[16,32,128]{2,1,0:T(8,128)S(1)} %near_x_step.1.refs_4_.refs_2_, bf16[32,16]{1,0:T(8,128)(2,1)S(1)} %copy-done.8, bf16[128,128]{1,0:T(8,128)(2,1)S(1)} %copy-done.3), custom_call_target="tpu_custom_call" | custom-call | flops 1000000 | bytes 1000000 | tf_op jit(solution)/shard_map/last_step/pallas_call | solution.py:99
Async XLA Ops:
  0.0 0.9 %copy-start = (bf16[16,32,128]{2,1,0:T(8,128)(2,1)S(1)}, bf16[16,32,128]{2,1,0:T(8,128)(2,1)}, u32[]{:S(2)}) copy-start(bf16[16,32,128]{2,1,0:T(8,128)(2,1)} %refs_0_.11) | copy-start | bytes 393220
  0.9 21.3 %copy-start.2 = (bf16[128,128]{1,0:T(8,128)(2,1)S(1)}, bf16[128,128]{1,0:T(8,128)(2,1)}, u32[]{:S(2)}) copy-start(bf16[128,128]{1,0:T(8,128)(2,1)} %constant.14.clone.refs_1_.refs_6_) | copy-start | bytes 98308
  1.4 23.5 %collective-permute-start = (bf16[224,128]{1,0:T(8,128)(2,1)S(1)}, bf16[224,128]{1,0:T(8,128)(2,1)S(1)}, u32[]{:S(2)}, u32[]{:S(2)}) collective-permute-start(bf16[224,128]{1,0:T(8,128)(2,1)S(1)} %get-tuple-element.31.refs_2_), channel_id=1, source_target_pairs={{8,16},{16,8},{24,32},{32,24},{40,48},{48,40},{56,0},{0,56},{9,17}... | collective-permute-start | bytes 172040 | tf_op jit(solution)/shard_map/ppermute | solution.py:438
  20.1 2.4 %copy-start.7 = (f32[2,17]{1,0:T(2,128)S(1)}, f32[2,17]{1,0:T(2,128)}, u32[]{:S(2)}) copy-start(f32[2,17]{1,0:T(2,128)} %refs_0_.13) | copy-start | bytes 412
  20.1 3.1 %copy-start.6 = (f32[40,64]{1,0:T(8,128)S(1)}, f32[40,64]{1,0:T(8,128)}, u32[]{:S(2)}) copy-start(f32[40,64]{1,0:T(8,128)} %constant.15.clone.refs_1_) | copy-start | bytes 30724
  20.2 5.1 %copy-start.1 = (bf16[16,32,128]{2,1,0:T(8,128)(2,1)S(1)}, bf16[16,32,128]{2,1,0:T(8,128)(2,1)}, u32[]{:S(2)}) copy-start(bf16[16,32,128]{2,1,0:T(8,128)(2,1)} %refs_0_.11) | copy-start | bytes 393220
  20.2 5.1 %collective-permute-start.1 = (bf16[224,128]{1,0:T(8,128)(2,1)S(1)}, bf16[224,128]{1,0:T(8,128)(2,1)S(1)}, u32[]{:S(2)}, u32[]{:S(2)}) collective-permute-start(bf16[224,128]{1,0:T(8,128)(2,1)S(1)} %get-tuple-element.32), channel_id=1, source_target_pairs={{0,8},{8,0},{16,24},{24,16},{32,40},{40,32},{48,56},{56,48},{1,9},... | collective-permute-start | bytes 172040 | tf_op jit(solution)/shard_map/ppermute | solution.py:439
  22.2 1.7 %copy-start.10 = (f32[256]{0:T(256)S(1)}, f32[256]{0:T(256)}, u32[]{:S(2)}) copy-start(f32[256]{0:T(256)} %param.16) | copy-start | bytes 3076
  22.3 1.7 %copy-start.11 = (f32[32]{0:T(128)S(1)}, f32[32]{0:T(128)}, u32[]{:S(2)}) copy-start(f32[32]{0:T(128)} %param.14) | copy-start | bytes 388
  22.3 1.7 %copy-start.12 = (f32[64]{0:T(128)S(1)}, f32[64]{0:T(128)}, u32[]{:S(2)}) copy-start(f32[64]{0:T(128)} %param.15) | copy-start | bytes 772
  22.5 2.7 %copy-start.5 = (bf16[128,128]{1,0:T(8,128)(2,1)S(1)}, bf16[128,128]{1,0:T(8,128)(2,1)}, u32[]{:S(2)}) copy-start(bf16[128,128]{1,0:T(8,128)(2,1)} %constant.16.clone.refs_7_) | copy-start | bytes 98308
  26.1 11.5 %collective-permute-start.2 = (f32[88,128]{1,0:T(8,128)S(1)}, f32[88,128]{1,0:T(8,128)S(1)}, u32[]{:S(2)}, u32[]{:S(2)}) collective-permute-start(f32[88,128]{1,0:T(8,128)S(1)} %get-tuple-element.38), channel_id=1, source_target_pairs={{1,2},{2,1},{3,4},{4,3},{5,6},{6,5},{7,0},{0,7},{9,10},{10,9},{11,... | collective-permute-start | bytes 135176 | tf_op jit(solution)/shard_map/ppermute | solution.py:457
  31.8 5.9 %collective-permute-start.3 = (f32[88,128]{1,0:T(8,128)S(1)}, f32[88,128]{1,0:T(8,128)S(1)}, u32[]{:S(2)}, u32[]{:S(2)}) collective-permute-start(f32[88,128]{1,0:T(8,128)S(1)} %get-tuple-element.39), channel_id=1, source_target_pairs={{0,1},{1,0},{2,3},{3,2},{4,5},{5,4},{6,7},{7,6},{8,9},{9,8},{10,11... | collective-permute-start | bytes 135176 | tf_op jit(solution)/shard_map/ppermute | solution.py:458
  37.8 5.5 %collective-permute-start.4 = (f32[8,128]{1,0:T(8,128)S(1)}, f32[8,128]{1,0:T(8,128)S(1)}, u32[]{:S(2)}, u32[]{:S(2)}) collective-permute-start(f32[8,128]{1,0:T(8,128)S(1)} %get-tuple-element.40), channel_id=1, source_target_pairs={{0,448},{64,0},{128,64},{192,128},{256,192},{320,256},{384,320},{4... | collective-permute-start | bytes 12296 | tf_op jit(solution)/shard_map/ppermute | solution.py:434
  40.9 2.4 %collective-permute-start.5 = (f32[8,128]{1,0:T(8,128)S(1)}, f32[8,128]{1,0:T(8,128)S(1)}, u32[]{:S(2)}, u32[]{:S(2)}) collective-permute-start(f32[8,128]{1,0:T(8,128)S(1)} %get-tuple-element.42), channel_id=1, source_target_pairs={{0,64},{64,128},{128,192},{192,256},{256,320},{320,384},{384,448},... | collective-permute-start | bytes 12296 | tf_op jit(solution)/shard_map/ppermute | solution.py:434
  44.0 27.6 %all-to-all-start = ((bf16[64,8,128]{2,1,0:T(8,128)(2,1)}), bf16[64,8,128]{2,1,0:T(8,128)(2,1)S(1)}, u32[]{:S(2)}, u32[]{:S(2)}) async-start(bf16[64,8,128]{2,1,0:T(8,128)(2,1)} %bitcast.3), calls=%async_computation | async-start | bytes 262144 | tf_op jit(solution)/shard_map/all_to_all | solution.py:462
  57.4 11.5 %collective-permute-start.8 = (f32[520,128]{1,0:T(8,128)S(1)}, f32[520,128]{1,0:T(8,128)S(1)}, u32[]{:S(2)}, u32[]{:S(2)}) collective-permute-start(f32[520,128]{1,0:T(8,128)S(1)} %get-tuple-element.55), channel_id=1, source_target_pairs={{0,448},{64,0},{128,64},{192,128},{256,192},{320,256},{384,320},{4... | collective-permute-start | bytes 798728 | tf_op jit(solution)/shard_map/ppermute | solution.py:434
  60.7 8.1 %collective-permute-start.9 = (f32[520,128]{1,0:T(8,128)S(1)}, f32[520,128]{1,0:T(8,128)S(1)}, u32[]{:S(2)}, u32[]{:S(2)}) collective-permute-start(f32[520,128]{1,0:T(8,128)S(1)} %get-tuple-element.56), channel_id=1, source_target_pairs={{0,64},{64,128},{128,192},{192,256},{256,320},{320,384},{384,448},... | collective-permute-start | bytes 798728 | tf_op jit(solution)/shard_map/ppermute | solution.py:434
  60.7 7.3 %collective-permute-start.6 = (f32[72,128]{1,0:T(8,128)S(1)}, f32[72,128]{1,0:T(8,128)S(1)}, u32[]{:S(2)}, u32[]{:S(2)}) collective-permute-start(f32[72,128]{1,0:T(8,128)S(1)} %get-tuple-element.53), channel_id=1, source_target_pairs={{0,128},{128,0},{64,192},{192,64},{256,384},{384,256},{320,448},{4... | collective-permute-start | bytes 110600 | tf_op jit(solution)/shard_map/ppermute | solution.py:471
  62.7 6.2 %collective-permute-start.7 = (f32[72,128]{1,0:T(8,128)S(1)}, f32[72,128]{1,0:T(8,128)S(1)}, u32[]{:S(2)}, u32[]{:S(2)}) collective-permute-start(f32[72,128]{1,0:T(8,128)S(1)} %get-tuple-element.54), channel_id=1, source_target_pairs={{128,256},{256,128},{192,320},{320,192},{384,0},{0,384},{448,64},{... | collective-permute-start | bytes 110600 | tf_op jit(solution)/shard_map/ppermute | solution.py:472
  67.2 1.7 %copy-start.4 = (bf16[128,128]{1,0:T(8,128)(2,1)S(1)}, bf16[128,128]{1,0:T(8,128)(2,1)}, u32[]{:S(2)}) copy-start(bf16[128,128]{1,0:T(8,128)(2,1)} %constant.18.clone.refs_8_) | copy-start | bytes 98308
  67.2 1.7 %copy-start.9 = (bf16[32,24]{1,0:T(8,128)(2,1)S(1)}, bf16[32,24]{1,0:T(8,128)(2,1)}, u32[]{:S(2)}) copy-start(bf16[32,24]{1,0:T(8,128)(2,1)} %constant.17.clone.refs_7_) | copy-start | bytes 4612
  72.1 12.4 %copy-start.3 = (bf16[128,128]{1,0:T(8,128)(2,1)S(1)}, bf16[128,128]{1,0:T(8,128)(2,1)}, u32[]{:S(2)}) copy-start(bf16[128,128]{1,0:T(8,128)(2,1)} %constant.20.clone.refs_4_) | copy-start | bytes 98308
  72.1 12.4 %copy-start.8 = (bf16[32,16]{1,0:T(8,128)(2,1)S(1)}, bf16[32,16]{1,0:T(8,128)(2,1)}, u32[]{:S(2)}) copy-start(bf16[32,16]{1,0:T(8,128)(2,1)} %constant.19.clone.refs_3_) | copy-start | bytes 3076
